TPU v7x, 128 devices: a whole 4x4x4 slice. The times are simulated.
128 devices in a mesh: row: 16 (over x, y), col: 8 (over z, core).
Axes of the slice: x: 4, y: 4, z: 4, core: 2. Of those that a mesh axis runs over, the one named last changes fastest.
Arguments:
- excitation: float32 [2, 8, 131072], P(None, None, ('row', 'col')), may hold values from -6 to 6
- precond: float32 [131072], P(('row', 'col')), may hold values from 0.4 to 0.8
- near_blocks: bfloat16 [8, 1024, 2, 2, 128, 128], P('col', 'row')
- near_index: int32 [8, 1024, 2], P('col', 'row'), may hold values from 0 to 127, as said below
- coupling: bfloat16 [2048, 8, 2, 128, 128], P(('row', 'col')), may hold values from -0.1875 to 0.1875
- visible: int32 [2048, 8], P(('row', 'col')), may hold values from -1 to 1023, as said below
- reflect: float32 [2, 262144], P(None, ('row', 'col')), may hold values from -1 to 1
Outputs:
- currents: float32 [2, 8, 131072], P(None, None, ('row', 'col'))
- facet_currents: float32 [2, 8, 262144], P(None, None, ('row', 'col'))
Inputs may be any that keep to these rules, and one draw needn't show every extreme that they name: `near_index`: within one column group every block row lists 2 different column blocks; on the column group that owns the block row's own unknowns, the first listed block is that diagonal block. `visible`: the tiles of one device never list a block twice, and list at most 2 blocks of any one device's 8 blocks (block b belongs to device b // 8 along row+col); some device's tiles list exactly 2 blocks of some device. The tiles of one device see the blocks of at most 64 devices.
All inputs are finite; a program needn't handle non-finite values.
Results may differ from a plain program's by a relative error of at most 0.0048.
Values may be sent and summed in bfloat16 or wider, within the bound.
No kernel may reach another device: no remote copies, remote signals or barrier semaphores. Data moves between devices by JAX's collectives and lax.ppermute only.
A program may use at most 128 MiB of HBM per device.

v0:
```python
import jax
import jax.numpy as jnp
from jax import lax
from jax.sharding import PartitionSpec as P

ITERS = 2


def shards(excitation, precond, near_blocks, near_index, coupling, visible, reflect):
    exc_count = excitation.shape[1]
    seg_len = excitation.shape[2]
    block_size = coupling.shape[-1]
    seg_blocks = seg_len // block_size
    tile_count = coupling.shape[0]
    slot_count = coupling.shape[1]
    facet_size = coupling.shape[3]
    device_count = lax.axis_size(("row", "col"))
    entry_count = tile_count * slot_count
    block_ids = visible.reshape(-1)
    is_live = block_ids >= 0
    safe_ids = jnp.where(is_live, block_ids, 0)
    coef_real = reflect[0].reshape(tile_count, facet_size)[:, None, :]
    coef_imag = reflect[1].reshape(tile_count, facet_size)[:, None, :]
    currents = precond[None, None, :] * excitation
    facet_out = jnp.zeros((2, exc_count, tile_count * facet_size), jnp.float32)
    for iteration in range(ITERS):
        rounded = currents.astype(jnp.bfloat16)
        columns = lax.all_gather(rounded, "row", axis=2, tiled=True)
        col_blocks = columns.reshape(2, exc_count, -1, block_size)
        chosen = col_blocks[:, :, near_index[0], :]
        product = jnp.einsum(
            "bkpij,qebkj->pqebi", near_blocks[0], chosen, preferred_element_type=jnp.float32
        )
        real_part = product[0, 0] - product[1, 1]
        imag_part = product[0, 1] + product[1, 0]
        partial_rows = jnp.stack([real_part, imag_part]).reshape(2, exc_count, -1)
        near = lax.psum_scatter(partial_rows, "col", scatter_dimension=2, tiled=True)
        everything = lax.all_gather(rounded, ("row", "col"), axis=2, tiled=True)
        all_blocks = everything.reshape(2, exc_count, -1, block_size)
        entries = jnp.transpose(jnp.take(all_blocks, safe_ids, axis=2), (2, 0, 1, 3))
        optics_entries = jnp.where(
            is_live[:, None, None, None], entries, jnp.zeros((), jnp.bfloat16)
        ).reshape(tile_count, slot_count, 2, exc_count, block_size)
        incident = jnp.einsum(
            "tvpfj,tvqej->pqtef", coupling, optics_entries, preferred_element_type=jnp.float32
        )
        inc_real = incident[0, 0] - incident[1, 1]
        inc_imag = incident[0, 1] + incident[1, 0]
        facets = jnp.stack(
            [
                coef_real * inc_real - coef_imag * inc_imag,
                coef_real * inc_imag + coef_imag * inc_real,
            ]
        )
        facet_rounded = facets.astype(jnp.bfloat16)
        backward = jnp.einsum(
            "tvpfj,qtef->pqtvej", coupling, facet_rounded, preferred_element_type=jnp.float32
        )
        backward = jnp.stack([backward[0, 0] - backward[1, 1], backward[0, 1] + backward[1, 0]])
        backward = backward.reshape(2, entry_count, exc_count, block_size)
        backward = jnp.where(is_live[None, :, None, None], backward, 0.0)
        optics_facet_out = jnp.transpose(facets, (0, 2, 1, 3)).reshape(
            2, exc_count, tile_count * facet_size
        )
        values = jnp.transpose(backward, (0, 2, 1, 3))
        partial_all = jnp.zeros((2, exc_count, device_count * seg_blocks, block_size), jnp.float32)
        partial_all = partial_all.at[:, :, safe_ids, :].add(values).reshape(2, exc_count, -1)
        back = lax.psum_scatter(partial_all, ("row", "col"), scatter_dimension=2, tiled=True)
        facet_out = optics_facet_out
        currents = currents + precond[None, None, :] * (excitation - near - back)
    return (currents, facet_out)


def solution(mesh):
    placed = (
        P(None, None, ("row", "col")),
        P(("row", "col")),
        P("col", "row", None, None, None, None),
        P("col", "row", None),
        P(("row", "col"), None, None, None, None),
        P(("row", "col"), None),
        P(None, ("row", "col")),
    )
    return jax.shard_map(
        shards,
        mesh=mesh,
        in_specs=placed,
        out_specs=(P(None, None, ("row", "col")), P(None, None, ("row", "col"))),
        check_vma=False,
    )
```

profile of v0, /device:TPU:1, one launch (start us, length us, event | category | flops | bytes accessed | tf_op | source)
XLA Modules:
  0.0 1509.1 jit_solution(12915138569606907115)
XLA Ops:
  8.0 0.0 copy-start.5
  8.0 0.0 copy-start.4
  8.0 0.0 all-gather.3.cloned.1.call-start
  8.1 1.5 multiply_convert_fusion
  9.5 0.0 all-gather.3.cloned.1.call-update
  9.6 0.0 reduce-scatter.5.cloned.1.call-start
  9.6 0.7 compare_select_fusion
  10.3 0.1 copy.25
  10.4 0.1 reshape.451
  10.5 20.1 %all_gather.12 = bf16[2,8,16384]{2,1,0:T(8,128)(2,1)S(1)} all-gather(bf16[2,8,1024]{2,1,0:T(8,128)(2,1)} %multiply_convert_fusion), channel_id=1, replica_groups=mesh['row'=16,'col'=8] {'row'}, dimensions={2}, use_global_device_ids=true | all-gather | bytes 557056 | tf_op jit(solution)/shard_map/all_gather | solution.py:28
  30.6 0.8 gather_fusion
  31.4 5.7 fusion.18
  37.0 0.1 fusion.39
  37.1 0.9 pad_maximum_fusion
  38.0 0.0 reduce-scatter.5.cloned.1.call-update
  38.0 0.0 reduce-scatter.7.cloned.1.call-start
  38.0 0.0 copy-done.5
  38.0 0.1 copy.28
  38.1 0.1 reshape.424
  38.2 0.1 reshape.423
  38.3 0.0 copy-done.4
  38.4 45.3 %all-gather.3.cloned.1.call-done = bf16[2,8,131072]{2,1,0:T(8,128)(2,1)} async-done(((bf16[2,8,1024]{2,1,0:T(8,128)(2,1)}), bf16[2,8,131072]{2,1,0:T(8,128)(2,1)}) %all-gather.3.cloned.1.call-update) | async-done | bytes 4194320 | tf_op jit(solution)/shard_map/all_gather | solution.py:38
  83.7 2.9 gather_fusion.2
  86.6 0.3 bitcast_select_fusion.1
  87.0 5.6 fusion.24
  92.7 4.6 fusion.12
  97.2 0.1 slice_subtract_fusion.1
  97.4 0.2 fusion.30
  97.6 0.0 copy-start
  97.6 0.0 copy-start.3
  97.6 3.8 broadcast.134.clone
  101.4 15.1 %scatter_fusion = f32[2,8,1024,128]{3,1,2,0:T(8,128)} fusion(f32[2,8,1024,128]{3,1,2,0:T(8,128)} %broadcast.134.clone, s32[128]{0:T(128)S(1)} %fusion.51, f32[128,2,8,128]{3,2,1,0:T(8,128)S(1)} %fusion.30), kind=kCustom, calls=%fused_computation.4 | custom fusion | flops 262144 | bytes 3146240 | tf_op jit(solution)/shard_map/scatter-add | solution.py:67
  116.5 0.0 reduce-scatter.7.cloned.1.call-update
  116.5 0.0 all-gather.5.cloned.1.call-start
  116.6 0.0 reduce-scatter.5.cloned.1.call-done
  116.6 640.4 %reduce-scatter.7.cloned.1.call-done = f32[2,8,1024]{2,1,0:T(8,128)} async-done(((f32[2,8,131072]{2,1,0:T(8,128)}), f32[2,8,1024]{2,1,0:T(8,128)}) %reduce-scatter.7.cloned.1.call-update) | async-done | bytes 65552 | tf_op jit(solution)/shard_map/reduce_scatter | solution.py:68
  757.0 0.0 copy-done
  757.0 0.0 copy-done.3
  757.0 1.5 fusion.50
  758.5 0.0 all-gather.5.cloned.1.call-update
  758.5 0.0 reduce-scatter.9.cloned.1.call-start
  758.5 16.9 %all_gather.14 = bf16[2,8,16384]{2,1,0:T(8,128)(2,1)S(1)} all-gather(bf16[2,8,1024]{2,1,0:T(8,128)(2,1)} %fusion.50), channel_id=1, replica_groups=mesh['row'=16,'col'=8] {'row'}, dimensions={2}, use_global_device_ids=true | all-gather | bytes 557056 | tf_op jit(solution)/shard_map/all_gather | solution.py:28
  775.5 0.8 gather_fusion.1
  776.2 5.7 fusion.21
  781.9 0.1 fusion.37
  782.0 0.9 pad_maximum_fusion.1
  782.8 0.0 reduce-scatter.9.cloned.1.call-update
  782.9 0.2 reduce-scatter.11.cloned.1.call-start
  783.1 43.5 %all-gather.5.cloned.1.call-done = bf16[2,8,131072]{2,1,0:T(8,128)(2,1)} async-done(((bf16[2,8,1024]{2,1,0:T(8,128)(2,1)}), bf16[2,8,131072]{2,1,0:T(8,128)(2,1)}) %all-gather.5.cloned.1.call-update) | async-done | bytes 4194320 | tf_op jit(solution)/shard_map/all_gather | solution.py:38
  826.6 2.9 gather_fusion.3
  829.5 0.3 bitcast_select_fusion
  829.9 5.6 fusion.27
  835.6 4.6 fusion.15
  840.1 0.1 slice_subtract_fusion
  840.3 0.2 fusion.31
  840.5 0.0 copy-start.1
  840.5 0.0 copy-start.2
  840.5 3.8 broadcast.134
  844.3 15.1 %scatter_fusion.1 = f32[2,8,1024,128]{3,1,2,0:T(8,128)} fusion(f32[2,8,1024,128]{3,1,2,0:T(8,128)} %broadcast.134, s32[128]{0:T(128)S(1)} %fusion.51, f32[128,2,8,128]{3,2,1,0:T(8,128)S(1)} %fusion.31), kind=kCustom, calls=%fused_computation.5 | custom fusion | flops 262144 | bytes 3146240 | tf_op jit(solution)/shard_map/scatter-add | solution.py:67
  859.4 0.0 reduce-scatter.11.cloned.1.call-update
  859.4 0.7 fusion.40
  860.0 639.9 %reduce-scatter.11.cloned.1.call-done = f32[2,8,1024]{2,1,0:T(8,128)} async-done(((f32[2,8,131072]{2,1,0:T(8,128)}), f32[2,8,1024]{2,1,0:T(8,128)}) %reduce-scatter.11.cloned.1.call-update) | async-done | bytes 65552 | tf_op jit(solution)/shard_map/reduce_scatter | solution.py:68
  1499.9 0.0 copy-done.1
  1499.9 1.5 multiply_add_fusion
  (9 shorter events, 0.1 us)
Async XLA Ops:
  8.0 30.0 %copy-start.5 = (s32[16,8]{0,1:T(8,128)S(1)}, s32[16,8]{0,1:T(8,128)}, u32[]{:S(2)}) copy-start(s32[16,8]{0,1:T(8,128)} %param.14) | copy-start | bytes 1540
  8.0 30.3 %copy-start.4 = (f32[2,2048]{1,0:T(2,128)S(1)}, f32[2,2048]{1,0:T(2,128)}, u32[]{:S(2)}) copy-start(f32[2,2048]{1,0:T(2,128)} %param.15) | copy-start | bytes 49156
  8.0 75.7 %all-gather.3.cloned.1.call-start = ((), (), s32[]{:S(2)}) async-start(), calls=%async_computation.5 | async-start | bytes 4227072 | tf_op jit(solution)/shard_map/all_gather | solution.py:38
  9.6 107.0 %reduce-scatter.5.cloned.1.call-start = ((), (), s32[]{:S(2)}) async-start(), calls=%async_computation.4 | async-start | bytes 589824 | tf_op jit(solution)/shard_map/reduce_scatter | solution.py:37
  38.0 719.0 %reduce-scatter.7.cloned.1.call-start = ((), (), s32[]{:S(2)}) async-start(), calls=%async_computation.6 | async-start | bytes 8454144 | tf_op jit(solution)/shard_map/reduce_scatter | solution.py:68
  97.6 659.4 %copy-start = (f32[2,8,1024]{2,1,0:T(8,128)S(1)}, f32[2,8,1024]{2,1,0:T(8,128)}, u32[]{:S(2)}) copy-start(f32[2,8,1024]{2,1,0:T(8,128)} %param.9) | copy-start | bytes 196612
  97.6 659.4 %copy-start.3 = (f32[1024]{0:T(1024)S(1)}, f32[1024]{0:T(1024)}, u32[]{:S(2)}) copy-start(f32[1024]{0:T(1024)} %param.10) | copy-start | bytes 12292
  116.5 710.1 %all-gather.5.cloned.1.call-start = ((), (), s32[]{:S(2)}) async-start(), calls=%async_computation.8 | async-start | bytes 4227072 | tf_op jit(solution)/shard_map/all_gather | solution.py:38
  758.5 101.6 %reduce-scatter.9.cloned.1.call-start = ((), (), s32[]{:S(2)}) async-start(), calls=%async_computation.7 | async-start | bytes 589824 | tf_op jit(solution)/shard_map/reduce_scatter | solution.py:37
  782.9 717.1 %reduce-scatter.11.cloned.1.call-start = ((), (), s32[]{:S(2)}) async-start(), calls=%async_computation.9 | async-start | bytes 8454144 | tf_op jit(solution)/shard_map/reduce_scatter | solution.py:68
  840.5 659.5 %copy-start.1 = (f32[2,8,1024]{2,1,0:T(8,128)S(1)}, f32[2,8,1024]{2,1,0:T(8,128)}, u32[]{:S(2)}) copy-start(f32[2,8,1024]{2,1,0:T(8,128)} %reduce-scatter.5.cloned.1.call-done) | copy-start | bytes 196612
  840.5 659.5 %copy-start.2 = (f32[2,8,1024]{2,1,0:T(8,128)S(1)}, f32[2,8,1024]{2,1,0:T(8,128)}, u32[]{:S(2)}) copy-start(f32[2,8,1024]{2,1,0:T(8,128)} %reduce-scatter.7.cloned.1.call-done) | copy-start | bytes 196612
Sparse Core Ops, SparseCore 0:
  12.9 70.7 all-gather.2
  758.6 67.9 all-gather.4
Sparse Core Ops, SparseCore 1:
  38.1 35.1 reduce-scatter.4
  116.6 640.3 reduce-scatter.6
  782.9 37.5 reduce-scatter.8
  859.5 640.4 reduce-scatter.10
where the time goes:
time: 1520 us; the launch traced here: 1510 us
  waiting for transfers between devices  1370 us (90%)
  other arithmetic  39.3 us (3%)
  blocking collectives  37 us (2%)
  matrix products  31.8 us (2%)
  between operations  15.9 us (1%)
  local copies, waits for them, and re-layouts  15.4 us (1%)
    reduce_scatter x2, waiting for transfers between devices, shards(): lax.psum_scatter(partial_all, ('row', 'col'), scatter_dimension=2, tiled=...  1280 us
    all_gather x2, waiting for transfers between devices, shards(): everything = lax.all_gather(rounded, ('row', 'col'), axis=2, tiled=True)  88.8 us
    all_gather x2, blocking collectives, shards(): columns = lax.all_gather(rounded, 'row', axis=2, tiled=True)  37 us
  transfers between devices with their start and end apart: 6, of which 4 were waited for; matrix products, arithmetic and copies ran while one was open for 5% of the time, Pallas kernels for 0%

commit v1 on v0

v1 whole, which is shorter than its diff:
```python
import functools

import jax
import jax.numpy as jnp
from jax import lax
from jax.experimental import pallas as pl
from jax.experimental.pallas import tpu as pltpu
from jax.sharding import PartitionSpec as P

ITERS = 2
TURNS = 2
VMEM = pl.BlockSpec(memory_space=pltpu.VMEM)
SMEM = pl.BlockSpec(memory_space=pltpu.SMEM)


def params(mib, **more):
    return pltpu.CompilerParams(vmem_limit_bytes=mib << 20, **more)


def dot_t(a, b):
    return lax.dot_general(a, b, (((1,), (1,)), ((), ())), preferred_element_type=jnp.float32)


def slots_kernel(rows, cols, seg, me_ref, visible_ref, forward_ref, back_ref, wanted_ref, count_ref):
    tiles, slots = visible_ref.shape
    me = me_ref[0]
    none = rows * cols

    def clear(i, _):
        count_ref[i] = 0
        return 0

    lax.fori_loop(0, none + 1, clear, 0, unroll=8)

    def clear_wanted(i, _):
        for j in range(rows * TURNS):
            wanted_ref[i, j] = seg
        return 0

    lax.fori_loop(0, cols, clear_wanted, 0)

    def tile(t, _):
        for v in range(slots):
            block = visible_ref[t, v]
            entry = t * slots + v
            live = block >= 0
            owner = jnp.where(live, lax.shift_right_arithmetic(block, log2(seg)), none)
            turn = count_ref[owner]
            count_ref[owner] = turn + live.astype(jnp.int32)
            row = lax.shift_right_arithmetic(owner, log2(cols))
            col = owner & (cols - 1)
            place = row * TURNS + turn
            forward_ref[entry] = jnp.where(live, col * (rows * TURNS) + place, -1)
            back_ref[entry] = jnp.where(live, owner * TURNS + turn, -1)
            line = jnp.where(live, (col - me) & (cols - 1), cols)
            wanted_ref[line, jnp.where(live, place, 0)] = block & (seg - 1)
        return 0

    lax.fori_loop(0, tiles, tile, 0)

    def find(i, free):
        return jnp.where(count_ref[i] < TURNS, i * TURNS + TURNS - 1, free)

    back_ref[tiles * slots] = lax.fori_loop(0, none, find, 0, unroll=8)


def log2(n):
    return n.bit_length() - 1


def make_slots(me, visible, rows, cols, seg):
    count = visible.size
    return pl.pallas_call(
        functools.partial(slots_kernel, rows, cols, seg),
        out_shape=(
            jax.ShapeDtypeStruct((count,), jnp.int32),
            jax.ShapeDtypeStruct((count + 1,), jnp.int32),
            jax.ShapeDtypeStruct((cols + 1, 128), jnp.int32),
        ),
        in_specs=[SMEM, SMEM],
        out_specs=(SMEM, SMEM, SMEM),
        scratch_shapes=[pltpu.SMEM((rows * cols + 1,), jnp.int32)],
        name="slots",
    )(me, visible)


def send_kernel(me_ref, index_ref, wanted_ref, blocks_ref, group_ref, *rest):
    count, per_row, _, size, _ = blocks_ref.shape
    tag_ref = rest[0] if len(rest) == 3 else None
    out_ref, own_ref = rest[-2:]
    exc = own_ref.shape[1]
    half = exc // 2
    me = me_ref[0]
    peers = pl.num_programs(0)
    p = pl.program_id(0)
    line = ((me - p) & (peers - 1)) * 128
    slots = group_ref.shape[0] * TURNS
    for s in range(slots):
        block = wanted_ref[line + s] & (count - 1)
        out_ref[0, s] = group_ref[s // TURNS, pl.ds(pl.multiple_of(block * exc, exc), exc), :]
    if tag_ref is not None:
        out_ref[0, slots + count] = tag_ref[0]
    for i in range(count):
        parts = []
        for k in range(per_row):
            block = index_ref[(p * count + i) * per_row + k]
            place = pl.multiple_of((block & (count - 1)) * exc, exc)
            parts.append(
                group_ref[lax.shift_right_arithmetic(block, log2(count)), pl.ds(place, exc), :]
            )
        weights = [blocks_ref[i, k].reshape(2 * size, size) for k in range(per_row)]
        total = dot_t(jnp.concatenate(parts, axis=1), jnp.concatenate(weights, axis=1))
        by_re, by_im = total[:, :size], total[:, size:]
        sums = jnp.concatenate([by_re[:half] - by_im[half:], by_re[half:] + by_im[:half]], axis=0)
        out_ref[0, slots + i] = jnp.where(p == me, 0.0, sums).astype(jnp.bfloat16)
        own_ref[i] = jnp.where(p == me, sums, own_ref[i])


def send(me, index, wanted, blocks, group, tags, seg, exc):
    rows, per_row, _, size, _ = blocks.shape
    cols = rows // seg
    slots = group.shape[0] * TURNS + seg + (tags is not None)
    in_specs = [
        pl.BlockSpec((seg, per_row, 2, size, size), lambda i, *s: (i, 0, 0, 0, 0)),
        pl.BlockSpec(group.shape, lambda i, *s: (0, 0, 0)),
    ]
    operands = [blocks, group]
    if tags is not None:
        in_specs.append(pl.BlockSpec((1, exc, size), lambda i, *s: (i, 0, 0)))
        operands.append(tags)
    return pl.pallas_call(
        send_kernel,
        out_shape=(
            jax.ShapeDtypeStruct((cols, slots, exc, size), jnp.bfloat16),
            jax.ShapeDtypeStruct((seg, exc, size), jnp.float32),
        ),
        grid_spec=pltpu.PrefetchScalarGridSpec(
            num_scalar_prefetch=3,
            grid=(cols,),
            in_specs=in_specs,
            out_specs=(
                pl.BlockSpec((1, slots, exc, size), lambda i, *s: (i, 0, 0, 0)),
                pl.BlockSpec((seg, exc, size), lambda i, *s: (0, 0, 0)),
            ),
        ),
        compiler_params=params(57),
        cost_estimate=pl.CostEstimate(
            flops=2 * exc * blocks.size, bytes_accessed=2 * blocks.size, transcendentals=0
        ),
        name="send",
    )(me, index, wanted, *operands)


def optics_kernel(forward_ref, back_ref, coupling_ref, x_ref, own_ref, reflect_ref, facet_ref, out_ref, near_ref):
    tiles, slots, _, facets, size = coupling_ref.shape
    cols = x_ref.shape[0]
    seg, exc = own_ref.shape[:2]
    half = exc // 2
    step = pl.program_id(0)
    places = out_ref.shape[0] // cols
    free = back_ref[back_ref.shape[0] - 1]

    @pl.when(step == 0)
    def _():
        for b in range(seg):
            total = own_ref[b]
            for c in range(cols):
                total += x_ref[c, places + b].astype(jnp.float32)
            near_ref[b] = total

    for t in range(tiles):
        first = (step * tiles + t) * slots
        total = None
        weights = []
        for v in range(0, slots, 2):
            parts = []
            for u in (v, v + 1):
                slot = forward_ref[first + u]
                live = slot >= 0
                slot = jnp.where(live, slot, 0)
                x = x_ref[lax.shift_right_arithmetic(slot, log2(places)), slot & (places - 1)]
                parts.append(jnp.where(live, x, jnp.zeros_like(x)))
            weights.append(
                jnp.concatenate(
                    [coupling_ref[t, u].reshape(2 * facets, size) for u in (v, v + 1)], axis=1
                )
            )
            product = dot_t(jnp.concatenate(parts, axis=1), weights[-1])
            total = product if total is None else total + product
        by_re, by_im = total[:, :facets], total[:, facets:]
        inc_re = by_re[:half] - by_im[half:]
        inc_im = by_re[half:] + by_im[:half]
        lanes = slice(t * facets, (t + 1) * facets)
        coef_re, coef_im = reflect_ref[0:1, lanes], reflect_ref[1:2, lanes]
        out_re = coef_re * inc_re - coef_im * inc_im
        out_im = coef_re * inc_im + coef_im * inc_re
        facet_ref[0, :, lanes] = out_re
        facet_ref[1, :, lanes] = out_im
        both = jnp.concatenate(
            [
                jnp.concatenate([out_re, -out_im], axis=1),
                jnp.concatenate([out_im, out_re], axis=1),
            ],
            axis=0,
        ).astype(jnp.bfloat16)
        for v in range(0, slots, 2):
            sums = jnp.dot(both, weights[v // 2], preferred_element_type=jnp.float32)
            sums = sums.astype(jnp.bfloat16)
            for u in range(2):
                slot = back_ref[first + v + u]
                out_ref[jnp.where(slot >= 0, slot, free)] = sums[:, u * size : (u + 1) * size]


def optics(forward, back, coupling, x, own, reflect, devices):
    tiles, slots, _, facets, size = coupling.shape
    exc = x.shape[2]
    step = 2
    return pl.pallas_call(
        optics_kernel,
        out_shape=(
            jax.ShapeDtypeStruct((2, exc // 2, tiles * facets), jnp.float32),
            jax.ShapeDtypeStruct((devices * TURNS, exc, size), jnp.bfloat16),
            jax.ShapeDtypeStruct(own.shape, jnp.float32),
        ),
        grid_spec=pltpu.PrefetchScalarGridSpec(
            num_scalar_prefetch=2,
            grid=(tiles // step,),
            in_specs=[
                pl.BlockSpec((step, slots, 2, facets, size), lambda i, *s: (i, 0, 0, 0, 0)),
                pl.BlockSpec(x.shape, lambda i, *s: (0, 0, 0, 0)),
                pl.BlockSpec(own.shape, lambda i, *s: (0, 0, 0)),
                pl.BlockSpec((2, step * facets), lambda i, *s: (0, i)),
            ],
            out_specs=(
                pl.BlockSpec((2, exc // 2, step * facets), lambda i, *s: (0, 0, i)),
                pl.BlockSpec((devices * TURNS, exc, size), lambda i, *s: (0, 0, 0)),
                pl.BlockSpec(own.shape, lambda i, *s: (0, 0, 0)),
            ),
        ),
        compiler_params=params(57),
        cost_estimate=pl.CostEstimate(
            flops=4 * exc * coupling.size, bytes_accessed=2 * coupling.size, transcendentals=0
        ),
        name="optics",
    )(forward, back, coupling, x, own, reflect)


def update_kernel(cols, owner_ref, back_ref, near_ref, currents_ref, excitation_ref, precond_ref, out_ref, *rest):
    count, exc, size = back_ref.shape
    seg = near_ref.shape[0]
    half = exc // 2
    total_ref = rest[-1]
    total_ref[:seg] = near_ref[...]
    rows = count // (cols * TURNS)

    def add(r, _):
        for c in range(cols):
            for turn in range(TURNS):
                block = owner_ref[(c * rows + r) * TURNS + turn]
                slot = (r * cols + c) * TURNS + turn
                total_ref[block] = total_ref[block] + back_ref[slot].astype(jnp.float32)
        return 0

    lax.fori_loop(0, rows, add, 0)
    for b in range(seg):
        lanes = slice(b * size, (b + 1) * size)
        scale = precond_ref[:, lanes]
        for q in range(2):
            part = total_ref[b, q * half : (q + 1) * half]
            new = currents_ref[q, :, lanes] + scale * (excitation_ref[q, :, lanes] - part)
            out_ref[q, :, lanes] = new
            if len(rest) > 1:
                total_ref[b, q * half : (q + 1) * half] = new
    if len(rest) > 1:
        copies_ref = rest[0]
        rounded = total_ref[:seg].astype(jnp.bfloat16).reshape(seg * exc, size)
        for r in range(copies_ref.shape[0]):
            copies_ref[r] = rounded


def update(owner, back, near, currents, excitation, precond, copies, cols):
    seg, exc, size = near.shape
    out_shape = [jax.ShapeDtypeStruct(currents.shape, jnp.float32)]
    if copies:
        out_shape.append(jax.ShapeDtypeStruct((copies, seg * exc, size), jnp.bfloat16))
    return pl.pallas_call(
        functools.partial(update_kernel, cols),
        out_shape=out_shape,
        in_specs=[SMEM] + [VMEM] * 5,
        out_specs=[VMEM] * len(out_shape),
        scratch_shapes=[pltpu.VMEM((seg + 1, exc, size), jnp.float32)],
        compiler_params=params(16),
        name="update",
    )(owner, back, near, currents, excitation, precond[None, :])


def shards(excitation, precond, near_blocks, near_index, coupling, visible, reflect):
    exc = 2 * excitation.shape[1]
    size = coupling.shape[-1]
    seg = excitation.shape[2] // size
    rows, cols = lax.axis_size("row"), lax.axis_size("col")
    devices = rows * cols

    me = lax.axis_index("col").astype(jnp.int32).reshape(1)
    forward, back, wanted = make_slots(me, visible, rows, cols, seg)
    mine = lax.dynamic_slice_in_dim(
        jnp.concatenate([wanted[:cols], wanted[:cols]]), cols - me[0], cols, axis=0
    )
    tags = jnp.transpose(mine[:, : rows * TURNS].reshape(cols, rows, TURNS), (1, 0, 2))
    tags = jnp.repeat(tags.astype(jnp.bfloat16), size // TURNS, axis=2)
    tags = jnp.concatenate([tags, jnp.zeros((rows, exc - cols, size), jnp.bfloat16)], axis=1)

    currents = precond[None, None, :] * excitation
    rounded = currents.astype(jnp.bfloat16).reshape(2, exc // 2, seg, size)
    rounded = jnp.transpose(rounded, (2, 0, 1, 3)).reshape(1, seg * exc, size)
    copies = jnp.concatenate(
        [jnp.broadcast_to(rounded, (rows,) + rounded.shape[1:]), tags], axis=1
    )
    lines = [wanted[:1]]
    for k in range(1, cols):
        with jax.named_scope("wanted_exchange"):
            ring = [(i, (i + k) % cols) for i in range(cols)]
            lines.append(lax.ppermute(wanted[k : k + 1], "col", ring))
    wanted = jnp.concatenate(lines).reshape(-1)
    index = near_index[0].reshape(-1)
    owner = None
    for iteration in range(ITERS):
        last = iteration == ITERS - 1
        with jax.named_scope("row_exchange"):
            group = lax.all_to_all(copies, "row", 0, 0, tiled=True)
        tags = None
        if iteration == 0:
            tags = jnp.transpose(group[:, seg * exc : seg * exc + cols], (1, 0, 2))
        packed, own = send(me, index, wanted, near_blocks[0], group, tags, seg, exc)
        with jax.named_scope("col_exchange"):
            x = lax.all_to_all(packed, "col", 0, 0, tiled=True)
        if iteration == 0:
            owner = x[:, -1, :, :: size // TURNS].astype(jnp.int32).reshape(-1)
        facets, sums, near = optics(forward, back, coupling, x, own, reflect, devices)
        with jax.named_scope("back_exchange"):
            sums = lax.all_to_all(
                sums.reshape(devices, TURNS * exc, size), ("row", "col"), 0, 0, tiled=True
            )
        sums = sums.reshape(devices * TURNS, exc, size)
        out = update(
            owner, sums, near, currents, excitation, precond, 0 if last else rows, cols
        )
        currents = out[0]
        copies = None if last else out[1]
    return currents, facets


def solution(mesh):
    placed = (
        P(None, None, ("row", "col")),
        P(("row", "col")),
        P("col", "row", None, None, None, None),
        P("col", "row", None),
        P(("row", "col"), None, None, None, None),
        P(("row", "col"), None),
        P(None, ("row", "col")),
    )
    return jax.shard_map(
        shards,
        mesh=mesh,
        in_specs=placed,
        out_specs=(P(None, None, ("row", "col")), P(None, None, ("row", "col"))),
        check_vma=False,
    )
```

time: 1520 us -> 193 us (0.13)
  waiting for transfers between devices: 1370 us -> 16.8 us
  Pallas kernels: 0 us -> 51.2 us
  blocking collectives: 37 us -> 86.6 us
  other arithmetic: 39.3 us -> 1.9 us
  matrix products: 31.8 us -> 0 us
  starting transfers between devices: 0.44 us -> 25.5 us
    reduce_scatter x4 -> x0, waiting for transfers between devices: 1280 us -> none  [the longest x2 1280 us: shards(): lax.psum_scatter(partial_all, ('row', 'col'), scatter_dimension=2, tiled=...]
    all_gather x2 -> x0, waiting for transfers between devices: 88.8 us -> none  [shards(): everything = lax.all_gather(rounded, ('row', 'col'), axis=2, tiled=True)]
    all_to_all x0 -> x4, blocking collectives: none -> 86.6 us  [the longest x2 48.9 us: shards(): x = lax.all_to_all(packed, 'col', 0, 0, tiled=True)]
    pallas_call x0 -> x7, Pallas kernels: none -> 51.2 us  [the longest x2 25.4 us: optics(): pl.pallas_call(optics_kernel, out_shape=(jax.ShapeDtypeStruct((2, exc //...]
    all_gather x2 -> x0, blocking collectives: 37 us -> none  [shards(): columns = lax.all_gather(rounded, 'row', axis=2, tiled=True)]
    dot_general x6 -> x0, matrix products: 31.8 us -> none  [the longest x2 11.3 us: shards(): jnp.einsum('bkpij,qebkj->pqebi', near_blocks[0], chosen, preferred_elemen...]
    scatter-add x2 -> x0, other arithmetic: 30.2 us -> none  [shards(): partial_all.at[:, :, safe_ids, :].add(values).reshape(2, exc_count, -1)]
    all_to_all x0 -> x2, waiting for transfers between devices: none -> 16 us  [the longest x1 16 us: shards(): lax.all_to_all(sums.reshape(devices, TURNS * exc, size), ('row', 'col'),...]
  transfers between devices with their start and end apart: 6 -> 9, of which waited for: 4 -> 2; matrix products, arithmetic and copies ran while one was open for 5% -> 2% of each run, Pallas kernels for 0% -> 0%
where the time goes in v1:
time: 193 us; the launch traced here: 191 us
  blocking collectives  86.6 us (45%)
  Pallas kernels  51.2 us (27%)
  starting transfers between devices  25.5 us (13%)
  waiting for transfers between devices  16.8 us (9%)
  local copies, waits for them, and re-layouts  8.42 us (4%)
    all_to_all x2, blocking collectives, shards(): x = lax.all_to_all(packed, 'col', 0, 0, tiled=True)  48.9 us
    pallas_call x2, Pallas kernels, optics(): pl.pallas_call(optics_kernel, out_shape=(jax.ShapeDtypeStruct((2, exc //...  25.4 us
    all_to_all x1, blocking collectives, shards(): lax.all_to_all(sums.reshape(devices, TURNS * exc, size), ('row', 'col'),...  24.3 us
    pallas_call x2, Pallas kernels, send(): pl.pallas_call(send_kernel, out_shape=(jax.ShapeDtypeStruct((cols, slots,...  18.1 us
    all_to_all x1, waiting for transfers between devices, shards(): lax.all_to_all(sums.reshape(devices, TURNS * exc, size), ('row', 'col'),...  16 us
    all_to_all x1, blocking collectives, shards(): group = lax.all_to_all(copies, 'row', 0, 0, tiled=True)  13.4 us
    ppermute x7, starting transfers between devices, shards(): lines.append(lax.ppermute(wanted[k:k + 1], 'col', ring))  10.3 us
    all_to_all x1, starting transfers between devices, shards(): lax.all_to_all(sums.reshape(devices, TURNS * exc, size), ('row', 'col'),...  7.65 us
  transfers between devices with their start and end apart: 9, of which 2 were waited for; matrix products, arithmetic and copies ran while one was open for 2% of the time, Pallas kernels for 0%

profile of v1, /device:TPU:1, one launch (start us, length us, event | category | flops | bytes accessed | tf_op | source)
XLA Modules:
  0.0 191.2 jit_solution(6110435592245725067)
XLA Ops:
  0.6 1.4 copy.19.visible_ref
  2.0 3.4 %slots.1 = (s32[128]{0:T(128)}, s32[129]{0:T(256)}, s32[9,128]{1,0:T(8,128)}) custom-call(s32[1]{0:T(128)} %bitcast.me_ref, s32[16,8]{1,0:T(8,128)} %copy.19.visible_ref), custom_call_target="tpu_custom_call" | custom-call | tf_op jit(solution)/shard_map/slots/pallas_call | solution.py:73
  5.4 0.7 slice.46
  6.1 0.1 copy.21
  6.2 0.2 copy.22
  6.4 0.2 broadcast_in_dim.20
  6.6 0.1 reshape.40
  6.7 0.9 convert_bitcast_fusion
  7.6 0.1 pad.2.clone
  7.6 0.0 copy-start.5
  7.6 0.1 broadcast_in_dim.19
  7.7 0.0 copy-start.6
  7.8 1.0 maximum_maximum_fusion
  8.8 7.6 %all-to-all-start = ((bf16[16,144,128]{2,1,0:T(8,128)(2,1)}), bf16[16,144,128]{2,1,0:T(8,128)(2,1)S(1)}, u32[]{:S(2)}, u32[]{:S(2)}) async-start(bf16[16,144,128]{2,1,0:T(8,128)(2,1)} %maximum_maximum_fusion), calls=%async_computation | async-start | bytes 1179648 | tf_op jit(solution)/shard_map/row_exchange/all_to_all | solution.py:330
  16.4 0.0 copy-done.5
  16.4 1.0 collective-permute-start.6
  17.4 3.8 %collective-permute-start.5 = (s32[1,128]{1,0:T(1,128)S(1)}, s32[1,128]{1,0:T(1,128)S(1)}, u32[]{:S(2)}, u32[]{:S(2)}) collective-permute-start(s32[1,128]{1,0:T(1,128)S(1)} %get-tuple-element.33), channel_id=1, source_target_pairs={{0,6},{1,7},{2,0},{3,1},{4,2},{5,3},{6,4},{7,5},{8,14},{9,15},{10,... | collective-permute-start | bytes 1544 | tf_op jit(solution)/shard_map/wanted_exchange/ppermute | solution.py:323
  21.1 0.4 collective-permute-start.4
  21.5 2.5 %collective-permute-start.3 = (s32[1,128]{1,0:T(1,128)S(1)}, s32[1,128]{1,0:T(1,128)S(1)}, u32[]{:S(2)}, u32[]{:S(2)}) collective-permute-start(s32[1,128]{1,0:T(1,128)S(1)} %get-tuple-element.35), channel_id=1, source_target_pairs={{0,4},{1,5},{2,6},{3,7},{4,0},{5,1},{6,2},{7,3},{8,12},{9,13},{10,... | collective-permute-start | bytes 1544 | tf_op jit(solution)/shard_map/wanted_exchange/ppermute | solution.py:323
  24.0 0.6 collective-permute-start.2
  24.6 0.0 collective-permute-done.6
  24.6 0.8 collective-permute-start.1
  25.4 0.0 collective-permute-done.5
  25.4 1.2 collective-permute-start
  26.7 0.0 copy-done.6
  26.7 0.1 copy.18
  26.8 0.7 reshape_squeeze.3.index_ref
  27.5 0.0 collective-permute-done.4
  27.5 0.0 collective-permute-done.3
  27.5 0.8 collective-permute-done.2
  28.3 0.0 collective-permute-done.1
  28.3 0.0 collective-permute-done
  28.3 0.6 concatenate.9
  29.0 0.0 all-to-all-done.group_ref
  29.0 0.0 copy-start.4
  29.0 0.7 copy.26
  29.6 0.2 copy-done.4
  29.8 9.1 %send.2 = (bf16[8,41,16,128]{3,2,1,0:T(8,128)(2,1)}, f32[8,16,128]{2,1,0:T(8,128)}) custom-call(s32[1]{0:T(128)} %bitcast.me_ref, s32[128]{0:T(128)} %reshape_squeeze.3.index_ref, s32[1024]{0:T(1024)} %bitcast.32, bf16[64,2,2,128,128]{4,3,2,1,0:T(8,128)(2,1)} %bitcast.26, bf16[16,144,128]{2,1,0:T(8,128)(2,1)} %copy-done.4, bf16[8,16,128]{2,1,0:T(8,128)(2,1)} %bitcast.30), custom_call_target="tpu_custom_call" | custom-call | flops 134217728 | bytes 8388608 | tf_op jit(solution)/shard_map/send/pallas_call | solution.py:131
  38.9 24.4 %all_to_all.30.x_ref = bf16[8,41,16,128]{3,2,1,0:T(8,128)(2,1)} all-to-all(bf16[8,41,16,128]{3,2,1,0:T(8,128)(2,1)} %get-tuple-element.17), channel_id=1, replica_groups=mesh['row'=16,'col'=8] {'col'}, dimensions={0} | all-to-all | bytes 2686976 | tf_op jit(solution)/shard_map/col_exchange/all_to_all | solution.py:336
  63.3 12.7 %optics.2 = (f32[2,8,2048]{2,1,0:T(8,128)}, bf16[256,16,128]{2,1,0:T(8,128)(2,1)}, f32[8,16,128]{2,1,0:T(8,128)}) custom-call(s32[128]{0:T(128)} %get-tuple-element.18.forward_ref, s32[129]{0:T(256)} %get-tuple-element.19.back_ref, bf16[16,8,2,128,128]{4,3,2,1,0:T(8,128)(2,1)} %coupling_ref.3, bf16[8,41,16,128]{3,2,1,0:T(8,128)(2,1)} %all_to_all.30.x_ref, ...), custom_call_target="tpu_custom_call" | custom-call | flops 268435456 | bytes 8388608 | tf_op jit(solution)/shard_map/optics/pallas_call | solution.py:218
  76.0 0.0 copy-start
  76.0 0.0 copy-start.1
  76.0 0.0 copy-start.3
  76.1 7.6 %all-to-all-start.2 = ((bf16[128,32,128]{2,1,0:T(8,128)(2,1)}), bf16[128,32,128]{2,1,0:T(8,128)(2,1)S(1)}, u32[]{:S(2)}, u32[]{:S(2)}) async-start(bf16[128,32,128]{2,1,0:T(8,128)(2,1)} %bitcast.28), calls=%async_computation.2 | async-start | bytes 2097152 | tf_op jit(solution)/shard_map/back_exchange/all_to_all | solution.py:341
  83.7 3.2 %slice.49 = bf16[8,1,16,2]{3,2,1,0:T(8,128)(2,1)S(1)} slice(bf16[8,41,16,128]{3,2,1,0:T(8,128)(2,1)} %all_to_all.30.x_ref), slice={[0:8:1], [40:41:1], [0:16:1], [0:128:64]} | slice | bytes 1024 | tf_op jit(solution)/shard_map/slice | solution.py:338
  86.9 0.1 reshape.45.owner_ref
  87.0 16.0 %all-to-all-done.2 = bf16[128,32,128]{2,1,0:T(8,128)(2,1)S(1)} async-done(((bf16[128,32,128]{2,1,0:T(8,128)(2,1)}), bf16[128,32,128]{2,1,0:T(8,128)(2,1)S(1)}, u32[]{:S(2)}, u32[]{:S(2)}) %all-to-all-start.2) | async-done | bytes 1048608 | tf_op jit(solution)/shard_map/back_exchange/all_to_all | solution.py:341
  103.0 0.0 copy-done
  103.0 0.0 copy-done.1
  103.0 0.0 copy-done.3
  103.0 1.8 update.2
  104.9 13.4 %all_to_all.31.group_ref = bf16[16,128,128]{2,1,0:T(8,128)(2,1)} all-to-all(bf16[16,128,128]{2,1,0:T(8,128)(2,1)S(1)} %get-tuple-element.23), channel_id=1, replica_groups=mesh['row'=16,'col'=8] {'row'}, dimensions={0} | all-to-all | bytes 1048576 | tf_op jit(solution)/shard_map/row_exchange/all_to_all | solution.py:330
  118.2 9.0 %send.3 = (bf16[8,40,16,128]{3,2,1,0:T(8,128)(2,1)}, f32[8,16,128]{2,1,0:T(8,128)}) custom-call(s32[1]{0:T(128)} %bitcast.me_ref, s32[128]{0:T(128)} %reshape_squeeze.3.index_ref, s32[1024]{0:T(1024)} %bitcast.33, bf16[64,2,2,128,128]{4,3,2,1,0:T(8,128)(2,1)} %bitcast.27, bf16[16,128,128]{2,1,0:T(8,128)(2,1)} %all_to_all.31.group_ref), custom_call_target="tpu_custom_call" | custom-call | flops 134217728 | bytes 8388608 | tf_op jit(solution)/shard_map/send/pallas_call | solution.py:131
  127.2 24.5 %all_to_all.32.x_ref = bf16[8,40,16,128]{3,2,1,0:T(8,128)(2,1)} all-to-all(bf16[8,40,16,128]{3,2,1,0:T(8,128)(2,1)} %get-tuple-element.24), channel_id=1, replica_groups=mesh['row'=16,'col'=8] {'col'}, dimensions={0} | all-to-all | bytes 2621440 | tf_op jit(solution)/shard_map/col_exchange/all_to_all | solution.py:336
  151.8 12.7 %optics.3 = (f32[2,8,2048]{2,1,0:T(8,128)}, bf16[256,16,128]{2,1,0:T(8,128)(2,1)}, f32[8,16,128]{2,1,0:T(8,128)}) custom-call(s32[128]{0:T(128)} %get-tuple-element.18.forward_ref, s32[129]{0:T(256)} %get-tuple-element.19.back_ref, bf16[16,8,2,128,128]{4,3,2,1,0:T(8,128)(2,1)} %coupling_ref.3, bf16[8,40,16,128]{3,2,1,0:T(8,128)(2,1)} %all_to_all.32.x_ref, ...), custom_call_target="tpu_custom_call" | custom-call | flops 268435456 | bytes 8388608 | tf_op jit(solution)/shard_map/optics/pallas_call | solution.py:218
  164.5 0.0 copy-start.2
  164.5 24.3 %all_to_all.33 = bf16[128,32,128]{2,1,0:T(8,128)(2,1)S(1)} all-to-all(bf16[128,32,128]{2,1,0:T(8,128)(2,1)} %bitcast.29), channel_id=1, replica_groups=mesh['row'=16,'col'=8] {'row','col'}, dimensions={0} | all-to-all | bytes 2097152 | tf_op jit(solution)/shard_map/back_exchange/all_to_all | solution.py:341
  188.8 0.0 copy-done.2
  188.8 2.4 %update.3 = f32[2,8,1024]{2,1,0:T(8,128)} custom-call(s32[256]{0:T(256)S(1)} %reshape.45.owner_ref, bf16[256,16,128]{2,1,0:T(8,128)(2,1)S(1)} %bitcast.23, f32[8,16,128]{2,1,0:T(8,128)S(1)} %copy-done.2, f32[2,8,1024]{2,1,0:T(8,128)S(1)} %get-tuple-element.28.currents_ref, f32[2,8,1024]{2,1,0:T(8,128)S(1)} %copy-done, f32[1,1024]{1,0:T(1,128)S(1)} %bitcast.25), custom_call_target="tpu_custom_call" | custom-call | tf_op jit(solution)/shard_map/update/pallas_call | solution.py:286
  (6 shorter events, 0.0 us)
Async XLA Ops:
  7.6 8.7 %copy-start.5 = (s32[9,128]{1,0:T(8,128)S(1)}, s32[9,128]{1,0:T(8,128)}, u32[]{:S(2)}) copy-start(s32[9,128]{1,0:T(8,128)} %get-tuple-element.16) | copy-start | bytes 13828
  7.7 18.9 %copy-start.6 = (s32[1,64,2]{1,2,0:T(2,128)S(1)}, s32[1,64,2]{1,2,0:T(2,128)}, u32[]{:S(2)}) copy-start(s32[1,64,2]{1,2,0:T(2,128)} %param.10) | copy-start | bytes 1540
  8.8 20.2 %all-to-all-start = ((bf16[16,144,128]{2,1,0:T(8,128)(2,1)}), bf16[16,144,128]{2,1,0:T(8,128)(2,1)S(1)}, u32[]{:S(2)}, u32[]{:S(2)}) async-start(bf16[16,144,128]{2,1,0:T(8,128)(2,1)} %maximum_maximum_fusion), calls=%async_computation | async-start | bytes 1179648 | tf_op jit(solution)/shard_map/row_exchange/all_to_all | solution.py:330
  16.4 8.2 %collective-permute-start.6 = (s32[1,128]{1,0:T(1,128)S(1)}, s32[1,128]{1,0:T(1,128)S(1)}, u32[]{:S(2)}, u32[]{:S(2)}) collective-permute-start(s32[1,128]{1,0:T(1,128)S(1)} %get-tuple-element.32), channel_id=1, source_target_pairs={{0,7},{1,0},{2,1},{3,2},{4,3},{5,4},{6,5},{7,6},{8,15},{9,8},{10,9... | collective-permute-start | bytes 1544 | tf_op jit(solution)/shard_map/wanted_exchange/ppermute | solution.py:323
  17.4 8.1 %collective-permute-start.5 = (s32[1,128]{1,0:T(1,128)S(1)}, s32[1,128]{1,0:T(1,128)S(1)}, u32[]{:S(2)}, u32[]{:S(2)}) collective-permute-start(s32[1,128]{1,0:T(1,128)S(1)} %get-tuple-element.33), channel_id=1, source_target_pairs={{0,6},{1,7},{2,0},{3,1},{4,2},{5,3},{6,4},{7,5},{8,14},{9,15},{10,... | collective-permute-start | bytes 1544 | tf_op jit(solution)/shard_map/wanted_exchange/ppermute | solution.py:323
  21.1 6.4 %collective-permute-start.4 = (s32[1,128]{1,0:T(1,128)S(1)}, s32[1,128]{1,0:T(1,128)S(1)}, u32[]{:S(2)}, u32[]{:S(2)}) collective-permute-start(s32[1,128]{1,0:T(1,128)S(1)} %get-tuple-element.34), channel_id=1, source_target_pairs={{0,5},{1,6},{2,7},{3,0},{4,1},{5,2},{6,3},{7,4},{8,13},{9,14},{10,... | collective-permute-start | bytes 1544 | tf_op jit(solution)/shard_map/wanted_exchange/ppermute | solution.py:323
  21.5 6.0 %collective-permute-start.3 = (s32[1,128]{1,0:T(1,128)S(1)}, s32[1,128]{1,0:T(1,128)S(1)}, u32[]{:S(2)}, u32[]{:S(2)}) collective-permute-start(s32[1,128]{1,0:T(1,128)S(1)} %get-tuple-element.35), channel_id=1, source_target_pairs={{0,4},{1,5},{2,6},{3,7},{4,0},{5,1},{6,2},{7,3},{8,12},{9,13},{10,... | collective-permute-start | bytes 1544 | tf_op jit(solution)/shard_map/wanted_exchange/ppermute | solution.py:323
  24.0 4.4 %collective-permute-start.2 = (s32[1,128]{1,0:T(1,128)S(1)}, s32[1,128]{1,0:T(1,128)S(1)}, u32[]{:S(2)}, u32[]{:S(2)}) collective-permute-start(s32[1,128]{1,0:T(1,128)S(1)} %get-tuple-element.36), channel_id=1, source_target_pairs={{0,3},{1,4},{2,5},{3,6},{4,7},{5,0},{6,1},{7,2},{8,11},{9,12},{10,... | collective-permute-start | bytes 1544 | tf_op jit(solution)/shard_map/wanted_exchange/ppermute | solution.py:323
  24.6 3.7 %collective-permute-start.1 = (s32[1,128]{1,0:T(1,128)S(1)}, s32[1,128]{1,0:T(1,128)S(1)}, u32[]{:S(2)}, u32[]{:S(2)}) collective-permute-start(s32[1,128]{1,0:T(1,128)S(1)} %get-tuple-element.37), channel_id=1, source_target_pairs={{0,2},{1,3},{2,4},{3,5},{4,6},{5,7},{6,0},{7,1},{8,10},{9,11},{10,... | collective-permute-start | bytes 1544 | tf_op jit(solution)/shard_map/wanted_exchange/ppermute | solution.py:323
  25.4 2.9 %collective-permute-start = (s32[1,128]{1,0:T(1,128)S(1)}, s32[1,128]{1,0:T(1,128)S(1)}, u32[]{:S(2)}, u32[]{:S(2)}) collective-permute-start(s32[1,128]{1,0:T(1,128)S(1)} %get-tuple-element.38), channel_id=1, source_target_pairs={{0,1},{1,2},{2,3},{3,4},{4,5},{5,6},{6,7},{7,0},{8,9},{9,10},{10,1... | collective-permute-start | bytes 1544 | tf_op jit(solution)/shard_map/wanted_exchange/ppermute | solution.py:323
  29.0 0.9 copy-start.4
  76.0 27.0 %copy-start = (f32[2,8,1024]{2,1,0:T(8,128)S(1)}, f32[2,8,1024]{2,1,0:T(8,128)}, u32[]{:S(2)}) copy-start(f32[2,8,1024]{2,1,0:T(8,128)} %excitation_ref.3) | copy-start | bytes 196612
  76.0 27.0 %copy-start.1 = (f32[8,16,128]{2,1,0:T(8,128)S(1)}, f32[8,16,128]{2,1,0:T(8,128)}, u32[]{:S(2)}) copy-start(f32[8,16,128]{2,1,0:T(8,128)} %get-tuple-element.22.near_ref) | copy-start | bytes 196612
  76.0 27.0 %copy-start.3 = (f32[1024]{0:T(1024)S(1)}, f32[1024]{0:T(1024)}, u32[]{:S(2)}) copy-start(f32[1024]{0:T(1024)} %param.8) | copy-start | bytes 12292
  76.1 26.9 %all-to-all-start.2 = ((bf16[128,32,128]{2,1,0:T(8,128)(2,1)}), bf16[128,32,128]{2,1,0:T(8,128)(2,1)S(1)}, u32[]{:S(2)}, u32[]{:S(2)}) async-start(bf16[128,32,128]{2,1,0:T(8,128)(2,1)} %bitcast.28), calls=%async_computation.2 | async-start | bytes 2097152 | tf_op jit(solution)/shard_map/back_exchange/all_to_all | solution.py:341
  164.5 24.3 %copy-start.2 = (f32[8,16,128]{2,1,0:T(8,128)S(1)}, f32[8,16,128]{2,1,0:T(8,128)}, u32[]{:S(2)}) copy-start(f32[8,16,128]{2,1,0:T(8,128)} %get-tuple-element.27.near_ref) | copy-start | bytes 196612

commit v2 on v0

v2 whole, which is shorter than its diff:
```python
import functools

import jax
import jax.numpy as jnp
from jax import lax
from jax.experimental import pallas as pl
from jax.experimental.pallas import tpu as pltpu
from jax.sharding import PartitionSpec as P

ITERS = 2
TURNS = 2
VMEM = pl.BlockSpec(memory_space=pltpu.VMEM)
SMEM = pl.BlockSpec(memory_space=pltpu.SMEM)
HBM = pl.BlockSpec(memory_space=pltpu.HBM)


def params(mib, **more):
    return pltpu.CompilerParams(vmem_limit_bytes=mib << 20, **more)


def dot_t(a, b):
    return lax.dot_general(a, b, (((1,), (1,)), ((), ())), preferred_element_type=jnp.float32)


def log2(n):
    return n.bit_length() - 1


def start_kernel(
    rows, cols, me_ref, visible_in, excitation_in, precond_in,
    forward_out, back_out, wanted_ref, currents_ref, copies_ref,
    count_ref, code_ref, visible_ref, excitation_ref, precond_ref, forward_ref, back_ref, sems,
):
    fetches = [
        pltpu.make_async_copy(visible_in, visible_ref, sems.at[0]),
        pltpu.make_async_copy(excitation_in, excitation_ref, sems.at[1]),
        pltpu.make_async_copy(precond_in, precond_ref, sems.at[2]),
    ]
    stores = [
        pltpu.make_async_copy(forward_ref, forward_out, sems.at[3]),
        pltpu.make_async_copy(back_ref, back_out, sems.at[4]),
    ]
    for fetch in fetches:
        fetch.start()
    slots, tiles = visible_ref.shape
    half, lanes = excitation_ref.shape[1:]
    size = copies_ref.shape[2]
    seg, exc = lanes // size, 2 * half
    me = me_ref[0]
    none = rows * cols
    base = 2 * seg

    def clear(i, _):
        count_ref[i] = 0
        code_ref[i] = seg * base + seg
        return 0

    lax.fori_loop(0, none + 1, clear, 0, unroll=8)
    fetches[0].wait()

    def tile(t, _):
        for v in range(slots):
            block = visible_ref[v, t]
            entry = t * slots + v
            live = block >= 0
            owner = jnp.where(live, lax.shift_right_arithmetic(block, log2(seg)), none)
            turn = count_ref[owner]
            count_ref[owner] = turn + live.astype(jnp.int32)
            row = lax.shift_right_arithmetic(owner, log2(cols))
            col = owner & (cols - 1)
            place = row * TURNS + turn
            forward_ref[entry] = jnp.where(live, col * (rows * TURNS + 1) + place, -1)
            back_ref[entry] = jnp.where(live, owner * TURNS + turn, -1)
            line = jnp.where(live, (col - me) & (cols - 1), cols)
            mine = block & (seg - 1)
            wanted_ref[line, jnp.where(live, place, 0)] = mine
            code_ref[owner] = code_ref[owner] + jnp.where(turn == 0, base, 1) * (mine - seg)
        return 0

    lax.fori_loop(0, tiles, tile, 0)

    def find(i, free):
        return jnp.where(count_ref[i] < TURNS, i * TURNS + TURNS - 1, free)

    back_ref[tiles * slots] = lax.fori_loop(0, none, find, 0, unroll=8)
    for store in stores:
        store.start()
    for fetch in fetches[1:]:
        fetch.wait()
    parts = []
    for b in range(seg):
        at = slice(b * size, (b + 1) * size)
        for q in range(2):
            new = precond_ref[:, at] * excitation_ref[q, :, at]
            currents_ref[q, :, at] = new
            parts.append(new)
    rounded = jnp.concatenate(parts, axis=0).astype(jnp.bfloat16)
    line = lax.broadcasted_iota(jnp.int32, (exc, size), 0)

    def fill(r, _):
        tag = jnp.zeros((exc, size), jnp.float32)
        for c in range(cols):
            tag = jnp.where(line == c, code_ref[r * cols + c].astype(jnp.float32), tag)
        copies_ref[r, : seg * exc] = rounded
        copies_ref[r, seg * exc :] = tag.astype(jnp.bfloat16)
        return 0

    lax.fori_loop(0, rows, fill, 0)
    for store in stores:
        store.wait()


def start(me, visible, excitation, precond, rows, cols, size):
    count = visible.size
    exc = 2 * excitation.shape[1]
    lines = excitation.shape[2] // size * exc
    return pl.pallas_call(
        functools.partial(start_kernel, rows, cols),
        out_shape=(
            jax.ShapeDtypeStruct((count,), jnp.int32),
            jax.ShapeDtypeStruct((count + 1,), jnp.int32),
            jax.ShapeDtypeStruct((cols + 1, 128), jnp.int32),
            jax.ShapeDtypeStruct(excitation.shape, jnp.float32),
            jax.ShapeDtypeStruct((rows, lines + exc, size), jnp.bfloat16),
        ),
        in_specs=[SMEM, HBM, HBM, HBM],
        out_specs=(HBM, HBM, SMEM, VMEM, VMEM),
        compiler_params=params(64),
        scratch_shapes=[
            pltpu.SMEM((rows * cols + 1,), jnp.int32),
            pltpu.SMEM((rows * cols + 1,), jnp.int32),
            pltpu.SMEM(visible.shape[::-1], jnp.int32),
            pltpu.VMEM(excitation.shape, jnp.float32),
            pltpu.VMEM((1, precond.size), jnp.float32),
            pltpu.SMEM((count,), jnp.int32),
            pltpu.SMEM((count + 1,), jnp.int32),
            pltpu.SemaphoreType.DMA((5,)),
        ],
        name="start",
    )(me, visible.T, excitation, precond[None, :])


def pack_kernel(me_ref, wanted_ref, group_ref, out_ref):
    cols, places, exc, size = out_ref.shape
    rows = group_ref.shape[0]
    seg = group_ref.shape[1] // exc - 1
    slots = places - 1
    me = me_ref[0]
    tags = [group_ref[r, seg * exc :].astype(jnp.float32) for r in range(rows)]
    for p in range(cols):
        tag = jnp.concatenate([tag[p : p + 1] for tag in tags], axis=0)
        out_ref[p, slots] = tag.astype(jnp.bfloat16)

    def peer(p, _):
        line = ((me - p) & (cols - 1)) * 128
        for s in range(slots):
            block = wanted_ref[line + s] & (seg - 1)
            out_ref[p, s] = group_ref[s // TURNS, pl.ds(pl.multiple_of(block * exc, exc), exc), :]
        return 0

    lax.fori_loop(0, cols, peer, 0)


def pack(me, wanted, group, cols, exc):
    rows, _, size = group.shape
    return pl.pallas_call(
        pack_kernel,
        out_shape=jax.ShapeDtypeStruct((cols, rows * TURNS + 1, exc, size), jnp.bfloat16),
        in_specs=[SMEM, SMEM, VMEM],
        out_specs=VMEM,
        compiler_params=params(16),
        name="pack",
    )(me, wanted, group)


def near_kernel(count, me_ref, index_ref, blocks_ref, *rest):
    group_refs, outs, (weights_ref, sems, gather_ref) = rest[:count], rest[count:-3], rest[-3:]
    cols = len(outs)
    rows, per_row, _, size, _ = blocks_ref.shape
    seg, exc = outs[0].shape[:2]
    half = exc // 2
    me = me_ref[0]
    peers = [(me + k) & (cols - 1) for k in range(cols)]
    order = list(range(1, cols)) + [0]
    copies = {}
    for k in order:
        some = pl.ds(pl.multiple_of(peers[k] * seg, seg), seg)
        copies[k] = pltpu.make_async_copy(blocks_ref.at[some], weights_ref.at[k], sems.at[k])
        copies[k].start()
    group_ref = group_refs[0]
    if count > 1:
        group_ref = gather_ref
        x, y = lax.shift_right_arithmetic(me_ref[1], log2(count)), me_ref[1] & (count - 1)
        for i in range(count):
            for j in range(count):
                source = ((x - i) & (count - 1)) * count + ((y - j) & (count - 1))
                gather_ref[source] = group_refs[i][j]
    for k in order:
        copies[k].wait()
        for i in range(seg):
            parts = []
            for j in range(per_row):
                block = index_ref[j, peers[k] * seg + i]
                line = pl.multiple_of((block & (seg - 1)) * exc, exc)
                parts.append(
                    group_ref[lax.shift_right_arithmetic(block, log2(seg)), pl.ds(line, exc), :]
                )
            weights = [weights_ref[k, i, j].reshape(2 * size, size) for j in range(per_row)]
            total = dot_t(jnp.concatenate(parts, axis=1), jnp.concatenate(weights, axis=1))
            by_re, by_im = total[:, :size], total[:, size:]
            sums = [by_re[:half] - by_im[half:], by_re[half:] + by_im[:half]]
            outs[k][i] = jnp.concatenate(sums, axis=0).astype(outs[k].dtype)


def near_sums(me, index, blocks, groups, seg, exc):
    rows, per_row, _, size, _ = blocks.shape
    cols = rows // seg
    count = len(groups)
    gather = (count * count, seg * exc, size) if count > 1 else (1, exc, size)
    return pl.pallas_call(
        functools.partial(near_kernel, count),
        out_shape=[
            jax.ShapeDtypeStruct((seg, exc, size), jnp.bfloat16 if k else jnp.float32)
            for k in range(cols)
        ],
        in_specs=[SMEM, SMEM, pl.BlockSpec(memory_space=pl.ANY)] + [VMEM] * count,
        out_specs=[VMEM] * cols,
        scratch_shapes=[
            pltpu.VMEM((cols, seg) + blocks.shape[1:], jnp.bfloat16),
            pltpu.SemaphoreType.DMA((cols,)),
            pltpu.VMEM(gather, jnp.bfloat16),
        ],
        compiler_params=params(57),
        cost_estimate=pl.CostEstimate(
            flops=2 * exc * blocks.size, bytes_accessed=2 * blocks.size, transcendentals=0
        ),
        name="near",
    )(me, index, blocks, *groups)


def optics_kernel(
    forward_ref, back_ref, x_ref, reflect_ref, coupling_ref, facet_ref, out_ref, weights_ref, sems
):
    tiles, slots, _, facets, size = coupling_ref.shape
    exc = x_ref.shape[1]
    half = exc // 2
    group = 4
    free = back_ref[back_ref.shape[0] - 1]

    def fetch(t):
        return pltpu.make_async_copy(coupling_ref.at[t], weights_ref.at[t], sems.at[t])

    for t in range(tiles):
        fetch(t).start()

    def weights(t, v):
        pair = [weights_ref[t, u].reshape(2 * facets, size) for u in (v, v + 1)]
        return jnp.concatenate(pair, axis=1)

    def some(g, _):
        rounded = []
        for i in range(group):
            fetch(g * group + i).wait()
        for i in range(group):
            t = g * group + i
            total = None
            for v in range(0, slots, 2):
                parts = []
                for u in (v, v + 1):
                    slot = forward_ref[t * slots + u]
                    live = slot >= 0
                    x = x_ref[jnp.where(live, slot, 0)]
                    parts.append(jnp.where(live, x, jnp.zeros_like(x)))
                product = dot_t(jnp.concatenate(parts, axis=1), weights(t, v))
                total = product if total is None else total + product
            by_re, by_im = total[:, :facets], total[:, facets:]
            inc_re = by_re[:half] - by_im[half:]
            inc_im = by_re[half:] + by_im[:half]
            lanes = pl.ds(pl.multiple_of(t * facets, facets), facets)
            coef_re, coef_im = reflect_ref[0:1, lanes], reflect_ref[1:2, lanes]
            out_re = coef_re * inc_re - coef_im * inc_im
            out_im = coef_re * inc_im + coef_im * inc_re
            facet_ref[0, :, lanes] = out_re
            facet_ref[1, :, lanes] = out_im
            both = [
                jnp.concatenate([out_re, -out_im], axis=1),
                jnp.concatenate([out_im, out_re], axis=1),
            ]
            rounded.append(jnp.concatenate(both, axis=0).astype(jnp.bfloat16))
        for i in range(group):
            t = g * group + i
            for v in range(0, slots, 2):
                sums = jnp.dot(rounded[i], weights(t, v), preferred_element_type=jnp.float32)
                sums = sums.astype(jnp.bfloat16)
                for u in range(2):
                    slot = back_ref[t * slots + v + u]
                    slot = jnp.where(slot >= 0, slot, free)
                    out_ref[slot] = sums[:, u * size : (u + 1) * size]
        return 0

    lax.fori_loop(0, tiles // group, some, 0)


def optics(forward, back, coupling, x, reflect, devices):
    tiles, slots, _, facets, size = coupling.shape
    exc = x.shape[1]
    return pl.pallas_call(
        optics_kernel,
        out_shape=(
            jax.ShapeDtypeStruct((2, exc // 2, tiles * facets), jnp.float32),
            jax.ShapeDtypeStruct((devices * TURNS, exc, size), jnp.bfloat16),
        ),
        in_specs=[SMEM, SMEM, VMEM, VMEM, pl.BlockSpec(memory_space=pl.ANY)],
        out_specs=(VMEM, VMEM),
        scratch_shapes=[
            pltpu.VMEM(coupling.shape, jnp.bfloat16),
            pltpu.SemaphoreType.DMA((tiles,)),
        ],
        compiler_params=params(57),
        cost_estimate=pl.CostEstimate(
            flops=4 * exc * coupling.size, bytes_accessed=2 * coupling.size, transcendentals=0
        ),
        name="optics",
    )(forward, back, x, reflect, coupling)


def update_kernel(cols, tag_ref, back_ref, currents_ref, excitation_ref, precond_ref, *rest):
    near_refs, rest = rest[:cols], rest[cols:]
    out_ref, (total_ref, own_ref, sem) = rest[0], rest[-3:]
    own = pltpu.make_async_copy(near_refs[0], own_ref, sem)
    own.start()
    count, exc, size = back_ref.shape
    seg = near_refs[0].shape[0]
    half = exc // 2
    rows = count // (cols * TURNS)
    total = near_refs[1][...].astype(jnp.float32)
    for near_ref in near_refs[2:]:
        total += near_ref[...].astype(jnp.float32)
    total_ref[:seg] = total

    def seen(r):
        for c in range(cols):
            tag = tag_ref[c * rows + r]
            slot = (r * cols + c) * TURNS
            yield slot, lax.shift_right_arithmetic(tag, log2(2 * seg))
            yield slot + 1, tag & (2 * seg - 1)

    def add(r, _):
        for slot, block in seen(r):
            total_ref[block] = total_ref[block] + back_ref[slot].astype(jnp.float32)
        return 0

    lax.fori_loop(0, rows, add, 0)
    own.wait()
    for b in range(seg):
        lanes = slice(b * size, (b + 1) * size)
        scale = precond_ref[:, lanes]
        for q in range(2):
            some = slice(q * half, (q + 1) * half)
            part = total_ref[b, some] + own_ref[b, some]
            new = currents_ref[q, :, lanes] + scale * (excitation_ref[q, :, lanes] - part)
            out_ref[q, :, lanes] = new
            if len(rest) > 4:
                total_ref[b, some] = new
    if len(rest) > 4:
        rounded_ref, sent_ref = rest[1:3]
        for b in range(seg):
            rounded_ref[b * exc : (b + 1) * exc] = total_ref[b].astype(jnp.bfloat16)

        def fill(r, _):
            for slot, block in seen(r):
                line = pl.multiple_of((block & (seg - 1)) * exc, exc)
                sent_ref[slot] = rounded_ref[pl.ds(line, exc), :]
            return 0

        lax.fori_loop(0, rows, fill, 0)


def update(tags, back, near, currents, excitation, precond, last):
    seg, exc, size = near[0].shape
    out_shape = [jax.ShapeDtypeStruct(currents.shape, jnp.float32)]
    if not last:
        out_shape.append(jax.ShapeDtypeStruct((seg * exc, size), jnp.bfloat16))
        out_shape.append(jax.ShapeDtypeStruct(back.shape, jnp.bfloat16))
    return pl.pallas_call(
        functools.partial(update_kernel, len(near)),
        out_shape=out_shape,
        in_specs=[SMEM] + [VMEM] * 4 + [HBM] + [VMEM] * (len(near) - 1),
        out_specs=[VMEM] * len(out_shape),
        scratch_shapes=[
            pltpu.VMEM((seg + 1, exc, size), jnp.float32),
            pltpu.VMEM((seg, exc, size), jnp.float32),
            pltpu.SemaphoreType.DMA,
        ],
        compiler_params=params(16),
        name="update",
    )(tags, back, currents, excitation, precond[None, :], *near)


def along(x, k, cols):
    return lax.ppermute(x, "col", [(i, (i + k) % cols) for i in range(cols)])


def along_square(a, dx, dy, side):
    pairs = []
    for i in range(side):
        for j in range(side):
            pairs.append((i * side + j, (i + dx) % side * side + (j + dy) % side))
    return lax.ppermute(a, "row", pairs)


def all_devices(x, devices):
    slots, exc, size = x.shape
    sent = x.reshape(devices, slots // devices * exc, size)
    return lax.all_to_all(sent, ("row", "col"), 0, 0, tiled=True).reshape(x.shape)


def shards(excitation, precond, near_blocks, near_index, coupling, visible, reflect):
    exc = 2 * excitation.shape[1]
    size = coupling.shape[-1]
    seg = excitation.shape[2] // size
    rows, cols = lax.axis_size("row"), lax.axis_size("col")
    devices = rows * cols
    side = 1 << log2(rows) // 2

    me = jnp.stack([lax.axis_index("col"), lax.axis_index("row")]).astype(jnp.int32)
    forward, back, wanted, currents, copies = start(
        me, visible, excitation, precond, rows, cols, size
    )
    lines = [wanted[:1]]
    for k in range(1, cols):
        with jax.named_scope("wanted_exchange"):
            lines.append(along(wanted[k : k + 1], k, cols))
    wanted = jnp.concatenate(lines).reshape(-1)
    index = near_index[0].T
    rounded = sent = tags = None
    for iteration in range(ITERS):
        last = iteration == ITERS - 1
        if iteration == 0:
            with jax.named_scope("row_exchange"):
                groups = [lax.all_to_all(copies, "row", 0, 0, tiled=True)]
            packed = pack(me, wanted, groups[0], cols, exc)
            with jax.named_scope("col_exchange"):
                x = lax.all_to_all(packed, "col", 0, 0, tiled=True)
            tags = x[:, -1, :, 0].astype(jnp.int32).reshape(-1)
            x = x.reshape((-1,) + x.shape[2:])
        else:
            with jax.named_scope("forward_exchange"):
                x = all_devices(sent, devices)
            with jax.named_scope("row_gather"):
                line = [along_square(rounded, 0, k, side) for k in range(1, side)]
                x, line = lax.optimization_barrier((x, jnp.stack([rounded] + line)))
                groups = [line] + [along_square(line, k, 0, side) for k in range(1, side)]
            forward = back
        facets, sums = optics(forward, back, coupling, x, reflect, devices)
        sums, groups = lax.optimization_barrier((sums, groups))
        near = near_sums(me, index, near_blocks[0], groups, seg, exc)
        with jax.named_scope("near_exchange"):
            near = [near[0]] + [along(near[k], k, cols) for k in range(1, cols)]
        with jax.named_scope("back_exchange"):
            sums = all_devices(sums, devices)
        out = update(tags, sums, near, currents, excitation, precond, last)
        currents = out[0]
        if not last:
            rounded, sent = out[1:]
    return currents, facets


def solution(mesh):
    placed = (
        P(None, None, ("row", "col")),
        P(("row", "col")),
        P("col", "row", None, None, None, None),
        P("col", "row", None),
        P(("row", "col"), None, None, None, None),
        P(("row", "col"), None),
        P(None, ("row", "col")),
    )
    return jax.shard_map(
        shards,
        mesh=mesh,
        in_specs=placed,
        out_specs=(P(None, None, ("row", "col")), P(None, None, ("row", "col"))),
        check_vma=False,
    )
```

time: 1520 us -> 157 us (0.10)
  waiting for transfers between devices: 1370 us -> 29.7 us
  starting transfers between devices: 0.44 us -> 60.6 us
  Pallas kernels: 0 us -> 39.6 us
  other arithmetic: 39.3 us -> 1.65 us
  matrix products: 31.8 us -> 0 us
    reduce_scatter x4 -> x0, waiting for transfers between devices: 1280 us -> none  [the longest x2 1280 us: shards(): lax.psum_scatter(partial_all, ('row', 'col'), scatter_dimension=2, tiled=...]
    all_gather x2 -> x0, waiting for transfers between devices: 88.8 us -> none  [shards(): everything = lax.all_gather(rounded, ('row', 'col'), axis=2, tiled=True)]
    pallas_call x0 -> x8, Pallas kernels: none -> 39.6 us  [the longest x2 15.3 us: optics(): pl.pallas_call(optics_kernel, out_shape=(jax.ShapeDtypeStruct((2, exc //...]
    all_gather x2 -> x0, blocking collectives: 37 us -> none  [shards(): columns = lax.all_gather(rounded, 'row', axis=2, tiled=True)]
    ppermute x0 -> x27, starting transfers between devices: none -> 32.6 us  [the longest x21 26.6 us: along(): return lax.ppermute(x, 'col', [(i, (i + k) % cols) for i in range(cols)])]
    dot_general x6 -> x0, matrix products: 31.8 us -> none  [the longest x2 11.3 us: shards(): jnp.einsum('bkpij,qebkj->pqebi', near_blocks[0], chosen, preferred_elemen...]
    scatter-add x2 -> x0, other arithmetic: 30.2 us -> none  [shards(): partial_all.at[:, :, safe_ids, :].add(values).reshape(2, exc_count, -1)]
    all_to_all x0 -> x4, starting transfers between devices: none -> 28 us  [the longest x3 20.4 us: all_devices(): lax.all_to_all(sent, ('row', 'col'), 0, 0, tiled=True).reshape(x.shape)]
  transfers between devices with their start and end apart: 6 -> 31, of which waited for: 4 -> 12; matrix products, arithmetic and copies ran while one was open for 5% -> 1% of each run, Pallas kernels for 0% -> 13%
where the time goes in v2:
time: 157 us; the launch traced here: 156 us
  starting transfers between devices  60.6 us (39%)
  Pallas kernels  39.6 us (25%)
  waiting for transfers between devices  29.7 us (19%)
  blocking collectives  21.9 us (14%)
  local copies, waits for them, and re-layouts  1.84 us (1%)
  other arithmetic  1.65 us (1%)
    ppermute x21, starting transfers between devices, along(): return lax.ppermute(x, 'col', [(i, (i + k) % cols) for i in range(cols)])  26.6 us
    all_to_all x1, blocking collectives, shards(): x = lax.all_to_all(packed, 'col', 0, 0, tiled=True)  21.9 us
    all_to_all x3, starting transfers between devices, all_devices(): lax.all_to_all(sent, ('row', 'col'), 0, 0, tiled=True).reshape(x.shape)  20.4 us
    pallas_call x2, Pallas kernels, optics(): pl.pallas_call(optics_kernel, out_shape=(jax.ShapeDtypeStruct((2, exc //...  15.3 us
    ppermute x21, waiting for transfers between devices, along(): return lax.ppermute(x, 'col', [(i, (i + k) % cols) for i in range(cols)])  14.3 us
    pallas_call x2, Pallas kernels, near_sums(): pl.pallas_call(functools.partial(near_kernel, count), out_shape=[jax.Shap...  12.4 us
    ppermute x6, waiting for transfers between devices, along_square(): return lax.ppermute(a, 'row', pairs)  11.1 us
    all_to_all x1, starting transfers between devices, shards(): groups = [lax.all_to_all(copies, 'row', 0, 0, tiled=True)]  7.6 us
  transfers between devices with their start and end apart: 31, of which 12 were waited for; matrix products, arithmetic and copies ran while one was open for 1% of the time, Pallas kernels for 13%

profile of v2, /device:TPU:1, one launch (start us, length us, event | category | flops | bytes accessed | tf_op | source)
XLA Modules:
  0.0 156.5 jit_solution(17758150697265906389)
XLA Ops:
  0.6 0.7 pad_add_fusion.me_ref
  1.3 4.8 %start.1 = (s32[128]{0:T(128)}, s32[129]{0:T(256)}, s32[9,128]{1,0:T(8,128)}, f32[2,8,1024]{2,1,0:T(8,128)}, bf16[16,144,128]{2,1,0:T(8,128)(2,1)}) custom-call(s32[2]{0:T(128)} %pad_add_fusion.me_ref, s32[8,16]{1,0:T(8,128)} %bitcast.38, f32[2,8,1024]{2,1,0:T(8,128)} %excitation_ref.3, f32[1,1024]{1,0:T(1,128)} %bitcast.22), custom_call_target="tpu_custom_call" | custom-call | tf_op jit(solution)/shard_map/start/pallas_call | solution.py:117
  6.1 0.0 copy-start.12
  6.1 7.6 %all-to-all-start = ((bf16[16,144,128]{2,1,0:T(8,128)(2,1)}), bf16[16,144,128]{2,1,0:T(8,128)(2,1)S(1)}, u32[]{:S(2)}, u32[]{:S(2)}) async-start(bf16[16,144,128]{2,1,0:T(8,128)(2,1)} %get-tuple-element.39), calls=%async_computation | async-start | bytes 1179648 | tf_op jit(solution)/shard_map/row_exchange/all_to_all | solution.py:441
  13.8 1.0 collective-permute-start.6
  14.7 3.8 %collective-permute-start.5 = (s32[1,128]{1,0:T(1,128)S(1)}, s32[1,128]{1,0:T(1,128)S(1)}, u32[]{:S(2)}, u32[]{:S(2)}) collective-permute-start(s32[1,128]{1,0:T(1,128)S(1)} %get-tuple-element.75), channel_id=1, source_target_pairs={{0,6},{1,7},{2,0},{3,1},{4,2},{5,3},{6,4},{7,5},{8,14},{9,15},{10,... | collective-permute-start | bytes 1544 | tf_op jit(solution)/shard_map/wanted_exchange/ppermute | solution.py:401
  18.5 0.4 collective-permute-start.4
  18.9 2.5 %collective-permute-start.3 = (s32[1,128]{1,0:T(1,128)S(1)}, s32[1,128]{1,0:T(1,128)S(1)}, u32[]{:S(2)}, u32[]{:S(2)}) collective-permute-start(s32[1,128]{1,0:T(1,128)S(1)} %get-tuple-element.77), channel_id=1, source_target_pairs={{0,4},{1,5},{2,6},{3,7},{4,0},{5,1},{6,2},{7,3},{8,12},{9,13},{10,... | collective-permute-start | bytes 1544 | tf_op jit(solution)/shard_map/wanted_exchange/ppermute | solution.py:401
  21.4 0.6 collective-permute-start.2
  22.0 0.8 collective-permute-start.1
  22.8 0.0 collective-permute-done.5
  22.8 1.2 collective-permute-start
  24.0 1.7 %collective-permute-done.2 = s32[1,128]{1,0:T(1,128)S(1)} collective-permute-done((s32[1,128]{1,0:T(1,128)S(1)}, s32[1,128]{1,0:T(1,128)S(1)}, u32[]{:S(2)}, u32[]{:S(2)}) %collective-permute-start.2) | collective-permute-done | bytes 544 | tf_op jit(solution)/shard_map/wanted_exchange/ppermute | solution.py:401
  25.7 0.0 collective-permute-done
  25.8 1.1 pack.1
  26.9 21.9 %all_to_all.25 = bf16[8,33,16,128]{3,2,1,0:T(8,128)(2,1)} all-to-all(bf16[8,33,16,128]{3,2,1,0:T(8,128)(2,1)S(1)} %pack.1), channel_id=1, replica_groups=mesh['row'=16,'col'=8] {'col'}, dimensions={0} | all-to-all | bytes 2162688 | tf_op jit(solution)/shard_map/col_exchange/all_to_all | solution.py:444
  48.9 7.6 %optics.2 = (f32[2,8,2048]{2,1,0:T(8,128)}, bf16[256,16,128]{2,1,0:T(8,128)(2,1)}) custom-call(s32[128]{0:T(128)} %get-tuple-element.41.forward_ref, s32[129]{0:T(256)} %get-tuple-element.40.back_ref.forward_ref, bf16[264,16,128]{2,1,0:T(8,128)(2,1)} %bitcast.29, f32[2,2048]{1,0:T(2,128)} %reflect_ref.3, bf16[16,8,2,128,128]{4,3,2,1,0:T(8,128)(2,1)} %coupling_ref.3), custom_call_target="tpu_custom_call" | custom-call | flops 268435456 | bytes 8388608 | tf_op jit(solution)/shard_map/optics/pallas_call | solution.py:307
  56.5 6.2 %all-to-all-start.2 = ((bf16[128,32,128]{2,1,0:T(8,128)(2,1)}), bf16[128,32,128]{2,1,0:T(8,128)(2,1)S(1)}, u32[]{:S(2)}, u32[]{:S(2)}) async-start(bf16[128,32,128]{2,1,0:T(8,128)(2,1)} %bitcast.32), calls=%async_computation.2 | async-start | bytes 2097152 | tf_op jit(solution)/shard_map/back_exchange/all_to_all | solution.py:415
  62.7 0.0 copy-start.1
  62.7 0.0 copy-start.3
  62.7 0.0 copy-start.5
  62.7 6.2 %near.2 = (f32[8,16,128]{2,1,0:T(8,128)}, bf16[8,16,128]{2,1,0:T(8,128)(2,1)}, bf16[8,16,128]{2,1,0:T(8,128)(2,1)}, bf16[8,16,128]{2,1,0:T(8,128)(2,1)}, bf16[8,...) custom-call(s32[2]{0:T(128)} %pad_add_fusion.me_ref, ...), custom_call_target="tpu_custom_call" | custom-call | flops 134217728 | bytes 8388608 | tf_op jit(solution)/shard_map/near/pallas_call | solution.py:220
  68.9 1.8 %collective-permute-start.7 = (bf16[8,16,128]{2,1,0:T(8,128)(2,1)}, bf16[8,16,128]{2,1,0:T(8,128)(2,1)S(1)}, u32[]{:S(2)}, u32[]{:S(2)}) collective-permute-start(bf16[8,16,128]{2,1,0:T(8,128)(2,1)} %get-tuple-element.47), channel_id=1, source_target_pairs={{0,1},{1,2},{2,3},{3,4},{4,5},{5,6},{6,7},{7,0},{8,9},{9,10},{10,1... | collective-permute-start | bytes 98312 | tf_op jit(solution)/shard_map/near_exchange/ppermute | solution.py:401
  70.7 1.5 collective-permute-start.8
  72.1 1.9 %collective-permute-start.9 = (bf16[8,16,128]{2,1,0:T(8,128)(2,1)}, bf16[8,16,128]{2,1,0:T(8,128)(2,1)S(1)}, u32[]{:S(2)}, u32[]{:S(2)}) collective-permute-start(bf16[8,16,128]{2,1,0:T(8,128)(2,1)} %get-tuple-element.49), channel_id=1, source_target_pairs={{0,3},{1,4},{2,5},{3,6},{4,7},{5,0},{6,1},{7,2},{8,11},{9,12},{10,... | collective-permute-start | bytes 98312 | tf_op jit(solution)/shard_map/near_exchange/ppermute | solution.py:401
  74.0 0.0 collective-permute-start.10
  74.1 2.3 %collective-permute-start.11 = (bf16[8,16,128]{2,1,0:T(8,128)(2,1)}, bf16[8,16,128]{2,1,0:T(8,128)(2,1)S(1)}, u32[]{:S(2)}, u32[]{:S(2)}) collective-permute-start(bf16[8,16,128]{2,1,0:T(8,128)(2,1)} %get-tuple-element.51), channel_id=1, source_target_pairs={{0,5},{1,6},{2,7},{3,0},{4,1},{5,2},{6,3},{7,4},{8,13},{9,14},{10,... | collective-permute-start | bytes 98312 | tf_op jit(solution)/shard_map/near_exchange/ppermute | solution.py:401
  76.3 0.7 collective-permute-start.12
  77.1 3.1 %collective-permute-done.8.rest_2_ = bf16[8,16,128]{2,1,0:T(8,128)(2,1)S(1)} collective-permute-done((bf16[8,16,128]{2,1,0:T(8,128)(2,1)}, bf16[8,16,128]{2,1,0:T(8,128)(2,1)S(1)}, u32[]{:S(2)}, u32[]{:S(2)}) %collective-permute-start.8) | collective-permute-done | bytes 32800 | tf_op jit(solution)/shard_map/near_exchange/ppermute | solution.py:401
  80.2 0.0 collective-permute-start.13
  80.2 1.0 convert_reduce_fusion
  81.2 0.1 reshape.40.tag_ref
  81.2 0.0 collective-permute-done.9.rest_3_
  81.2 0.4 collective-permute-done.10.rest_4_
  81.6 0.6 collective-permute-done.11.rest_5_
  82.2 1.5 collective-permute-done.13.rest_7_
  83.8 0.0 copy-start.4
  83.8 0.8 copy-done.4
  84.6 3.5 %update.2 = (f32[2,8,1024]{2,1,0:T(8,128)S(1)}, bf16[128,128]{1,0:T(8,128)(2,1)S(1)}, bf16[256,16,128]{2,1,0:T(8,128)(2,1)}) custom-call(s32[128]{0:T(128)S(1)} %reshape.40.tag_ref, bf16[256,16,128]{2,1,0:T(8,128)(2,1)S(1)} %bitcast.20, f32[2,8,1024]{2,1,0:T(8,128)S(1)} %copy-done.3, f32[2,8,1024]{2,1,0:T(8,128)S(1)} %copy-done.1, f32[1,1024]{1,0:T(1,128)S(1)} %bitcast.23, ...), custom_call_target="tpu_custom_call" | custom-call | tf_op jit(solution)/shard_map/update/pallas_call | solution.py:385
  88.1 7.0 %all-to-all-start.3 = ((bf16[128,32,128]{2,1,0:T(8,128)(2,1)}), bf16[128,32,128]{2,1,0:T(8,128)(2,1)S(1)}, u32[]{:S(2)}, u32[]{:S(2)}) async-start(bf16[128,32,128]{2,1,0:T(8,128)(2,1)} %bitcast.11), calls=%async_computation.3 | async-start | bytes 2097152 | tf_op jit(solution)/shard_map/forward_exchange/all_to_all | solution.py:415
  95.0 2.7 %collective-permute-start.16 = (bf16[128,128]{1,0:T(8,128)(2,1)S(1)}, bf16[128,128]{1,0:T(8,128)(2,1)S(1)}, u32[]{:S(2)}, u32[]{:S(2)}) collective-permute-start(bf16[128,128]{1,0:T(8,128)(2,1)S(1)} %get-tuple-element.55), channel_id=1, source_target_pairs={{0,24},{8,0},{16,8},{24,16},{32,56},{40,32},{48,40},{56,48},{64,88... | collective-permute-start | bytes 98312 | tf_op jit(solution)/shard_map/row_gather/ppermute | solution.py:409
  97.7 0.5 collective-permute-start.15
  98.3 0.6 collective-permute-start.14
  98.8 3.0 %collective-permute-done.16 = bf16[128,128]{1,0:T(8,128)(2,1)S(1)} collective-permute-done((bf16[128,128]{1,0:T(8,128)(2,1)S(1)}, bf16[128,128]{1,0:T(8,128)(2,1)S(1)}, u32[]{:S(2)}, u32[]{:S(2)}) %collective-permute-start.16) | collective-permute-done | bytes 32800 | tf_op jit(solution)/shard_map/row_gather/ppermute | solution.py:409
  101.9 4.9 %collective-permute-done.15 = bf16[128,128]{1,0:T(8,128)(2,1)S(1)} collective-permute-done((bf16[128,128]{1,0:T(8,128)(2,1)S(1)}, bf16[128,128]{1,0:T(8,128)(2,1)S(1)}, u32[]{:S(2)}, u32[]{:S(2)}) %collective-permute-start.15) | collective-permute-done | bytes 32800 | tf_op jit(solution)/shard_map/row_gather/ppermute | solution.py:409
  106.8 3.2 %collective-permute-done.14 = bf16[128,128]{1,0:T(8,128)(2,1)S(1)} collective-permute-done((bf16[128,128]{1,0:T(8,128)(2,1)S(1)}, bf16[128,128]{1,0:T(8,128)(2,1)S(1)}, u32[]{:S(2)}, u32[]{:S(2)}) %collective-permute-start.14) | collective-permute-done | bytes 32800 | tf_op jit(solution)/shard_map/row_gather/ppermute | solution.py:409
  109.9 4.4 %all-to-all-done.3 = bf16[128,32,128]{2,1,0:T(8,128)(2,1)S(1)} async-done(((bf16[128,32,128]{2,1,0:T(8,128)(2,1)}), bf16[128,32,128]{2,1,0:T(8,128)(2,1)S(1)}, u32[]{:S(2)}, u32[]{:S(2)}) %all-to-all-start.3) | async-done | bytes 1048608 | tf_op jit(solution)/shard_map/forward_exchange/all_to_all | solution.py:415
  114.3 0.9 collective-permute-start.19
  115.2 1.2 collective-permute-start.18
  116.4 7.6 %optics.3 = (f32[2,8,2048]{2,1,0:T(8,128)}, bf16[256,16,128]{2,1,0:T(8,128)(2,1)}) custom-call(s32[129]{0:T(256)} %get-tuple-element.40.back_ref.forward_ref, s32[129]{0:T(256)} %get-tuple-element.40.back_ref.forward_ref, bf16[256,16,128]{2,1,0:T(8,128)(2,1)} %bitcast.30, f32[2,2048]{1,0:T(2,128)} %reflect_ref.3, bf16[16,8,2,128,128]{4,3,2,1,0:T(8,128)(2,1)} %coupling_ref.3), custom_call_target="tpu_custom_call" | custom-call | flops 268435456 | bytes 8388608 | tf_op jit(solution)/shard_map/optics/pallas_call | solution.py:307
  124.1 0.0 collective-permute-done.19.rest_3_
  124.1 7.3 %all-to-all-start.4 = ((bf16[128,32,128]{2,1,0:T(8,128)(2,1)}), bf16[128,32,128]{2,1,0:T(8,128)(2,1)S(1)}, u32[]{:S(2)}, u32[]{:S(2)}) async-start(bf16[128,32,128]{2,1,0:T(8,128)(2,1)} %bitcast.31), calls=%async_computation.4 | async-start | bytes 2097152 | tf_op jit(solution)/shard_map/back_exchange/all_to_all | solution.py:415
  131.5 6.2 %near.3 = (f32[8,16,128]{2,1,0:T(8,128)}, bf16[8,16,128]{2,1,0:T(8,128)(2,1)}, bf16[8,16,128]{2,1,0:T(8,128)(2,1)}, bf16[8,16,128]{2,1,0:T(8,128)(2,1)}, bf16[8,...) custom-call(s32[2]{0:T(128)} %pad_add_fusion.me_ref, ...), custom_call_target="tpu_custom_call" | custom-call | flops 134217728 | bytes 8388608 | tf_op jit(solution)/shard_map/near/pallas_call | solution.py:220
  137.7 1.8 %collective-permute-start.20 = (bf16[8,16,128]{2,1,0:T(8,128)(2,1)}, bf16[8,16,128]{2,1,0:T(8,128)(2,1)S(1)}, u32[]{:S(2)}, u32[]{:S(2)}) collective-permute-start(bf16[8,16,128]{2,1,0:T(8,128)(2,1)} %get-tuple-element.66), channel_id=1, source_target_pairs={{0,1},{1,2},{2,3},{3,4},{4,5},{5,6},{6,7},{7,0},{8,9},{9,10},{10,1... | collective-permute-start | bytes 98312 | tf_op jit(solution)/shard_map/near_exchange/ppermute | solution.py:401
  139.5 1.5 collective-permute-start.21
  140.9 1.9 %collective-permute-start.22 = (bf16[8,16,128]{2,1,0:T(8,128)(2,1)}, bf16[8,16,128]{2,1,0:T(8,128)(2,1)S(1)}, u32[]{:S(2)}, u32[]{:S(2)}) collective-permute-start(bf16[8,16,128]{2,1,0:T(8,128)(2,1)} %get-tuple-element.68), channel_id=1, source_target_pairs={{0,3},{1,4},{2,5},{3,6},{4,7},{5,0},{6,1},{7,2},{8,11},{9,12},{10,... | collective-permute-start | bytes 98312 | tf_op jit(solution)/shard_map/near_exchange/ppermute | solution.py:401
  142.8 0.1 collective-permute-start.23
  142.9 2.4 %collective-permute-start.24 = (bf16[8,16,128]{2,1,0:T(8,128)(2,1)}, bf16[8,16,128]{2,1,0:T(8,128)(2,1)S(1)}, u32[]{:S(2)}, u32[]{:S(2)}) collective-permute-start(bf16[8,16,128]{2,1,0:T(8,128)(2,1)} %get-tuple-element.70), channel_id=1, source_target_pairs={{0,5},{1,6},{2,7},{3,0},{4,1},{5,2},{6,3},{7,4},{8,13},{9,14},{10,... | collective-permute-start | bytes 98312 | tf_op jit(solution)/shard_map/near_exchange/ppermute | solution.py:401
  145.3 0.6 collective-permute-start.25
  145.9 3.4 %collective-permute-done.21.rest_2_ = bf16[8,16,128]{2,1,0:T(8,128)(2,1)S(1)} collective-permute-done((bf16[8,16,128]{2,1,0:T(8,128)(2,1)}, bf16[8,16,128]{2,1,0:T(8,128)(2,1)S(1)}, u32[]{:S(2)}, u32[]{:S(2)}) %collective-permute-start.21) | collective-permute-done | bytes 32800 | tf_op jit(solution)/shard_map/near_exchange/ppermute | solution.py:401
  149.3 1.9 %collective-permute-done.22.rest_3_ = bf16[8,16,128]{2,1,0:T(8,128)(2,1)S(1)} collective-permute-done((bf16[8,16,128]{2,1,0:T(8,128)(2,1)}, bf16[8,16,128]{2,1,0:T(8,128)(2,1)S(1)}, u32[]{:S(2)}, u32[]{:S(2)}) %collective-permute-start.22) | collective-permute-done | bytes 32800 | tf_op jit(solution)/shard_map/near_exchange/ppermute | solution.py:401
  151.3 1.6 %collective-permute-done.26.rest_7_ = bf16[8,16,128]{2,1,0:T(8,128)(2,1)S(1)} collective-permute-done((bf16[8,16,128]{2,1,0:T(8,128)(2,1)}, bf16[8,16,128]{2,1,0:T(8,128)(2,1)S(1)}, u32[]{:S(2)}, u32[]{:S(2)}) %collective-permute-start.26) | collective-permute-done | bytes 32800 | tf_op jit(solution)/shard_map/near_exchange/ppermute | solution.py:401
  152.9 0.8 copy-done.2
  153.7 2.6 %update.3 = f32[2,8,1024]{2,1,0:T(8,128)} custom-call(s32[128]{0:T(128)S(1)} %reshape.40.tag_ref, bf16[256,16,128]{2,1,0:T(8,128)(2,1)S(1)} %bitcast.21, f32[2,8,1024]{2,1,0:T(8,128)S(1)} %get-tuple-element.60.currents_ref, f32[2,8,1024]{2,1,0:T(8,128)S(1)} %copy-done.1, f32[1,1024]{1,0:T(1,128)S(1)} %bitcast.24, f32[8,16,128]{2,1,0:T(8,128)S(1)} %copy-done.2, ...), custom_call_target="tpu_custom_call" | custom-call | tf_op jit(solution)/shard_map/update/pallas_call | solution.py:385
  (39 shorter events, 0.1 us)
Async XLA Ops:
  6.1 7.6 %copy-start.12 = (s32[9,128]{1,0:T(8,128)S(1)}, s32[9,128]{1,0:T(8,128)}, u32[]{:S(2)}) copy-start(s32[9,128]{1,0:T(8,128)} %get-tuple-element.38) | copy-start | bytes 13828
  6.1 19.6 %copy-start.6 = (s32[2]{0:T(128)S(1)}, s32[2]{0:T(128)}, u32[]{:S(2)}) copy-start(s32[2]{0:T(128)} %pad_add_fusion.me_ref) | copy-start | bytes 28
  6.1 19.6 %all-to-all-start = ((bf16[16,144,128]{2,1,0:T(8,128)(2,1)}), bf16[16,144,128]{2,1,0:T(8,128)(2,1)S(1)}, u32[]{:S(2)}, u32[]{:S(2)}) async-start(bf16[16,144,128]{2,1,0:T(8,128)(2,1)} %get-tuple-element.39), calls=%async_computation | async-start | bytes 1179648 | tf_op jit(solution)/shard_map/row_exchange/all_to_all | solution.py:441
  13.8 8.2 %collective-permute-start.6 = (s32[1,128]{1,0:T(1,128)S(1)}, s32[1,128]{1,0:T(1,128)S(1)}, u32[]{:S(2)}, u32[]{:S(2)}) collective-permute-start(s32[1,128]{1,0:T(1,128)S(1)} %get-tuple-element.74), channel_id=1, source_target_pairs={{0,7},{1,0},{2,1},{3,2},{4,3},{5,4},{6,5},{7,6},{8,15},{9,8},{10,9... | collective-permute-start | bytes 1544 | tf_op jit(solution)/shard_map/wanted_exchange/ppermute | solution.py:401
  14.7 8.1 %collective-permute-start.5 = (s32[1,128]{1,0:T(1,128)S(1)}, s32[1,128]{1,0:T(1,128)S(1)}, u32[]{:S(2)}, u32[]{:S(2)}) collective-permute-start(s32[1,128]{1,0:T(1,128)S(1)} %get-tuple-element.75), channel_id=1, source_target_pairs={{0,6},{1,7},{2,0},{3,1},{4,2},{5,3},{6,4},{7,5},{8,14},{9,15},{10,... | collective-permute-start | bytes 1544 | tf_op jit(solution)/shard_map/wanted_exchange/ppermute | solution.py:401
  18.5 5.5 %collective-permute-start.4 = (s32[1,128]{1,0:T(1,128)S(1)}, s32[1,128]{1,0:T(1,128)S(1)}, u32[]{:S(2)}, u32[]{:S(2)}) collective-permute-start(s32[1,128]{1,0:T(1,128)S(1)} %get-tuple-element.76), channel_id=1, source_target_pairs={{0,5},{1,6},{2,7},{3,0},{4,1},{5,2},{6,3},{7,4},{8,13},{9,14},{10,... | collective-permute-start | bytes 1544 | tf_op jit(solution)/shard_map/wanted_exchange/ppermute | solution.py:401
  18.9 5.2 %collective-permute-start.3 = (s32[1,128]{1,0:T(1,128)S(1)}, s32[1,128]{1,0:T(1,128)S(1)}, u32[]{:S(2)}, u32[]{:S(2)}) collective-permute-start(s32[1,128]{1,0:T(1,128)S(1)} %get-tuple-element.77), channel_id=1, source_target_pairs={{0,4},{1,5},{2,6},{3,7},{4,0},{5,1},{6,2},{7,3},{8,12},{9,13},{10,... | collective-permute-start | bytes 1544 | tf_op jit(solution)/shard_map/wanted_exchange/ppermute | solution.py:401
  21.4 4.4 %collective-permute-start.2 = (s32[1,128]{1,0:T(1,128)S(1)}, s32[1,128]{1,0:T(1,128)S(1)}, u32[]{:S(2)}, u32[]{:S(2)}) collective-permute-start(s32[1,128]{1,0:T(1,128)S(1)} %get-tuple-element.78), channel_id=1, source_target_pairs={{0,3},{1,4},{2,5},{3,6},{4,7},{5,0},{6,1},{7,2},{8,11},{9,12},{10,... | collective-permute-start | bytes 1544 | tf_op jit(solution)/shard_map/wanted_exchange/ppermute | solution.py:401
  22.0 3.7 %collective-permute-start.1 = (s32[1,128]{1,0:T(1,128)S(1)}, s32[1,128]{1,0:T(1,128)S(1)}, u32[]{:S(2)}, u32[]{:S(2)}) collective-permute-start(s32[1,128]{1,0:T(1,128)S(1)} %get-tuple-element.79), channel_id=1, source_target_pairs={{0,2},{1,3},{2,4},{3,5},{4,6},{5,7},{6,0},{7,1},{8,10},{9,11},{10,... | collective-permute-start | bytes 1544 | tf_op jit(solution)/shard_map/wanted_exchange/ppermute | solution.py:401
  22.8 2.9 %collective-permute-start = (s32[1,128]{1,0:T(1,128)S(1)}, s32[1,128]{1,0:T(1,128)S(1)}, u32[]{:S(2)}, u32[]{:S(2)}) collective-permute-start(s32[1,128]{1,0:T(1,128)S(1)} %get-tuple-element.80), channel_id=1, source_target_pairs={{0,1},{1,2},{2,3},{3,4},{4,5},{5,6},{6,7},{7,0},{8,9},{9,10},{10,1... | collective-permute-start | bytes 1544 | tf_op jit(solution)/shard_map/wanted_exchange/ppermute | solution.py:401
  25.8 23.1 %copy-start = (bf16[16,144,128]{2,1,0:T(8,128)(2,1)}, bf16[16,144,128]{2,1,0:T(8,128)(2,1)S(1)}, u32[]{:S(2)}) copy-start(bf16[16,144,128]{2,1,0:T(8,128)(2,1)S(1)} %all-to-all-done.group_ref.rest_0_) | copy-start | bytes 1769476
  56.5 27.2 %all-to-all-start.2 = ((bf16[128,32,128]{2,1,0:T(8,128)(2,1)}), bf16[128,32,128]{2,1,0:T(8,128)(2,1)S(1)}, u32[]{:S(2)}, u32[]{:S(2)}) async-start(bf16[128,32,128]{2,1,0:T(8,128)(2,1)} %bitcast.32), calls=%async_computation.2 | async-start | bytes 2097152 | tf_op jit(solution)/shard_map/back_exchange/all_to_all | solution.py:415
  62.7 21.1 %copy-start.1 = (f32[2,8,1024]{2,1,0:T(8,128)S(1)}, f32[2,8,1024]{2,1,0:T(8,128)}, u32[]{:S(2)}) copy-start(f32[2,8,1024]{2,1,0:T(8,128)} %excitation_ref.3) | copy-start | bytes 196612
  62.7 21.1 %copy-start.3 = (f32[2,8,1024]{2,1,0:T(8,128)S(1)}, f32[2,8,1024]{2,1,0:T(8,128)}, u32[]{:S(2)}) copy-start(f32[2,8,1024]{2,1,0:T(8,128)} %get-tuple-element.44.currents_ref) | copy-start | bytes 196612
  62.7 21.1 %copy-start.5 = (f32[1024]{0:T(1024)S(1)}, f32[1024]{0:T(1024)}, u32[]{:S(2)}) copy-start(f32[1024]{0:T(1024)} %param.8) | copy-start | bytes 12292
  68.9 7.5 %collective-permute-start.7 = (bf16[8,16,128]{2,1,0:T(8,128)(2,1)}, bf16[8,16,128]{2,1,0:T(8,128)(2,1)S(1)}, u32[]{:S(2)}, u32[]{:S(2)}) collective-permute-start(bf16[8,16,128]{2,1,0:T(8,128)(2,1)} %get-tuple-element.47), channel_id=1, source_target_pairs={{0,1},{1,2},{2,3},{3,4},{4,5},{5,6},{6,7},{7,0},{8,9},{9,10},{10,1... | collective-permute-start | bytes 98312 | tf_op jit(solution)/shard_map/near_exchange/ppermute | solution.py:401
  70.7 9.5 %collective-permute-start.8 = (bf16[8,16,128]{2,1,0:T(8,128)(2,1)}, bf16[8,16,128]{2,1,0:T(8,128)(2,1)S(1)}, u32[]{:S(2)}, u32[]{:S(2)}) collective-permute-start(bf16[8,16,128]{2,1,0:T(8,128)(2,1)} %get-tuple-element.48), channel_id=1, source_target_pairs={{0,2},{1,3},{2,4},{3,5},{4,6},{5,7},{6,0},{7,1},{8,10},{9,11},{10,... | collective-permute-start | bytes 98312 | tf_op jit(solution)/shard_map/near_exchange/ppermute | solution.py:401
  72.1 9.1 %collective-permute-start.9 = (bf16[8,16,128]{2,1,0:T(8,128)(2,1)}, bf16[8,16,128]{2,1,0:T(8,128)(2,1)S(1)}, u32[]{:S(2)}, u32[]{:S(2)}) collective-permute-start(bf16[8,16,128]{2,1,0:T(8,128)(2,1)} %get-tuple-element.49), channel_id=1, source_target_pairs={{0,3},{1,4},{2,5},{3,6},{4,7},{5,0},{6,1},{7,2},{8,11},{9,12},{10,... | collective-permute-start | bytes 98312 | tf_op jit(solution)/shard_map/near_exchange/ppermute | solution.py:401
  74.0 7.6 %collective-permute-start.10 = (bf16[8,16,128]{2,1,0:T(8,128)(2,1)}, bf16[8,16,128]{2,1,0:T(8,128)(2,1)S(1)}, u32[]{:S(2)}, u32[]{:S(2)}) collective-permute-start(bf16[8,16,128]{2,1,0:T(8,128)(2,1)} %get-tuple-element.50), channel_id=1, source_target_pairs={{0,4},{1,5},{2,6},{3,7},{4,0},{5,1},{6,2},{7,3},{8,12},{9,13},{10,... | collective-permute-start | bytes 98312 | tf_op jit(solution)/shard_map/near_exchange/ppermute | solution.py:401
  74.1 8.2 %collective-permute-start.11 = (bf16[8,16,128]{2,1,0:T(8,128)(2,1)}, bf16[8,16,128]{2,1,0:T(8,128)(2,1)S(1)}, u32[]{:S(2)}, u32[]{:S(2)}) collective-permute-start(bf16[8,16,128]{2,1,0:T(8,128)(2,1)} %get-tuple-element.51), channel_id=1, source_target_pairs={{0,5},{1,6},{2,7},{3,0},{4,1},{5,2},{6,3},{7,4},{8,13},{9,14},{10,... | collective-permute-start | bytes 98312 | tf_op jit(solution)/shard_map/near_exchange/ppermute | solution.py:401
  76.3 5.9 %collective-permute-start.12 = (bf16[8,16,128]{2,1,0:T(8,128)(2,1)}, bf16[8,16,128]{2,1,0:T(8,128)(2,1)S(1)}, u32[]{:S(2)}, u32[]{:S(2)}) collective-permute-start(bf16[8,16,128]{2,1,0:T(8,128)(2,1)} %get-tuple-element.52), channel_id=1, source_target_pairs={{0,6},{1,7},{2,0},{3,1},{4,2},{5,3},{6,4},{7,5},{8,14},{9,15},{10,... | collective-permute-start | bytes 98312 | tf_op jit(solution)/shard_map/near_exchange/ppermute | solution.py:401
  80.2 3.6 %collective-permute-start.13 = (bf16[8,16,128]{2,1,0:T(8,128)(2,1)}, bf16[8,16,128]{2,1,0:T(8,128)(2,1)S(1)}, u32[]{:S(2)}, u32[]{:S(2)}) collective-permute-start(bf16[8,16,128]{2,1,0:T(8,128)(2,1)} %get-tuple-element.53), channel_id=1, source_target_pairs={{0,7},{1,0},{2,1},{3,2},{4,3},{5,4},{6,5},{7,6},{8,15},{9,8},{10,9... | collective-permute-start | bytes 98312 | tf_op jit(solution)/shard_map/near_exchange/ppermute | solution.py:401
  83.8 0.8 copy-start.4
  88.1 26.2 %all-to-all-start.3 = ((bf16[128,32,128]{2,1,0:T(8,128)(2,1)}), bf16[128,32,128]{2,1,0:T(8,128)(2,1)S(1)}, u32[]{:S(2)}, u32[]{:S(2)}) async-start(bf16[128,32,128]{2,1,0:T(8,128)(2,1)} %bitcast.11), calls=%async_computation.3 | async-start | bytes 2097152 | tf_op jit(solution)/shard_map/forward_exchange/all_to_all | solution.py:415
  95.0 6.8 %collective-permute-start.16 = (bf16[128,128]{1,0:T(8,128)(2,1)S(1)}, bf16[128,128]{1,0:T(8,128)(2,1)S(1)}, u32[]{:S(2)}, u32[]{:S(2)}) collective-permute-start(bf16[128,128]{1,0:T(8,128)(2,1)S(1)} %get-tuple-element.55), channel_id=1, source_target_pairs={{0,24},{8,0},{16,8},{24,16},{32,56},{40,32},{48,40},{56,48},{64,88... | collective-permute-start | bytes 98312 | tf_op jit(solution)/shard_map/row_gather/ppermute | solution.py:409
  97.7 9.0 %collective-permute-start.15 = (bf16[128,128]{1,0:T(8,128)(2,1)S(1)}, bf16[128,128]{1,0:T(8,128)(2,1)S(1)}, u32[]{:S(2)}, u32[]{:S(2)}) collective-permute-start(bf16[128,128]{1,0:T(8,128)(2,1)S(1)} %get-tuple-element.55), channel_id=1, source_target_pairs={{0,16},{8,24},{16,0},{24,8},{32,48},{40,56},{48,32},{56,40},{64,80... | collective-permute-start | bytes 98312 | tf_op jit(solution)/shard_map/row_gather/ppermute | solution.py:409
  98.3 11.6 %collective-permute-start.14 = (bf16[128,128]{1,0:T(8,128)(2,1)S(1)}, bf16[128,128]{1,0:T(8,128)(2,1)S(1)}, u32[]{:S(2)}, u32[]{:S(2)}) collective-permute-start(bf16[128,128]{1,0:T(8,128)(2,1)S(1)} %get-tuple-element.55), channel_id=1, source_target_pairs={{0,8},{8,16},{16,24},{24,0},{32,40},{40,48},{48,56},{56,32},{64,72... | collective-permute-start | bytes 98312 | tf_op jit(solution)/shard_map/row_gather/ppermute | solution.py:409
  109.9 14.1 %copy-start.8 = (bf16[4,128,128]{2,1,0:T(8,128)(2,1)}, bf16[4,128,128]{2,1,0:T(8,128)(2,1)S(1)}, u32[]{:S(2)}) copy-start(bf16[4,128,128]{2,1,0:T(8,128)(2,1)S(1)} %pad_maximum_fusion.rest_0_) | copy-start | bytes 393220
  114.3 2.1 %copy-start.7 = (bf16[128,32,128]{2,1,0:T(8,128)(2,1)}, bf16[128,32,128]{2,1,0:T(8,128)(2,1)S(1)}, u32[]{:S(2)}) copy-start(bf16[128,32,128]{2,1,0:T(8,128)(2,1)S(1)} %all-to-all-done.3) | copy-start | bytes 3145732
  114.3 9.8 %collective-permute-start.19 = (bf16[4,128,128]{2,1,0:T(8,128)(2,1)S(1)}, bf16[4,128,128]{2,1,0:T(8,128)(2,1)S(1)}, u32[]{:S(2)}, u32[]{:S(2)}) collective-permute-start(bf16[4,128,128]{2,1,0:T(8,128)(2,1)S(1)} %pad_maximum_fusion.rest_0_), channel_id=1, source_target_pairs={{0,96},{8,104},{16,112},{24,120},{32,0},{40,8},{48,16},{56,24},{64... | collective-permute-start | bytes 393224 | tf_op jit(solution)/shard_map/row_gather/ppermute | solution.py:409
  115.2 8.9 %collective-permute-start.18 = (bf16[4,128,128]{2,1,0:T(8,128)(2,1)S(1)}, bf16[4,128,128]{2,1,0:T(8,128)(2,1)S(1)}, u32[]{:S(2)}, u32[]{:S(2)}) collective-permute-start(bf16[4,128,128]{2,1,0:T(8,128)(2,1)S(1)} %pad_maximum_fusion.rest_0_), channel_id=1, source_target_pairs={{0,64},{8,72},{16,80},{24,88},{32,96},{40,104},{48,112},{56,120},{... | collective-permute-start | bytes 393224 | tf_op jit(solution)/shard_map/row_gather/ppermute | solution.py:409
  116.4 7.7 %collective-permute-start.17 = (bf16[4,128,128]{2,1,0:T(8,128)(2,1)S(1)}, bf16[4,128,128]{2,1,0:T(8,128)(2,1)S(1)}, u32[]{:S(2)}, u32[]{:S(2)}) collective-permute-start(bf16[4,128,128]{2,1,0:T(8,128)(2,1)S(1)} %pad_maximum_fusion.rest_0_), channel_id=1, source_target_pairs={{0,32},{8,40},{16,48},{24,56},{32,64},{40,72},{48,80},{56,88},{64,... | collective-permute-start | bytes 393224 | tf_op jit(solution)/shard_map/row_gather/ppermute | solution.py:409
  124.1 7.4 %copy-start.9 = (bf16[4,128,128]{2,1,0:T(8,128)(2,1)}, bf16[4,128,128]{2,1,0:T(8,128)(2,1)S(1)}, u32[]{:S(2)}) copy-start(bf16[4,128,128]{2,1,0:T(8,128)(2,1)S(1)} %collective-permute-done.19.rest_3_) | copy-start | bytes 393220
  124.1 7.4 %copy-start.10 = (bf16[4,128,128]{2,1,0:T(8,128)(2,1)}, bf16[4,128,128]{2,1,0:T(8,128)(2,1)S(1)}, u32[]{:S(2)}) copy-start(bf16[4,128,128]{2,1,0:T(8,128)(2,1)S(1)} %collective-permute-done.18.rest_2_) | copy-start | bytes 393220
  124.1 7.4 %copy-start.11 = (bf16[4,128,128]{2,1,0:T(8,128)(2,1)}, bf16[4,128,128]{2,1,0:T(8,128)(2,1)S(1)}, u32[]{:S(2)}) copy-start(bf16[4,128,128]{2,1,0:T(8,128)(2,1)S(1)} %collective-permute-done.17.rest_1_) | copy-start | bytes 393220
  124.1 28.8 %all-to-all-start.4 = ((bf16[128,32,128]{2,1,0:T(8,128)(2,1)}), bf16[128,32,128]{2,1,0:T(8,128)(2,1)S(1)}, u32[]{:S(2)}, u32[]{:S(2)}) async-start(bf16[128,32,128]{2,1,0:T(8,128)(2,1)} %bitcast.31), calls=%async_computation.4 | async-start | bytes 2097152 | tf_op jit(solution)/shard_map/back_exchange/all_to_all | solution.py:415
  137.7 7.6 %collective-permute-start.20 = (bf16[8,16,128]{2,1,0:T(8,128)(2,1)}, bf16[8,16,128]{2,1,0:T(8,128)(2,1)S(1)}, u32[]{:S(2)}, u32[]{:S(2)}) collective-permute-start(bf16[8,16,128]{2,1,0:T(8,128)(2,1)} %get-tuple-element.66), channel_id=1, source_target_pairs={{0,1},{1,2},{2,3},{3,4},{4,5},{5,6},{6,7},{7,0},{8,9},{9,10},{10,1... | collective-permute-start | bytes 98312 | tf_op jit(solution)/shard_map/near_exchange/ppermute | solution.py:401
  139.5 9.9 %collective-permute-start.21 = (bf16[8,16,128]{2,1,0:T(8,128)(2,1)}, bf16[8,16,128]{2,1,0:T(8,128)(2,1)S(1)}, u32[]{:S(2)}, u32[]{:S(2)}) collective-permute-start(bf16[8,16,128]{2,1,0:T(8,128)(2,1)} %get-tuple-element.67), channel_id=1, source_target_pairs={{0,2},{1,3},{2,4},{3,5},{4,6},{5,7},{6,0},{7,1},{8,10},{9,11},{10,... | collective-permute-start | bytes 98312 | tf_op jit(solution)/shard_map/near_exchange/ppermute | solution.py:401
  140.9 10.3 %collective-permute-start.22 = (bf16[8,16,128]{2,1,0:T(8,128)(2,1)}, bf16[8,16,128]{2,1,0:T(8,128)(2,1)S(1)}, u32[]{:S(2)}, u32[]{:S(2)}) collective-permute-start(bf16[8,16,128]{2,1,0:T(8,128)(2,1)} %get-tuple-element.68), channel_id=1, source_target_pairs={{0,3},{1,4},{2,5},{3,6},{4,7},{5,0},{6,1},{7,2},{8,11},{9,12},{10,... | collective-permute-start | bytes 98312 | tf_op jit(solution)/shard_map/near_exchange/ppermute | solution.py:401
  142.8 8.4 %collective-permute-start.23 = (bf16[8,16,128]{2,1,0:T(8,128)(2,1)}, bf16[8,16,128]{2,1,0:T(8,128)(2,1)S(1)}, u32[]{:S(2)}, u32[]{:S(2)}) collective-permute-start(bf16[8,16,128]{2,1,0:T(8,128)(2,1)} %get-tuple-element.69), channel_id=1, source_target_pairs={{0,4},{1,5},{2,6},{3,7},{4,0},{5,1},{6,2},{7,3},{8,12},{9,13},{10,... | collective-permute-start | bytes 98312 | tf_op jit(solution)/shard_map/near_exchange/ppermute | solution.py:401
  142.9 8.4 %collective-permute-start.24 = (bf16[8,16,128]{2,1,0:T(8,128)(2,1)}, bf16[8,16,128]{2,1,0:T(8,128)(2,1)S(1)}, u32[]{:S(2)}, u32[]{:S(2)}) collective-permute-start(bf16[8,16,128]{2,1,0:T(8,128)(2,1)} %get-tuple-element.70), channel_id=1, source_target_pairs={{0,5},{1,6},{2,7},{3,0},{4,1},{5,2},{6,3},{7,4},{8,13},{9,14},{10,... | collective-permute-start | bytes 98312 | tf_op jit(solution)/shard_map/near_exchange/ppermute | solution.py:401
  145.3 5.9 %collective-permute-start.25 = (bf16[8,16,128]{2,1,0:T(8,128)(2,1)}, bf16[8,16,128]{2,1,0:T(8,128)(2,1)S(1)}, u32[]{:S(2)}, u32[]{:S(2)}) collective-permute-start(bf16[8,16,128]{2,1,0:T(8,128)(2,1)} %get-tuple-element.71), channel_id=1, source_target_pairs={{0,6},{1,7},{2,0},{3,1},{4,2},{5,3},{6,4},{7,5},{8,14},{9,15},{10,... | collective-permute-start | bytes 98312 | tf_op jit(solution)/shard_map/near_exchange/ppermute | solution.py:401
  149.3 3.6 %collective-permute-start.26 = (bf16[8,16,128]{2,1,0:T(8,128)(2,1)}, bf16[8,16,128]{2,1,0:T(8,128)(2,1)S(1)}, u32[]{:S(2)}, u32[]{:S(2)}) collective-permute-start(bf16[8,16,128]{2,1,0:T(8,128)(2,1)} %get-tuple-element.72), channel_id=1, source_target_pairs={{0,7},{1,0},{2,1},{3,2},{4,3},{5,4},{6,5},{7,6},{8,15},{9,8},{10,9... | collective-permute-start | bytes 98312 | tf_op jit(solution)/shard_map/near_exchange/ppermute | solution.py:401
  152.9 0.8 copy-start.2

commit v3 on v2

--- a/solution.py
+++ b/solution.py
@@ -27,26 +27,21 @@
 
 
 def start_kernel(
-    rows, cols, me_ref, visible_in, excitation_in, precond_in,
-    forward_out, back_out, wanted_ref, currents_ref, copies_ref,
-    count_ref, code_ref, visible_ref, excitation_ref, precond_ref, forward_ref, back_ref, sems,
+    rows, cols, visible_in, excitation_in, precond_in,
+    slot_out, wanted_ref, currents_ref, copies_out,
+    count_ref, code_ref, visible_ref, excitation_ref, precond_ref, slot_ref, rounded_ref, tag_ref, sems,
 ):
     fetches = [
         pltpu.make_async_copy(visible_in, visible_ref, sems.at[0]),
         pltpu.make_async_copy(excitation_in, excitation_ref, sems.at[1]),
         pltpu.make_async_copy(precond_in, precond_ref, sems.at[2]),
     ]
-    stores = [
-        pltpu.make_async_copy(forward_ref, forward_out, sems.at[3]),
-        pltpu.make_async_copy(back_ref, back_out, sems.at[4]),
-    ]
     for fetch in fetches:
         fetch.start()
     slots, tiles = visible_ref.shape
     half, lanes = excitation_ref.shape[1:]
-    size = copies_ref.shape[2]
-    seg, exc = lanes // size, 2 * half
-    me = me_ref[0]
+    exc, size = tag_ref.shape[1:]
+    seg = lanes // size
     none = rows * cols
     base = 2 * seg
 
@@ -56,75 +51,77 @@
         return 0
 
     lax.fori_loop(0, none + 1, clear, 0, unroll=8)
+    for fetch in fetches[1:]:
+        fetch.wait()
+    for b in range(seg):
+        at = slice(b * size, (b + 1) * size)
+        parts = []
+        for q in range(2):
+            new = precond_ref[:, at] * excitation_ref[q, :, at]
+            currents_ref[q, :, at] = new
+            parts.append(new)
+        rounded_ref[b * exc : (b + 1) * exc] = jnp.concatenate(parts, axis=0).astype(jnp.bfloat16)
+    stores = [
+        pltpu.make_async_copy(rounded_ref, copies_out.at[r, : seg * exc], sems.at[5 + r])
+        for r in range(rows)
+    ]
+    for store in stores:
+        store.start()
     fetches[0].wait()
 
     def tile(t, _):
         for v in range(slots):
             block = visible_ref[v, t]
-            entry = t * slots + v
             live = block >= 0
             owner = jnp.where(live, lax.shift_right_arithmetic(block, log2(seg)), none)
             turn = count_ref[owner]
             count_ref[owner] = turn + live.astype(jnp.int32)
             row = lax.shift_right_arithmetic(owner, log2(cols))
             col = owner & (cols - 1)
-            place = row * TURNS + turn
-            forward_ref[entry] = jnp.where(live, col * (rows * TURNS + 1) + place, -1)
-            back_ref[entry] = jnp.where(live, owner * TURNS + turn, -1)
-            line = jnp.where(live, (col - me) & (cols - 1), cols)
+            slot_ref[t * slots + v] = jnp.where(live, owner * TURNS + turn, -1)
             mine = block & (seg - 1)
-            wanted_ref[line, jnp.where(live, place, 0)] = mine
+            wanted_ref[jnp.where(live, col, cols), row * TURNS + turn] = mine
             code_ref[owner] = code_ref[owner] + jnp.where(turn == 0, base, 1) * (mine - seg)
         return 0
 
     lax.fori_loop(0, tiles, tile, 0)
-
-    def find(i, free):
-        return jnp.where(count_ref[i] < TURNS, i * TURNS + TURNS - 1, free)
-
-    back_ref[tiles * slots] = lax.fori_loop(0, none, find, 0, unroll=8)
-    for store in stores:
-        store.start()
-    for fetch in fetches[1:]:
-        fetch.wait()
-    parts = []
-    for b in range(seg):
-        at = slice(b * size, (b + 1) * size)
-        for q in range(2):
-            new = precond_ref[:, at] * excitation_ref[q, :, at]
-            currents_ref[q, :, at] = new
-            parts.append(new)
-    rounded = jnp.concatenate(parts, axis=0).astype(jnp.bfloat16)
     line = lax.broadcasted_iota(jnp.int32, (exc, size), 0)
 
     def fill(r, _):
         tag = jnp.zeros((exc, size), jnp.float32)
         for c in range(cols):
             tag = jnp.where(line == c, code_ref[r * cols + c].astype(jnp.float32), tag)
-        copies_ref[r, : seg * exc] = rounded
-        copies_ref[r, seg * exc :] = tag.astype(jnp.bfloat16)
+        tag_ref[r] = tag.astype(jnp.bfloat16)
         return 0
 
     lax.fori_loop(0, rows, fill, 0)
+    stores.append(pltpu.make_async_copy(tag_ref, copies_out.at[:, seg * exc :], sems.at[3]))
+    stores[-1].start()
+
+    def find(i, free):
+        return jnp.where(count_ref[i] < TURNS, i * TURNS + TURNS - 1, free)
+
+    slot_ref[tiles * slots] = lax.fori_loop(0, none, find, 0, unroll=8)
+    stores.append(pltpu.make_async_copy(slot_ref, slot_out, sems.at[4]))
+    stores[-1].start()
     for store in stores:
         store.wait()
 
 
-def start(me, visible, excitation, precond, rows, cols, size):
+def start(visible, excitation, precond, rows, cols, size):
     count = visible.size
     exc = 2 * excitation.shape[1]
     lines = excitation.shape[2] // size * exc
     return pl.pallas_call(
         functools.partial(start_kernel, rows, cols),
         out_shape=(
-            jax.ShapeDtypeStruct((count,), jnp.int32),
             jax.ShapeDtypeStruct((count + 1,), jnp.int32),
             jax.ShapeDtypeStruct((cols + 1, 128), jnp.int32),
             jax.ShapeDtypeStruct(excitation.shape, jnp.float32),
             jax.ShapeDtypeStruct((rows, lines + exc, size), jnp.bfloat16),
         ),
-        in_specs=[SMEM, HBM, HBM, HBM],
-        out_specs=(HBM, HBM, SMEM, VMEM, VMEM),
+        in_specs=[HBM, HBM, HBM],
+        out_specs=(HBM, SMEM, VMEM, HBM),
         compiler_params=params(64),
         scratch_shapes=[
             pltpu.SMEM((rows * cols + 1,), jnp.int32),
@@ -132,12 +129,13 @@
             pltpu.SMEM(visible.shape[::-1], jnp.int32),
             pltpu.VMEM(excitation.shape, jnp.float32),
             pltpu.VMEM((1, precond.size), jnp.float32),
-            pltpu.SMEM((count,), jnp.int32),
             pltpu.SMEM((count + 1,), jnp.int32),
-            pltpu.SemaphoreType.DMA((5,)),
+            pltpu.VMEM((lines, size), jnp.bfloat16),
+            pltpu.VMEM((rows, exc, size), jnp.bfloat16),
+            pltpu.SemaphoreType.DMA((5 + rows,)),
         ],
         name="start",
-    )(me, visible.T, excitation, precond[None, :])
+    )(visible.T, excitation, precond[None, :])
 
 
 def pack_kernel(me_ref, wanted_ref, group_ref, out_ref):
@@ -152,7 +150,8 @@
         out_ref[p, slots] = tag.astype(jnp.bfloat16)
 
     def peer(p, _):
-        line = ((me - p) & (cols - 1)) * 128
+        back = (lax.shift_right_arithmetic(me, 1) - lax.shift_right_arithmetic(p, 1)) & (cols // 2 - 1)
+        line = ((back * 2 + ((p ^ me) & 1)) * cols + me) * 128
         for s in range(slots):
             block = wanted_ref[line + s] & (seg - 1)
             out_ref[p, s] = group_ref[s // TURNS, pl.ds(pl.multiple_of(block * exc, exc), exc), :]
@@ -239,19 +238,31 @@
 
 
 def optics_kernel(
-    forward_ref, back_ref, x_ref, reflect_ref, coupling_ref, facet_ref, out_ref, weights_ref, sems
+    rows, cols, by_column, slot_ref, reflect_ref, x_in, coupling_ref, facet_ref, out_ref,
+    x_ref, weights_ref, sems,
 ):
     tiles, slots, _, facets, size = coupling_ref.shape
     exc = x_ref.shape[1]
     half = exc // 2
     group = 4
-    free = back_ref[back_ref.shape[0] - 1]
+    free = slot_ref[tiles * slots]
+    whole = pltpu.make_async_copy(x_in, x_ref, sems.at[tiles])
+    whole.start()
+
+    def place(slot):
+        slot = jnp.maximum(slot, 0)
+        if not by_column:
+            return slot
+        col = lax.shift_right_arithmetic(slot, log2(TURNS)) & (cols - 1)
+        row = lax.shift_right_arithmetic(slot, log2(TURNS * cols))
+        return col * (rows * TURNS + 1) + row * TURNS + (slot & (TURNS - 1))
 
     def fetch(t):
         return pltpu.make_async_copy(coupling_ref.at[t], weights_ref.at[t], sems.at[t])
 
     for t in range(tiles):
         fetch(t).start()
+    whole.wait()
 
     def weights(t, v):
         pair = [weights_ref[t, u].reshape(2 * facets, size) for u in (v, v + 1)]
@@ -267,10 +278,9 @@
             for v in range(0, slots, 2):
                 parts = []
                 for u in (v, v + 1):
-                    slot = forward_ref[t * slots + u]
-                    live = slot >= 0
-                    x = x_ref[jnp.where(live, slot, 0)]
-                    parts.append(jnp.where(live, x, jnp.zeros_like(x)))
+                    slot = slot_ref[t * slots + u]
+                    x = x_ref[place(slot)]
+                    parts.append(jnp.where(slot >= 0, x, jnp.zeros_like(x)))
                 product = dot_t(jnp.concatenate(parts, axis=1), weights(t, v))
                 total = product if total is None else total + product
             by_re, by_im = total[:, :facets], total[:, facets:]
@@ -293,7 +303,7 @@
                 sums = jnp.dot(rounded[i], weights(t, v), preferred_element_type=jnp.float32)
                 sums = sums.astype(jnp.bfloat16)
                 for u in range(2):
-                    slot = back_ref[t * slots + v + u]
+                    slot = slot_ref[t * slots + v + u]
                     slot = jnp.where(slot >= 0, slot, free)
                     out_ref[slot] = sums[:, u * size : (u + 1) * size]
         return 0
@@ -301,32 +311,33 @@
     lax.fori_loop(0, tiles // group, some, 0)
 
 
-def optics(forward, back, coupling, x, reflect, devices):
-    tiles, slots, _, facets, size = coupling.shape
+def optics(slots, coupling, x, reflect, rows, cols, by_column):
+    tiles, _, _, facets, size = coupling.shape
     exc = x.shape[1]
     return pl.pallas_call(
-        optics_kernel,
+        functools.partial(optics_kernel, rows, cols, by_column),
         out_shape=(
             jax.ShapeDtypeStruct((2, exc // 2, tiles * facets), jnp.float32),
-            jax.ShapeDtypeStruct((devices * TURNS, exc, size), jnp.bfloat16),
+            jax.ShapeDtypeStruct((rows * cols * TURNS, exc, size), jnp.bfloat16),
         ),
-        in_specs=[SMEM, SMEM, VMEM, VMEM, pl.BlockSpec(memory_space=pl.ANY)],
+        in_specs=[SMEM, VMEM] + [pl.BlockSpec(memory_space=pl.ANY)] * 2,
         out_specs=(VMEM, VMEM),
         scratch_shapes=[
+            pltpu.VMEM(x.shape, jnp.bfloat16),
             pltpu.VMEM(coupling.shape, jnp.bfloat16),
-            pltpu.SemaphoreType.DMA((tiles,)),
+            pltpu.SemaphoreType.DMA((tiles + 1,)),
         ],
         compiler_params=params(57),
         cost_estimate=pl.CostEstimate(
             flops=4 * exc * coupling.size, bytes_accessed=2 * coupling.size, transcendentals=0
         ),
         name="optics",
-    )(forward, back, x, reflect, coupling)
-
-
-def update_kernel(cols, tag_ref, back_ref, currents_ref, excitation_ref, precond_ref, *rest):
+    )(slots, reflect, x, coupling)
+
+
+def update_kernel(cols, last, tag_ref, back_ref, currents_ref, excitation_ref, precond_ref, *rest):
     near_refs, rest = rest[:cols], rest[cols:]
-    out_ref, (total_ref, own_ref, sem) = rest[0], rest[-3:]
+    out_ref, (total_ref, *more_refs, own_ref, sem) = rest[0], rest[-6:]
     own = pltpu.make_async_copy(near_refs[0], own_ref, sem)
     own.start()
     count, exc, size = back_ref.shape
@@ -337,6 +348,8 @@
     for near_ref in near_refs[2:]:
         total += near_ref[...].astype(jnp.float32)
     total_ref[:seg] = total
+    for more_ref in more_refs:
+        more_ref[...] = jnp.zeros_like(more_ref)
 
     def seen(r):
         for c in range(cols):
@@ -346,8 +359,9 @@
             yield slot + 1, tag & (2 * seg - 1)
 
     def add(r, _):
-        for slot, block in seen(r):
-            total_ref[block] = total_ref[block] + back_ref[slot].astype(jnp.float32)
+        for i, (slot, block) in enumerate(seen(r)):
+            sum_ref = (total_ref, *more_refs)[i % (1 + len(more_refs))]
+            sum_ref[block] = sum_ref[block] + back_ref[slot].astype(jnp.float32)
         return 0
 
     lax.fori_loop(0, rows, add, 0)
@@ -358,11 +372,13 @@
         for q in range(2):
             some = slice(q * half, (q + 1) * half)
             part = total_ref[b, some] + own_ref[b, some]
+            for more_ref in more_refs:
+                part += more_ref[b, some]
             new = currents_ref[q, :, lanes] + scale * (excitation_ref[q, :, lanes] - part)
             out_ref[q, :, lanes] = new
-            if len(rest) > 4:
+            if not last:
                 total_ref[b, some] = new
-    if len(rest) > 4:
+    if not last:
         rounded_ref, sent_ref = rest[1:3]
         for b in range(seg):
             rounded_ref[b * exc : (b + 1) * exc] = total_ref[b].astype(jnp.bfloat16)
@@ -383,12 +399,12 @@
         out_shape.append(jax.ShapeDtypeStruct((seg * exc, size), jnp.bfloat16))
         out_shape.append(jax.ShapeDtypeStruct(back.shape, jnp.bfloat16))
     return pl.pallas_call(
-        functools.partial(update_kernel, len(near)),
+        functools.partial(update_kernel, len(near), last),
         out_shape=out_shape,
         in_specs=[SMEM] + [VMEM] * 4 + [HBM] + [VMEM] * (len(near) - 1),
         out_specs=[VMEM] * len(out_shape),
         scratch_shapes=[
-            pltpu.VMEM((seg + 1, exc, size), jnp.float32),
+            *[pltpu.VMEM((seg + 1, exc, size), jnp.float32)] * 4,
             pltpu.VMEM((seg, exc, size), jnp.float32),
             pltpu.SemaphoreType.DMA,
         ],
@@ -424,14 +440,13 @@
     side = 1 << log2(rows) // 2
 
     me = jnp.stack([lax.axis_index("col"), lax.axis_index("row")]).astype(jnp.int32)
-    forward, back, wanted, currents, copies = start(
-        me, visible, excitation, precond, rows, cols, size
-    )
-    lines = [wanted[:1]]
-    for k in range(1, cols):
-        with jax.named_scope("wanted_exchange"):
-            lines.append(along(wanted[k : k + 1], k, cols))
-    wanted = jnp.concatenate(lines).reshape(-1)
+    slots, wanted, currents, copies = start(visible, excitation, precond, rows, cols, size)
+    with jax.named_scope("wanted_exchange"):
+        wanted = wanted[:cols]
+        other = lax.ppermute(wanted, "col", [(i, i ^ 1) for i in range(cols)])
+        pair = jnp.stack([wanted, other])
+        wanted = jnp.stack([pair] + [along(pair, 2 * k, cols) for k in range(1, cols // 2)])
+    wanted = wanted.reshape(-1)
     index = near_index[0].T
     rounded = sent = tags = None
     for iteration in range(ITERS):
@@ -451,8 +466,7 @@
                 line = [along_square(rounded, 0, k, side) for k in range(1, side)]
                 x, line = lax.optimization_barrier((x, jnp.stack([rounded] + line)))
                 groups = [line] + [along_square(line, k, 0, side) for k in range(1, side)]
-            forward = back
-        facets, sums = optics(forward, back, coupling, x, reflect, devices)
+        facets, sums = optics(slots, coupling, x, reflect, rows, cols, iteration == 0)
         sums, groups = lax.optimization_barrier((sums, groups))
         near = near_sums(me, index, near_blocks[0], groups, seg, exc)
         with jax.named_scope("near_exchange"):

time: 157 us -> 153 us (0.975)
  starting transfers between devices: 60.6 us -> 56.7 us
  Pallas kernels: 39.6 us -> 37.4 us
  waiting for transfers between devices: 29.7 us -> 31.6 us
    ppermute x21 -> x17, starting transfers between devices: 26.6 us -> 22.7 us  [along(): return lax.ppermute(x, 'col', [(i, (i + k) % cols) for i in range(cols)])]
    pallas_call x4, Pallas kernels: 21.3 us -> 19.2 us  [the longest x2 14.9 us: optics(): pl.pallas_call(functools.partial(optics_kernel, rows, cols, by_column), o...]
    ppermute x21 -> x17, waiting for transfers between devices: 14.3 us -> 13.8 us  [along(): return lax.ppermute(x, 'col', [(i, (i + k) % cols) for i in range(cols)])]
  transfers between devices with their start and end apart: 31 -> 28, of which waited for: 12 -> 14; matrix products, arithmetic and copies ran while one was open for 1% -> 1% of each run, Pallas kernels for 13% -> 13%
where the time goes in v3:
time: 153 us
  starting transfers between devices  56.7 us (37%)
  Pallas kernels  37.4 us (24%)
  waiting for transfers between devices  31.6 us (21%)
  blocking collectives  23 us (15%)
  local copies, waits for them, and re-layouts  1.81 us (1%)
    all_to_all x1, blocking collectives, shards(): x = lax.all_to_all(packed, 'col', 0, 0, tiled=True)  23 us
    ppermute x17, starting transfers between devices, along(): return lax.ppermute(x, 'col', [(i, (i + k) % cols) for i in range(cols)])  22.7 us
    all_to_all x3, starting transfers between devices, all_devices(): lax.all_to_all(sent, ('row', 'col'), 0, 0, tiled=True).reshape(x.shape)  19.5 us
    pallas_call x2, Pallas kernels, optics(): pl.pallas_call(functools.partial(optics_kernel, rows, cols, by_column), o...  14.9 us
    ppermute x17, waiting for transfers between devices, along(): return lax.ppermute(x, 'col', [(i, (i + k) % cols) for i in range(cols)])  13.8 us
    pallas_call x2, Pallas kernels, near_sums(): pl.pallas_call(functools.partial(near_kernel, count), out_shape=[jax.Shap...  12.4 us
    ppermute x6, waiting for transfers between devices, along_square(): return lax.ppermute(a, 'row', pairs)  11.1 us
    all_to_all x1, starting transfers between devices, shards(): groups = [lax.all_to_all(copies, 'row', 0, 0, tiled=True)]  7.6 us
  transfers between devices with their start and end apart: 28, of which 14 were waited for; matrix products, arithmetic and copies ran while one was open for 1% of the time, Pallas kernels for 13%

profile of v3, /device:TPU:1, one launch (start us, length us, event | category | flops | bytes accessed | tf_op | source)
XLA Modules:
  0.0 152.6 jit_solution(791508978840186233)
XLA Ops:
  0.6 4.2 %start.1 = (s32[129]{0:T(256)}, s32[9,128]{1,0:T(8,128)}, f32[2,8,1024]{2,1,0:T(8,128)}, bf16[16,144,128]{2,1,0:T(8,128)(2,1)}) custom-call(s32[8,16]{1,0:T(8,128)} %bitcast.49, f32[2,8,1024]{2,1,0:T(8,128)} %excitation_ref.3, f32[1,1024]{1,0:T(1,128)} %bitcast.31), custom_call_target="tpu_custom_call" | custom-call | tf_op jit(solution)/shard_map/start/pallas_call | solution.py:115
  4.8 0.0 copy-start.12
  4.8 7.6 %all-to-all-start = ((bf16[16,144,128]{2,1,0:T(8,128)(2,1)}), bf16[16,144,128]{2,1,0:T(8,128)(2,1)S(1)}, u32[]{:S(2)}, u32[]{:S(2)}) async-start(bf16[16,144,128]{2,1,0:T(8,128)(2,1)} %get-tuple-element.38), calls=%async_computation | async-start | bytes 1179648 | tf_op jit(solution)/shard_map/row_exchange/all_to_all | solution.py:456
  12.4 1.0 collective-permute-start
  13.5 0.8 collective-permute-done
  14.3 3.6 %collective-permute-start.2 = (s32[2,8,128]{2,1,0:T(8,128)S(1)}, s32[2,8,128]{2,1,0:T(8,128)S(1)}, u32[]{:S(2)}, u32[]{:S(2)}) collective-permute-start(s32[2,8,128]{2,1,0:T(8,128)S(1)} %get-tuple-element.73), channel_id=1, source_target_pairs={{0,4},{1,5},{2,6},{3,7},{4,0},{5,1},{6,2},{7,3},{8,12},{9,13},{10,... | collective-permute-start | bytes 24584 | tf_op jit(solution)/shard_map/wanted_exchange/ppermute | solution.py:417
  17.9 0.7 collective-permute-start.1
  18.6 1.9 %collective-permute-start.3 = (s32[2,8,128]{2,1,0:T(8,128)S(1)}, s32[2,8,128]{2,1,0:T(8,128)S(1)}, u32[]{:S(2)}, u32[]{:S(2)}) collective-permute-start(s32[2,8,128]{2,1,0:T(8,128)S(1)} %get-tuple-element.73), channel_id=1, source_target_pairs={{0,6},{1,7},{2,0},{3,1},{4,2},{5,3},{6,4},{7,5},{8,14},{9,15},{10,... | collective-permute-start | bytes 24584 | tf_op jit(solution)/shard_map/wanted_exchange/ppermute | solution.py:417
  20.6 0.1 pad_add_fusion.2.me_ref
  20.7 1.2 collective-permute-done.1
  21.9 0.0 collective-permute-done.3
  21.9 1.5 all-to-all-done.group_ref.rest_0_
  23.4 1.6 %pack.1 = bf16[8,33,16,128]{3,2,1,0:T(8,128)(2,1)S(1)} custom-call(s32[2]{0:T(128)S(1)} %pad_add_fusion.2.me_ref, s32[8192]{0:T(1024)S(1)} %bitcast.30, bf16[16,144,128]{2,1,0:T(8,128)(2,1)S(1)} %all-to-all-done.group_ref.rest_0_), custom_call_target="tpu_custom_call" | custom-call | tf_op jit(solution)/shard_map/pack/pallas_call | solution.py:165
  25.1 23.0 %all_to_all.25 = bf16[8,33,16,128]{3,2,1,0:T(8,128)(2,1)} all-to-all(bf16[8,33,16,128]{3,2,1,0:T(8,128)(2,1)S(1)} %pack.1), channel_id=1, replica_groups=mesh['row'=16,'col'=8] {'col'}, dimensions={0} | all-to-all | bytes 2162688 | tf_op jit(solution)/shard_map/col_exchange/all_to_all | solution.py:459
  48.0 7.4 %optics.2 = (f32[2,8,2048]{2,1,0:T(8,128)}, bf16[256,16,128]{2,1,0:T(8,128)(2,1)}) custom-call(s32[129]{0:T(256)} %get-tuple-element.39.slot_ref, f32[2,2048]{1,0:T(2,128)} %reflect_ref.3, bf16[264,16,128]{2,1,0:T(8,128)(2,1)} %bitcast.37, bf16[16,8,2,128,128]{4,3,2,1,0:T(8,128)(2,1)} %coupling_ref.3), custom_call_target="tpu_custom_call" | custom-call | flops 268435456 | bytes 8388608 | tf_op jit(solution)/shard_map/optics/pallas_call | solution.py:317
  55.5 5.2 %all-to-all-start.2 = ((bf16[128,32,128]{2,1,0:T(8,128)(2,1)}), bf16[128,32,128]{2,1,0:T(8,128)(2,1)S(1)}, u32[]{:S(2)}, u32[]{:S(2)}) async-start(bf16[128,32,128]{2,1,0:T(8,128)(2,1)} %bitcast.40), calls=%async_computation.2 | async-start | bytes 2097152 | tf_op jit(solution)/shard_map/back_exchange/all_to_all | solution.py:431
  60.7 0.0 copy-start.1
  60.7 0.0 copy-start.3
  60.7 0.0 copy-start.5
  60.7 6.2 %near.2 = (f32[8,16,128]{2,1,0:T(8,128)}, bf16[8,16,128]{2,1,0:T(8,128)(2,1)}, bf16[8,16,128]{2,1,0:T(8,128)(2,1)}, bf16[8,16,128]{2,1,0:T(8,128)(2,1)}, bf16[8,...) custom-call(s32[2]{0:T(128)} %copy-done.6, ...), custom_call_target="tpu_custom_call" | custom-call | flops 134217728 | bytes 8388608 | tf_op jit(solution)/shard_map/near/pallas_call | solution.py:219
  66.9 1.8 %collective-permute-start.4 = (bf16[8,16,128]{2,1,0:T(8,128)(2,1)}, bf16[8,16,128]{2,1,0:T(8,128)(2,1)S(1)}, u32[]{:S(2)}, u32[]{:S(2)}) collective-permute-start(bf16[8,16,128]{2,1,0:T(8,128)(2,1)} %get-tuple-element.45), channel_id=1, source_target_pairs={{0,1},{1,2},{2,3},{3,4},{4,5},{5,6},{6,7},{7,0},{8,9},{9,10},{10,1... | collective-permute-start | bytes 98312 | tf_op jit(solution)/shard_map/near_exchange/ppermute | solution.py:417
  68.7 1.5 collective-permute-start.5
  70.1 1.9 %collective-permute-start.6 = (bf16[8,16,128]{2,1,0:T(8,128)(2,1)}, bf16[8,16,128]{2,1,0:T(8,128)(2,1)S(1)}, u32[]{:S(2)}, u32[]{:S(2)}) collective-permute-start(bf16[8,16,128]{2,1,0:T(8,128)(2,1)} %get-tuple-element.47), channel_id=1, source_target_pairs={{0,3},{1,4},{2,5},{3,6},{4,7},{5,0},{6,1},{7,2},{8,11},{9,12},{10,... | collective-permute-start | bytes 98312 | tf_op jit(solution)/shard_map/near_exchange/ppermute | solution.py:417
  72.1 0.0 collective-permute-start.7
  72.1 2.3 %collective-permute-start.8 = (bf16[8,16,128]{2,1,0:T(8,128)(2,1)}, bf16[8,16,128]{2,1,0:T(8,128)(2,1)S(1)}, u32[]{:S(2)}, u32[]{:S(2)}) collective-permute-start(bf16[8,16,128]{2,1,0:T(8,128)(2,1)} %get-tuple-element.49), channel_id=1, source_target_pairs={{0,5},{1,6},{2,7},{3,0},{4,1},{5,2},{6,3},{7,4},{8,13},{9,14},{10,... | collective-permute-start | bytes 98312 | tf_op jit(solution)/shard_map/near_exchange/ppermute | solution.py:417
  74.4 0.0 collective-permute-done.4.rest_1_
  74.4 0.7 collective-permute-start.9
  75.1 3.1 %collective-permute-done.5.rest_2_ = bf16[8,16,128]{2,1,0:T(8,128)(2,1)S(1)} collective-permute-done((bf16[8,16,128]{2,1,0:T(8,128)(2,1)}, bf16[8,16,128]{2,1,0:T(8,128)(2,1)S(1)}, u32[]{:S(2)}, u32[]{:S(2)}) %collective-permute-start.5) | collective-permute-done | bytes 32800 | tf_op jit(solution)/shard_map/near_exchange/ppermute | solution.py:417
  78.2 0.0 collective-permute-start.10
  78.2 1.0 convert_reduce_fusion
  79.2 0.1 reshape.40.tag_ref
  79.3 0.0 collective-permute-done.6.rest_3_
  79.3 0.4 collective-permute-done.7.rest_4_
  79.6 0.6 collective-permute-done.8.rest_5_
  80.3 1.5 collective-permute-done.10.rest_7_
  81.8 0.0 copy-start.4
  81.8 0.8 copy-done.4
  82.6 2.6 %update.2 = (f32[2,8,1024]{2,1,0:T(8,128)S(1)}, bf16[128,128]{1,0:T(8,128)(2,1)S(1)}, bf16[256,16,128]{2,1,0:T(8,128)(2,1)}) custom-call(s32[128]{0:T(128)S(1)} %reshape.40.tag_ref, bf16[256,16,128]{2,1,0:T(8,128)(2,1)S(1)} %bitcast.28, f32[2,8,1024]{2,1,0:T(8,128)S(1)} %copy-done.3, f32[2,8,1024]{2,1,0:T(8,128)S(1)} %copy-done.1, f32[1,1024]{1,0:T(1,128)S(1)} %bitcast.32, ...), custom_call_target="tpu_custom_call" | custom-call | tf_op jit(solution)/shard_map/update/pallas_call | solution.py:401
  85.2 6.9 %all-to-all-start.3 = ((bf16[128,32,128]{2,1,0:T(8,128)(2,1)}), bf16[128,32,128]{2,1,0:T(8,128)(2,1)S(1)}, u32[]{:S(2)}, u32[]{:S(2)}) async-start(bf16[128,32,128]{2,1,0:T(8,128)(2,1)} %bitcast.17), calls=%async_computation.3 | async-start | bytes 2097152 | tf_op jit(solution)/shard_map/forward_exchange/all_to_all | solution.py:431
  92.2 2.7 %collective-permute-start.13 = (bf16[128,128]{1,0:T(8,128)(2,1)S(1)}, bf16[128,128]{1,0:T(8,128)(2,1)S(1)}, u32[]{:S(2)}, u32[]{:S(2)}) collective-permute-start(bf16[128,128]{1,0:T(8,128)(2,1)S(1)} %get-tuple-element.53), channel_id=1, source_target_pairs={{0,24},{8,0},{16,8},{24,16},{32,56},{40,32},{48,40},{56,48},{64,88... | collective-permute-start | bytes 98312 | tf_op jit(solution)/shard_map/row_gather/ppermute | solution.py:425
  94.9 0.5 collective-permute-start.12
  95.4 0.6 collective-permute-start.11
  96.0 3.0 %collective-permute-done.13 = bf16[128,128]{1,0:T(8,128)(2,1)S(1)} collective-permute-done((bf16[128,128]{1,0:T(8,128)(2,1)S(1)}, bf16[128,128]{1,0:T(8,128)(2,1)S(1)}, u32[]{:S(2)}, u32[]{:S(2)}) %collective-permute-start.13) | collective-permute-done | bytes 32800 | tf_op jit(solution)/shard_map/row_gather/ppermute | solution.py:425
  99.0 4.9 %collective-permute-done.12 = bf16[128,128]{1,0:T(8,128)(2,1)S(1)} collective-permute-done((bf16[128,128]{1,0:T(8,128)(2,1)S(1)}, bf16[128,128]{1,0:T(8,128)(2,1)S(1)}, u32[]{:S(2)}, u32[]{:S(2)}) %collective-permute-start.12) | collective-permute-done | bytes 32800 | tf_op jit(solution)/shard_map/row_gather/ppermute | solution.py:425
  103.9 3.2 %collective-permute-done.11 = bf16[128,128]{1,0:T(8,128)(2,1)S(1)} collective-permute-done((bf16[128,128]{1,0:T(8,128)(2,1)S(1)}, bf16[128,128]{1,0:T(8,128)(2,1)S(1)}, u32[]{:S(2)}, u32[]{:S(2)}) %collective-permute-start.11) | collective-permute-done | bytes 32800 | tf_op jit(solution)/shard_map/row_gather/ppermute | solution.py:425
  107.1 4.4 %all-to-all-done.3 = bf16[128,32,128]{2,1,0:T(8,128)(2,1)S(1)} async-done(((bf16[128,32,128]{2,1,0:T(8,128)(2,1)}), bf16[128,32,128]{2,1,0:T(8,128)(2,1)S(1)}, u32[]{:S(2)}, u32[]{:S(2)}) %all-to-all-start.3) | async-done | bytes 1048608 | tf_op jit(solution)/shard_map/forward_exchange/all_to_all | solution.py:431
  111.5 0.9 collective-permute-start.16
  112.3 1.2 collective-permute-start.15
  113.6 7.4 %optics.3 = (f32[2,8,2048]{2,1,0:T(8,128)}, bf16[256,16,128]{2,1,0:T(8,128)(2,1)}) custom-call(s32[129]{0:T(256)} %get-tuple-element.39.slot_ref, f32[2,2048]{1,0:T(2,128)} %reflect_ref.3, bf16[256,16,128]{2,1,0:T(8,128)(2,1)} %bitcast.38, bf16[16,8,2,128,128]{4,3,2,1,0:T(8,128)(2,1)} %coupling_ref.3), custom_call_target="tpu_custom_call" | custom-call | flops 268435456 | bytes 8388608 | tf_op jit(solution)/shard_map/optics/pallas_call | solution.py:317
  121.1 0.0 collective-permute-done.15.rest_2_
  121.1 0.0 collective-permute-done.14.rest_1_
  121.1 7.3 %all-to-all-start.4 = ((bf16[128,32,128]{2,1,0:T(8,128)(2,1)}), bf16[128,32,128]{2,1,0:T(8,128)(2,1)S(1)}, u32[]{:S(2)}, u32[]{:S(2)}) async-start(bf16[128,32,128]{2,1,0:T(8,128)(2,1)} %bitcast.39), calls=%async_computation.4 | async-start | bytes 2097152 | tf_op jit(solution)/shard_map/back_exchange/all_to_all | solution.py:431
  128.5 6.2 %near.3 = (f32[8,16,128]{2,1,0:T(8,128)}, bf16[8,16,128]{2,1,0:T(8,128)(2,1)}, bf16[8,16,128]{2,1,0:T(8,128)(2,1)}, bf16[8,16,128]{2,1,0:T(8,128)(2,1)}, bf16[8,...) custom-call(s32[2]{0:T(128)} %copy-done.6, ...), custom_call_target="tpu_custom_call" | custom-call | flops 134217728 | bytes 8388608 | tf_op jit(solution)/shard_map/near/pallas_call | solution.py:219
  134.7 1.8 %collective-permute-start.17 = (bf16[8,16,128]{2,1,0:T(8,128)(2,1)}, bf16[8,16,128]{2,1,0:T(8,128)(2,1)S(1)}, u32[]{:S(2)}, u32[]{:S(2)}) collective-permute-start(bf16[8,16,128]{2,1,0:T(8,128)(2,1)} %get-tuple-element.64), channel_id=1, source_target_pairs={{0,1},{1,2},{2,3},{3,4},{4,5},{5,6},{6,7},{7,0},{8,9},{9,10},{10,1... | collective-permute-start | bytes 98312 | tf_op jit(solution)/shard_map/near_exchange/ppermute | solution.py:417
  136.4 1.5 collective-permute-start.18
  137.9 1.9 %collective-permute-start.19 = (bf16[8,16,128]{2,1,0:T(8,128)(2,1)}, bf16[8,16,128]{2,1,0:T(8,128)(2,1)S(1)}, u32[]{:S(2)}, u32[]{:S(2)}) collective-permute-start(bf16[8,16,128]{2,1,0:T(8,128)(2,1)} %get-tuple-element.66), channel_id=1, source_target_pairs={{0,3},{1,4},{2,5},{3,6},{4,7},{5,0},{6,1},{7,2},{8,11},{9,12},{10,... | collective-permute-start | bytes 98312 | tf_op jit(solution)/shard_map/near_exchange/ppermute | solution.py:417
  139.8 0.1 collective-permute-start.20
  139.9 2.5 %collective-permute-start.21 = (bf16[8,16,128]{2,1,0:T(8,128)(2,1)}, bf16[8,16,128]{2,1,0:T(8,128)(2,1)S(1)}, u32[]{:S(2)}, u32[]{:S(2)}) collective-permute-start(bf16[8,16,128]{2,1,0:T(8,128)(2,1)} %get-tuple-element.68), channel_id=1, source_target_pairs={{0,5},{1,6},{2,7},{3,0},{4,1},{5,2},{6,3},{7,4},{8,13},{9,14},{10,... | collective-permute-start | bytes 98312 | tf_op jit(solution)/shard_map/near_exchange/ppermute | solution.py:417
  142.3 0.6 collective-permute-start.22
  142.9 3.5 %collective-permute-done.18.rest_2_ = bf16[8,16,128]{2,1,0:T(8,128)(2,1)S(1)} collective-permute-done((bf16[8,16,128]{2,1,0:T(8,128)(2,1)}, bf16[8,16,128]{2,1,0:T(8,128)(2,1)S(1)}, u32[]{:S(2)}, u32[]{:S(2)}) %collective-permute-start.18) | collective-permute-done | bytes 32800 | tf_op jit(solution)/shard_map/near_exchange/ppermute | solution.py:417
  146.3 1.9 %collective-permute-done.19.rest_3_ = bf16[8,16,128]{2,1,0:T(8,128)(2,1)S(1)} collective-permute-done((bf16[8,16,128]{2,1,0:T(8,128)(2,1)}, bf16[8,16,128]{2,1,0:T(8,128)(2,1)S(1)}, u32[]{:S(2)}, u32[]{:S(2)}) %collective-permute-start.19) | collective-permute-done | bytes 32800 | tf_op jit(solution)/shard_map/near_exchange/ppermute | solution.py:417
  148.3 1.6 %collective-permute-done.23.rest_7_ = bf16[8,16,128]{2,1,0:T(8,128)(2,1)S(1)} collective-permute-done((bf16[8,16,128]{2,1,0:T(8,128)(2,1)}, bf16[8,16,128]{2,1,0:T(8,128)(2,1)S(1)}, u32[]{:S(2)}, u32[]{:S(2)}) %collective-permute-start.23) | collective-permute-done | bytes 32800 | tf_op jit(solution)/shard_map/near_exchange/ppermute | solution.py:417
  149.9 0.8 copy-done.2
  150.7 1.7 %update.3 = f32[2,8,1024]{2,1,0:T(8,128)} custom-call(s32[128]{0:T(128)S(1)} %reshape.40.tag_ref, bf16[256,16,128]{2,1,0:T(8,128)(2,1)S(1)} %bitcast.29, f32[2,8,1024]{2,1,0:T(8,128)S(1)} %get-tuple-element.58.currents_ref, f32[2,8,1024]{2,1,0:T(8,128)S(1)} %copy-done.1, f32[1,1024]{1,0:T(1,128)S(1)} %bitcast.33, f32[8,16,128]{2,1,0:T(8,128)S(1)} %copy-done.2, ...), custom_call_target="tpu_custom_call" | custom-call | tf_op jit(solution)/shard_map/update/pallas_call | solution.py:401
  (34 shorter events, 0.1 us)
Async XLA Ops:
  4.8 7.6 %copy-start.12 = (s32[9,128]{1,0:T(8,128)S(1)}, s32[9,128]{1,0:T(8,128)}, u32[]{:S(2)}) copy-start(s32[9,128]{1,0:T(8,128)} %get-tuple-element.37) | copy-start | bytes 13828
  4.8 18.6 %all-to-all-start = ((bf16[16,144,128]{2,1,0:T(8,128)(2,1)}), bf16[16,144,128]{2,1,0:T(8,128)(2,1)S(1)}, u32[]{:S(2)}, u32[]{:S(2)}) async-start(bf16[16,144,128]{2,1,0:T(8,128)(2,1)} %get-tuple-element.38), calls=%async_computation | async-start | bytes 1179648 | tf_op jit(solution)/shard_map/row_exchange/all_to_all | solution.py:456
  12.4 1.9 %collective-permute-start = (s32[8,128]{1,0:T(8,128)S(1)}, s32[8,128]{1,0:T(8,128)S(1)}, u32[]{:S(2)}, u32[]{:S(2)}) collective-permute-start(s32[8,128]{1,0:T(8,128)S(1)} %get-tuple-element.75), channel_id=1, source_target_pairs={{0,1},{1,0},{2,3},{3,2},{4,5},{5,4},{6,7},{7,6},{8,9},{9,8},{10,11... | collective-permute-start | bytes 12296 | tf_op jit(solution)/shard_map/wanted_exchange/ppermute | solution.py:446
  14.3 6.4 %collective-permute-start.2 = (s32[2,8,128]{2,1,0:T(8,128)S(1)}, s32[2,8,128]{2,1,0:T(8,128)S(1)}, u32[]{:S(2)}, u32[]{:S(2)}) collective-permute-start(s32[2,8,128]{2,1,0:T(8,128)S(1)} %get-tuple-element.73), channel_id=1, source_target_pairs={{0,4},{1,5},{2,6},{3,7},{4,0},{5,1},{6,2},{7,3},{8,12},{9,13},{10,... | collective-permute-start | bytes 24584 | tf_op jit(solution)/shard_map/wanted_exchange/ppermute | solution.py:417
  17.9 4.0 %collective-permute-start.1 = (s32[2,8,128]{2,1,0:T(8,128)S(1)}, s32[2,8,128]{2,1,0:T(8,128)S(1)}, u32[]{:S(2)}, u32[]{:S(2)}) collective-permute-start(s32[2,8,128]{2,1,0:T(8,128)S(1)} %get-tuple-element.73), channel_id=1, source_target_pairs={{0,2},{1,3},{2,4},{3,5},{4,6},{5,7},{6,0},{7,1},{8,10},{9,11},{10,... | collective-permute-start | bytes 24584 | tf_op jit(solution)/shard_map/wanted_exchange/ppermute | solution.py:417
  18.6 3.3 %collective-permute-start.3 = (s32[2,8,128]{2,1,0:T(8,128)S(1)}, s32[2,8,128]{2,1,0:T(8,128)S(1)}, u32[]{:S(2)}, u32[]{:S(2)}) collective-permute-start(s32[2,8,128]{2,1,0:T(8,128)S(1)} %get-tuple-element.73), channel_id=1, source_target_pairs={{0,6},{1,7},{2,0},{3,1},{4,2},{5,3},{6,4},{7,5},{8,14},{9,15},{10,... | collective-permute-start | bytes 24584 | tf_op jit(solution)/shard_map/wanted_exchange/ppermute | solution.py:417
  20.6 27.4 %copy-start.6 = (s32[2]{0:T(128)}, s32[2]{0:T(128)S(1)}, u32[]{:S(2)}) copy-start(s32[2]{0:T(128)S(1)} %pad_add_fusion.2.me_ref) | copy-start | bytes 28
  23.4 24.6 %copy-start = (bf16[16,144,128]{2,1,0:T(8,128)(2,1)}, bf16[16,144,128]{2,1,0:T(8,128)(2,1)S(1)}, u32[]{:S(2)}) copy-start(bf16[16,144,128]{2,1,0:T(8,128)(2,1)S(1)} %all-to-all-done.group_ref.rest_0_) | copy-start | bytes 1769476
  55.5 26.3 %all-to-all-start.2 = ((bf16[128,32,128]{2,1,0:T(8,128)(2,1)}), bf16[128,32,128]{2,1,0:T(8,128)(2,1)S(1)}, u32[]{:S(2)}, u32[]{:S(2)}) async-start(bf16[128,32,128]{2,1,0:T(8,128)(2,1)} %bitcast.40), calls=%async_computation.2 | async-start | bytes 2097152 | tf_op jit(solution)/shard_map/back_exchange/all_to_all | solution.py:431
  60.7 21.1 %copy-start.1 = (f32[2,8,1024]{2,1,0:T(8,128)S(1)}, f32[2,8,1024]{2,1,0:T(8,128)}, u32[]{:S(2)}) copy-start(f32[2,8,1024]{2,1,0:T(8,128)} %excitation_ref.3) | copy-start | bytes 196612
  60.7 21.1 %copy-start.3 = (f32[2,8,1024]{2,1,0:T(8,128)S(1)}, f32[2,8,1024]{2,1,0:T(8,128)}, u32[]{:S(2)}) copy-start(f32[2,8,1024]{2,1,0:T(8,128)} %get-tuple-element.42.currents_ref) | copy-start | bytes 196612
  60.7 21.1 %copy-start.5 = (f32[1024]{0:T(1024)S(1)}, f32[1024]{0:T(1024)}, u32[]{:S(2)}) copy-start(f32[1024]{0:T(1024)} %param.8) | copy-start | bytes 12292
  66.9 7.5 %collective-permute-start.4 = (bf16[8,16,128]{2,1,0:T(8,128)(2,1)}, bf16[8,16,128]{2,1,0:T(8,128)(2,1)S(1)}, u32[]{:S(2)}, u32[]{:S(2)}) collective-permute-start(bf16[8,16,128]{2,1,0:T(8,128)(2,1)} %get-tuple-element.45), channel_id=1, source_target_pairs={{0,1},{1,2},{2,3},{3,4},{4,5},{5,6},{6,7},{7,0},{8,9},{9,10},{10,1... | collective-permute-start | bytes 98312 | tf_op jit(solution)/shard_map/near_exchange/ppermute | solution.py:417
  68.7 9.5 %collective-permute-start.5 = (bf16[8,16,128]{2,1,0:T(8,128)(2,1)}, bf16[8,16,128]{2,1,0:T(8,128)(2,1)S(1)}, u32[]{:S(2)}, u32[]{:S(2)}) collective-permute-start(bf16[8,16,128]{2,1,0:T(8,128)(2,1)} %get-tuple-element.46), channel_id=1, source_target_pairs={{0,2},{1,3},{2,4},{3,5},{4,6},{5,7},{6,0},{7,1},{8,10},{9,11},{10,... | collective-permute-start | bytes 98312 | tf_op jit(solution)/shard_map/near_exchange/ppermute | solution.py:417
  70.1 9.1 %collective-permute-start.6 = (bf16[8,16,128]{2,1,0:T(8,128)(2,1)}, bf16[8,16,128]{2,1,0:T(8,128)(2,1)S(1)}, u32[]{:S(2)}, u32[]{:S(2)}) collective-permute-start(bf16[8,16,128]{2,1,0:T(8,128)(2,1)} %get-tuple-element.47), channel_id=1, source_target_pairs={{0,3},{1,4},{2,5},{3,6},{4,7},{5,0},{6,1},{7,2},{8,11},{9,12},{10,... | collective-permute-start | bytes 98312 | tf_op jit(solution)/shard_map/near_exchange/ppermute | solution.py:417
  72.1 7.6 %collective-permute-start.7 = (bf16[8,16,128]{2,1,0:T(8,128)(2,1)}, bf16[8,16,128]{2,1,0:T(8,128)(2,1)S(1)}, u32[]{:S(2)}, u32[]{:S(2)}) collective-permute-start(bf16[8,16,128]{2,1,0:T(8,128)(2,1)} %get-tuple-element.48), channel_id=1, source_target_pairs={{0,4},{1,5},{2,6},{3,7},{4,0},{5,1},{6,2},{7,3},{8,12},{9,13},{10,... | collective-permute-start | bytes 98312 | tf_op jit(solution)/shard_map/near_exchange/ppermute | solution.py:417
  72.1 8.2 %collective-permute-start.8 = (bf16[8,16,128]{2,1,0:T(8,128)(2,1)}, bf16[8,16,128]{2,1,0:T(8,128)(2,1)S(1)}, u32[]{:S(2)}, u32[]{:S(2)}) collective-permute-start(bf16[8,16,128]{2,1,0:T(8,128)(2,1)} %get-tuple-element.49), channel_id=1, source_target_pairs={{0,5},{1,6},{2,7},{3,0},{4,1},{5,2},{6,3},{7,4},{8,13},{9,14},{10,... | collective-permute-start | bytes 98312 | tf_op jit(solution)/shard_map/near_exchange/ppermute | solution.py:417
  74.4 5.9 %collective-permute-start.9 = (bf16[8,16,128]{2,1,0:T(8,128)(2,1)}, bf16[8,16,128]{2,1,0:T(8,128)(2,1)S(1)}, u32[]{:S(2)}, u32[]{:S(2)}) collective-permute-start(bf16[8,16,128]{2,1,0:T(8,128)(2,1)} %get-tuple-element.50), channel_id=1, source_target_pairs={{0,6},{1,7},{2,0},{3,1},{4,2},{5,3},{6,4},{7,5},{8,14},{9,15},{10,... | collective-permute-start | bytes 98312 | tf_op jit(solution)/shard_map/near_exchange/ppermute | solution.py:417
  78.2 3.6 %collective-permute-start.10 = (bf16[8,16,128]{2,1,0:T(8,128)(2,1)}, bf16[8,16,128]{2,1,0:T(8,128)(2,1)S(1)}, u32[]{:S(2)}, u32[]{:S(2)}) collective-permute-start(bf16[8,16,128]{2,1,0:T(8,128)(2,1)} %get-tuple-element.51), channel_id=1, source_target_pairs={{0,7},{1,0},{2,1},{3,2},{4,3},{5,4},{6,5},{7,6},{8,15},{9,8},{10,9... | collective-permute-start | bytes 98312 | tf_op jit(solution)/shard_map/near_exchange/ppermute | solution.py:417
  81.8 0.8 copy-start.4
  85.2 26.2 %all-to-all-start.3 = ((bf16[128,32,128]{2,1,0:T(8,128)(2,1)}), bf16[128,32,128]{2,1,0:T(8,128)(2,1)S(1)}, u32[]{:S(2)}, u32[]{:S(2)}) async-start(bf16[128,32,128]{2,1,0:T(8,128)(2,1)} %bitcast.17), calls=%async_computation.3 | async-start | bytes 2097152 | tf_op jit(solution)/shard_map/forward_exchange/all_to_all | solution.py:431
  92.2 6.8 %collective-permute-start.13 = (bf16[128,128]{1,0:T(8,128)(2,1)S(1)}, bf16[128,128]{1,0:T(8,128)(2,1)S(1)}, u32[]{:S(2)}, u32[]{:S(2)}) collective-permute-start(bf16[128,128]{1,0:T(8,128)(2,1)S(1)} %get-tuple-element.53), channel_id=1, source_target_pairs={{0,24},{8,0},{16,8},{24,16},{32,56},{40,32},{48,40},{56,48},{64,88... | collective-permute-start | bytes 98312 | tf_op jit(solution)/shard_map/row_gather/ppermute | solution.py:425
  94.9 9.0 %collective-permute-start.12 = (bf16[128,128]{1,0:T(8,128)(2,1)S(1)}, bf16[128,128]{1,0:T(8,128)(2,1)S(1)}, u32[]{:S(2)}, u32[]{:S(2)}) collective-permute-start(bf16[128,128]{1,0:T(8,128)(2,1)S(1)} %get-tuple-element.53), channel_id=1, source_target_pairs={{0,16},{8,24},{16,0},{24,8},{32,48},{40,56},{48,32},{56,40},{64,80... | collective-permute-start | bytes 98312 | tf_op jit(solution)/shard_map/row_gather/ppermute | solution.py:425
  95.4 11.6 %collective-permute-start.11 = (bf16[128,128]{1,0:T(8,128)(2,1)S(1)}, bf16[128,128]{1,0:T(8,128)(2,1)S(1)}, u32[]{:S(2)}, u32[]{:S(2)}) collective-permute-start(bf16[128,128]{1,0:T(8,128)(2,1)S(1)} %get-tuple-element.53), channel_id=1, source_target_pairs={{0,8},{8,16},{16,24},{24,0},{32,40},{40,48},{48,56},{56,32},{64,72... | collective-permute-start | bytes 98312 | tf_op jit(solution)/shard_map/row_gather/ppermute | solution.py:425
  107.1 13.9 %copy-start.8 = (bf16[4,128,128]{2,1,0:T(8,128)(2,1)}, bf16[4,128,128]{2,1,0:T(8,128)(2,1)S(1)}, u32[]{:S(2)}) copy-start(bf16[4,128,128]{2,1,0:T(8,128)(2,1)S(1)} %pad_maximum_fusion.rest_0_) | copy-start | bytes 393220
  111.5 2.1 %copy-start.7 = (bf16[128,32,128]{2,1,0:T(8,128)(2,1)}, bf16[128,32,128]{2,1,0:T(8,128)(2,1)S(1)}, u32[]{:S(2)}) copy-start(bf16[128,32,128]{2,1,0:T(8,128)(2,1)S(1)} %all-to-all-done.3) | copy-start | bytes 3145732
  111.5 9.6 %collective-permute-start.16 = (bf16[4,128,128]{2,1,0:T(8,128)(2,1)S(1)}, bf16[4,128,128]{2,1,0:T(8,128)(2,1)S(1)}, u32[]{:S(2)}, u32[]{:S(2)}) collective-permute-start(bf16[4,128,128]{2,1,0:T(8,128)(2,1)S(1)} %pad_maximum_fusion.rest_0_), channel_id=1, source_target_pairs={{0,96},{8,104},{16,112},{24,120},{32,0},{40,8},{48,16},{56,24},{64... | collective-permute-start | bytes 393224 | tf_op jit(solution)/shard_map/row_gather/ppermute | solution.py:425
  112.3 8.7 %collective-permute-start.15 = (bf16[4,128,128]{2,1,0:T(8,128)(2,1)S(1)}, bf16[4,128,128]{2,1,0:T(8,128)(2,1)S(1)}, u32[]{:S(2)}, u32[]{:S(2)}) collective-permute-start(bf16[4,128,128]{2,1,0:T(8,128)(2,1)S(1)} %pad_maximum_fusion.rest_0_), channel_id=1, source_target_pairs={{0,64},{8,72},{16,80},{24,88},{32,96},{40,104},{48,112},{56,120},{... | collective-permute-start | bytes 393224 | tf_op jit(solution)/shard_map/row_gather/ppermute | solution.py:425
  113.6 7.5 %collective-permute-start.14 = (bf16[4,128,128]{2,1,0:T(8,128)(2,1)S(1)}, bf16[4,128,128]{2,1,0:T(8,128)(2,1)S(1)}, u32[]{:S(2)}, u32[]{:S(2)}) collective-permute-start(bf16[4,128,128]{2,1,0:T(8,128)(2,1)S(1)} %pad_maximum_fusion.rest_0_), channel_id=1, source_target_pairs={{0,32},{8,40},{16,48},{24,56},{32,64},{40,72},{48,80},{56,88},{64,... | collective-permute-start | bytes 393224 | tf_op jit(solution)/shard_map/row_gather/ppermute | solution.py:425
  121.0 7.4 %copy-start.9 = (bf16[4,128,128]{2,1,0:T(8,128)(2,1)}, bf16[4,128,128]{2,1,0:T(8,128)(2,1)S(1)}, u32[]{:S(2)}) copy-start(bf16[4,128,128]{2,1,0:T(8,128)(2,1)S(1)} %collective-permute-done.16.rest_3_) | copy-start | bytes 393220
  121.1 7.4 %copy-start.10 = (bf16[4,128,128]{2,1,0:T(8,128)(2,1)}, bf16[4,128,128]{2,1,0:T(8,128)(2,1)S(1)}, u32[]{:S(2)}) copy-start(bf16[4,128,128]{2,1,0:T(8,128)(2,1)S(1)} %collective-permute-done.15.rest_2_) | copy-start | bytes 393220
  121.1 7.4 %copy-start.11 = (bf16[4,128,128]{2,1,0:T(8,128)(2,1)}, bf16[4,128,128]{2,1,0:T(8,128)(2,1)S(1)}, u32[]{:S(2)}) copy-start(bf16[4,128,128]{2,1,0:T(8,128)(2,1)S(1)} %collective-permute-done.14.rest_1_) | copy-start | bytes 393220
  121.1 28.8 %all-to-all-start.4 = ((bf16[128,32,128]{2,1,0:T(8,128)(2,1)}), bf16[128,32,128]{2,1,0:T(8,128)(2,1)S(1)}, u32[]{:S(2)}, u32[]{:S(2)}) async-start(bf16[128,32,128]{2,1,0:T(8,128)(2,1)} %bitcast.39), calls=%async_computation.4 | async-start | bytes 2097152 | tf_op jit(solution)/shard_map/back_exchange/all_to_all | solution.py:431
  134.7 7.6 %collective-permute-start.17 = (bf16[8,16,128]{2,1,0:T(8,128)(2,1)}, bf16[8,16,128]{2,1,0:T(8,128)(2,1)S(1)}, u32[]{:S(2)}, u32[]{:S(2)}) collective-permute-start(bf16[8,16,128]{2,1,0:T(8,128)(2,1)} %get-tuple-element.64), channel_id=1, source_target_pairs={{0,1},{1,2},{2,3},{3,4},{4,5},{5,6},{6,7},{7,0},{8,9},{9,10},{10,1... | collective-permute-start | bytes 98312 | tf_op jit(solution)/shard_map/near_exchange/ppermute | solution.py:417
  136.4 9.9 %collective-permute-start.18 = (bf16[8,16,128]{2,1,0:T(8,128)(2,1)}, bf16[8,16,128]{2,1,0:T(8,128)(2,1)S(1)}, u32[]{:S(2)}, u32[]{:S(2)}) collective-permute-start(bf16[8,16,128]{2,1,0:T(8,128)(2,1)} %get-tuple-element.65), channel_id=1, source_target_pairs={{0,2},{1,3},{2,4},{3,5},{4,6},{5,7},{6,0},{7,1},{8,10},{9,11},{10,... | collective-permute-start | bytes 98312 | tf_op jit(solution)/shard_map/near_exchange/ppermute | solution.py:417
  137.9 10.3 %collective-permute-start.19 = (bf16[8,16,128]{2,1,0:T(8,128)(2,1)}, bf16[8,16,128]{2,1,0:T(8,128)(2,1)S(1)}, u32[]{:S(2)}, u32[]{:S(2)}) collective-permute-start(bf16[8,16,128]{2,1,0:T(8,128)(2,1)} %get-tuple-element.66), channel_id=1, source_target_pairs={{0,3},{1,4},{2,5},{3,6},{4,7},{5,0},{6,1},{7,2},{8,11},{9,12},{10,... | collective-permute-start | bytes 98312 | tf_op jit(solution)/shard_map/near_exchange/ppermute | solution.py:417
  139.8 8.4 %collective-permute-start.20 = (bf16[8,16,128]{2,1,0:T(8,128)(2,1)}, bf16[8,16,128]{2,1,0:T(8,128)(2,1)S(1)}, u32[]{:S(2)}, u32[]{:S(2)}) collective-permute-start(bf16[8,16,128]{2,1,0:T(8,128)(2,1)} %get-tuple-element.67), channel_id=1, source_target_pairs={{0,4},{1,5},{2,6},{3,7},{4,0},{5,1},{6,2},{7,3},{8,12},{9,13},{10,... | collective-permute-start | bytes 98312 | tf_op jit(solution)/shard_map/near_exchange/ppermute | solution.py:417
  139.9 8.4 %collective-permute-start.21 = (bf16[8,16,128]{2,1,0:T(8,128)(2,1)}, bf16[8,16,128]{2,1,0:T(8,128)(2,1)S(1)}, u32[]{:S(2)}, u32[]{:S(2)}) collective-permute-start(bf16[8,16,128]{2,1,0:T(8,128)(2,1)} %get-tuple-element.68), channel_id=1, source_target_pairs={{0,5},{1,6},{2,7},{3,0},{4,1},{5,2},{6,3},{7,4},{8,13},{9,14},{10,... | collective-permute-start | bytes 98312 | tf_op jit(solution)/shard_map/near_exchange/ppermute | solution.py:417
  142.3 5.9 %collective-permute-start.22 = (bf16[8,16,128]{2,1,0:T(8,128)(2,1)}, bf16[8,16,128]{2,1,0:T(8,128)(2,1)S(1)}, u32[]{:S(2)}, u32[]{:S(2)}) collective-permute-start(bf16[8,16,128]{2,1,0:T(8,128)(2,1)} %get-tuple-element.69), channel_id=1, source_target_pairs={{0,6},{1,7},{2,0},{3,1},{4,2},{5,3},{6,4},{7,5},{8,14},{9,15},{10,... | collective-permute-start | bytes 98312 | tf_op jit(solution)/shard_map/near_exchange/ppermute | solution.py:417
  146.3 3.6 %collective-permute-start.23 = (bf16[8,16,128]{2,1,0:T(8,128)(2,1)}, bf16[8,16,128]{2,1,0:T(8,128)(2,1)S(1)}, u32[]{:S(2)}, u32[]{:S(2)}) collective-permute-start(bf16[8,16,128]{2,1,0:T(8,128)(2,1)} %get-tuple-element.70), channel_id=1, source_target_pairs={{0,7},{1,0},{2,1},{3,2},{4,3},{5,4},{6,5},{7,6},{8,15},{9,8},{10,9... | collective-permute-start | bytes 98312 | tf_op jit(solution)/shard_map/near_exchange/ppermute | solution.py:417
  149.9 0.8 copy-start.2

commit v4 on v3

--- a/solution.py
+++ b/solution.py
@@ -28,8 +28,9 @@
 
 def start_kernel(
     rows, cols, visible_in, excitation_in, precond_in,
-    slot_out, wanted_ref, currents_ref, copies_out,
-    count_ref, code_ref, visible_ref, excitation_ref, precond_ref, slot_ref, rounded_ref, tag_ref, sems,
+    slot_out, wanted_out, currents_out, copies_out,
+    code_ref, visible_ref, excitation_ref, precond_ref, slot_ref, wanted_ref, currents_ref,
+    rounded_ref, tag_ref, sems,
 ):
     fetches = [
         pltpu.make_async_copy(visible_in, visible_ref, sems.at[0]),
@@ -46,7 +47,6 @@
     base = 2 * seg
 
     def clear(i, _):
-        count_ref[i] = 0
         code_ref[i] = seg * base + seg
         return 0
 
@@ -65,6 +65,7 @@
         pltpu.make_async_copy(rounded_ref, copies_out.at[r, : seg * exc], sems.at[5 + r])
         for r in range(rows)
     ]
+    stores.append(pltpu.make_async_copy(currents_ref, currents_out, sems.at[5 + rows]))
     for store in stores:
         store.start()
     fetches[0].wait()
@@ -74,14 +75,15 @@
             block = visible_ref[v, t]
             live = block >= 0
             owner = jnp.where(live, lax.shift_right_arithmetic(block, log2(seg)), none)
-            turn = count_ref[owner]
-            count_ref[owner] = turn + live.astype(jnp.int32)
+            code = code_ref[owner]
+            turn = (code < seg * base).astype(jnp.int32)
             row = lax.shift_right_arithmetic(owner, log2(cols))
             col = owner & (cols - 1)
             slot_ref[t * slots + v] = jnp.where(live, owner * TURNS + turn, -1)
             mine = block & (seg - 1)
             wanted_ref[jnp.where(live, col, cols), row * TURNS + turn] = mine
-            code_ref[owner] = code_ref[owner] + jnp.where(turn == 0, base, 1) * (mine - seg)
+            mine = mine - seg
+            code_ref[owner] = code + jnp.where(turn == 0, mine * base, mine)
         return 0
 
     lax.fori_loop(0, tiles, tile, 0)
@@ -97,9 +99,11 @@
     lax.fori_loop(0, rows, fill, 0)
     stores.append(pltpu.make_async_copy(tag_ref, copies_out.at[:, seg * exc :], sems.at[3]))
     stores[-1].start()
+    stores.append(pltpu.make_async_copy(wanted_ref, wanted_out, sems.at[6 + rows]))
+    stores[-1].start()
 
     def find(i, free):
-        return jnp.where(count_ref[i] < TURNS, i * TURNS + TURNS - 1, free)
+        return jnp.where((code_ref[i] & (base - 1)) == seg, i * TURNS + TURNS - 1, free)
 
     slot_ref[tiles * slots] = lax.fori_loop(0, none, find, 0, unroll=8)
     stores.append(pltpu.make_async_copy(slot_ref, slot_out, sems.at[4]))
@@ -121,18 +125,19 @@
             jax.ShapeDtypeStruct((rows, lines + exc, size), jnp.bfloat16),
         ),
         in_specs=[HBM, HBM, HBM],
-        out_specs=(HBM, SMEM, VMEM, HBM),
+        out_specs=(HBM, HBM, HBM, HBM),
         compiler_params=params(64),
         scratch_shapes=[
-            pltpu.SMEM((rows * cols + 1,), jnp.int32),
             pltpu.SMEM((rows * cols + 1,), jnp.int32),
             pltpu.SMEM(visible.shape[::-1], jnp.int32),
             pltpu.VMEM(excitation.shape, jnp.float32),
             pltpu.VMEM((1, precond.size), jnp.float32),
             pltpu.SMEM((count + 1,), jnp.int32),
+            pltpu.SMEM((cols + 1, 128), jnp.int32),
+            pltpu.VMEM(excitation.shape, jnp.float32),
             pltpu.VMEM((lines, size), jnp.bfloat16),
             pltpu.VMEM((rows, exc, size), jnp.bfloat16),
-            pltpu.SemaphoreType.DMA((5 + rows,)),
+            pltpu.SemaphoreType.DMA((7 + rows,)),
         ],
         name="start",
     )(visible.T, excitation, precond[None, :])
@@ -238,16 +243,20 @@
 
 
 def optics_kernel(
-    rows, cols, by_column, slot_ref, reflect_ref, x_in, coupling_ref, facet_ref, out_ref,
-    x_ref, weights_ref, sems,
+    rows, cols, by_column, slot_in, reflect_in, x_in, coupling_ref, facet_out, out,
+    slot_ref, reflect_ref, x_ref, weights_ref, facet_ref, out_ref, sems,
 ):
     tiles, slots, _, facets, size = coupling_ref.shape
     exc = x_ref.shape[1]
     half = exc // 2
     group = 4
-    free = slot_ref[tiles * slots]
-    whole = pltpu.make_async_copy(x_in, x_ref, sems.at[tiles])
-    whole.start()
+    wholes = [
+        pltpu.make_async_copy(slot_in, slot_ref, sems.at[tiles]),
+        pltpu.make_async_copy(x_in, x_ref, sems.at[tiles + 1]),
+        pltpu.make_async_copy(reflect_in, reflect_ref, sems.at[tiles + 2]),
+    ]
+    for whole in wholes:
+        whole.start()
 
     def place(slot):
         slot = jnp.maximum(slot, 0)
@@ -262,7 +271,9 @@
 
     for t in range(tiles):
         fetch(t).start()
-    whole.wait()
+    for whole in wholes:
+        whole.wait()
+    free = slot_ref[tiles * slots]
 
     def weights(t, v):
         pair = [weights_ref[t, u].reshape(2 * facets, size) for u in (v, v + 1)]
@@ -309,23 +320,37 @@
         return 0
 
     lax.fori_loop(0, tiles // group, some, 0)
+    stores = [
+        pltpu.make_async_copy(out_ref, out, sems.at[0]),
+        pltpu.make_async_copy(facet_ref, facet_out, sems.at[1]),
+    ]
+    for store in stores:
+        store.start()
+    for store in stores:
+        store.wait()
 
 
 def optics(slots, coupling, x, reflect, rows, cols, by_column):
     tiles, _, _, facets, size = coupling.shape
     exc = x.shape[1]
+    facet_shape = (2, exc // 2, tiles * facets)
+    out_shape = (rows * cols * TURNS, exc, size)
     return pl.pallas_call(
         functools.partial(optics_kernel, rows, cols, by_column),
         out_shape=(
-            jax.ShapeDtypeStruct((2, exc // 2, tiles * facets), jnp.float32),
-            jax.ShapeDtypeStruct((rows * cols * TURNS, exc, size), jnp.bfloat16),
+            jax.ShapeDtypeStruct(facet_shape, jnp.float32),
+            jax.ShapeDtypeStruct(out_shape, jnp.bfloat16),
         ),
-        in_specs=[SMEM, VMEM] + [pl.BlockSpec(memory_space=pl.ANY)] * 2,
-        out_specs=(VMEM, VMEM),
+        in_specs=[pl.BlockSpec(memory_space=pl.ANY)] * 4,
+        out_specs=(HBM, HBM),
         scratch_shapes=[
+            pltpu.SMEM(slots.shape, jnp.int32),
+            pltpu.VMEM(reflect.shape, jnp.float32),
             pltpu.VMEM(x.shape, jnp.bfloat16),
             pltpu.VMEM(coupling.shape, jnp.bfloat16),
-            pltpu.SemaphoreType.DMA((tiles + 1,)),
+            pltpu.VMEM(facet_shape, jnp.float32),
+            pltpu.VMEM(out_shape, jnp.bfloat16),
+            pltpu.SemaphoreType.DMA((tiles + 3,)),
         ],
         compiler_params=params(57),
         cost_estimate=pl.CostEstimate(

time: 153 us -> 151 us (0.987)
  Pallas kernels: 37.4 us -> 35.4 us
  transfers between devices with their start and end apart: 28 -> 28, of which waited for: 14 -> 15; matrix products, arithmetic and copies ran while one was open for 1% -> 1% of each run, Pallas kernels for 13% -> 13%
where the time goes in v4:
time: 151 us
  starting transfers between devices  56.1 us (37%)
  Pallas kernels  35.4 us (23%)
  waiting for transfers between devices  32.2 us (21%)
  blocking collectives  23 us (15%)
  local copies, waits for them, and re-layouts  1.81 us (1%)
    all_to_all x1, blocking collectives, shards(): x = lax.all_to_all(packed, 'col', 0, 0, tiled=True)  23 us
    ppermute x17, starting transfers between devices, along(): return lax.ppermute(x, 'col', [(i, (i + k) % cols) for i in range(cols)])  22.7 us
    all_to_all x3, starting transfers between devices, all_devices(): lax.all_to_all(sent, ('row', 'col'), 0, 0, tiled=True).reshape(x.shape)  18.9 us
    ppermute x17, waiting for transfers between devices, along(): return lax.ppermute(x, 'col', [(i, (i + k) % cols) for i in range(cols)])  13.8 us
    pallas_call x2, Pallas kernels, optics(): pl.pallas_call(functools.partial(optics_kernel, rows, cols, by_column), o...  13.5 us
    pallas_call x2, Pallas kernels, near_sums(): pl.pallas_call(functools.partial(near_kernel, count), out_shape=[jax.Shap...  12.4 us
    ppermute x6, waiting for transfers between devices, along_square(): return lax.ppermute(a, 'row', pairs)  11.7 us
    all_to_all x1, starting transfers between devices, shards(): groups = [lax.all_to_all(copies, 'row', 0, 0, tiled=True)]  7.6 us
  transfers between devices with their start and end apart: 28, of which 15 were waited for; matrix products, arithmetic and copies ran while one was open for 1% of the time, Pallas kernels for 13%

profile of v4, /device:TPU:1, one launch (start us, length us, event | category | flops | bytes accessed | tf_op | source)
XLA Modules:
  0.0 150.6 jit_solution(5879789107308059713)
XLA Ops:
  0.6 3.5 %start.1 = (s32[129]{0:T(256)}, s32[9,128]{1,0:T(8,128)}, f32[2,8,1024]{2,1,0:T(8,128)}, bf16[16,144,128]{2,1,0:T(8,128)(2,1)}) custom-call(s32[8,16]{1,0:T(8,128)} %bitcast.49, f32[2,8,1024]{2,1,0:T(8,128)} %excitation_ref.3, f32[1,1024]{1,0:T(1,128)} %bitcast.31), custom_call_target="tpu_custom_call" | custom-call | tf_op jit(solution)/shard_map/start/pallas_call | solution.py:119
  4.1 0.0 copy-start.12
  4.1 7.6 %all-to-all-start = ((bf16[16,144,128]{2,1,0:T(8,128)(2,1)}), bf16[16,144,128]{2,1,0:T(8,128)(2,1)S(1)}, u32[]{:S(2)}, u32[]{:S(2)}) async-start(bf16[16,144,128]{2,1,0:T(8,128)(2,1)} %get-tuple-element.38), calls=%async_computation | async-start | bytes 1179648 | tf_op jit(solution)/shard_map/row_exchange/all_to_all | solution.py:481
  11.8 1.0 collective-permute-start
  12.8 0.8 collective-permute-done
  13.6 3.6 %collective-permute-start.2 = (s32[2,8,128]{2,1,0:T(8,128)S(1)}, s32[2,8,128]{2,1,0:T(8,128)S(1)}, u32[]{:S(2)}, u32[]{:S(2)}) collective-permute-start(s32[2,8,128]{2,1,0:T(8,128)S(1)} %get-tuple-element.73), channel_id=1, source_target_pairs={{0,4},{1,5},{2,6},{3,7},{4,0},{5,1},{6,2},{7,3},{8,12},{9,13},{10,... | collective-permute-start | bytes 24584 | tf_op jit(solution)/shard_map/wanted_exchange/ppermute | solution.py:442
  17.2 0.7 collective-permute-start.1
  17.9 1.9 %collective-permute-start.3 = (s32[2,8,128]{2,1,0:T(8,128)S(1)}, s32[2,8,128]{2,1,0:T(8,128)S(1)}, u32[]{:S(2)}, u32[]{:S(2)}) collective-permute-start(s32[2,8,128]{2,1,0:T(8,128)S(1)} %get-tuple-element.73), channel_id=1, source_target_pairs={{0,6},{1,7},{2,0},{3,1},{4,2},{5,3},{6,4},{7,5},{8,14},{9,15},{10,... | collective-permute-start | bytes 24584 | tf_op jit(solution)/shard_map/wanted_exchange/ppermute | solution.py:442
  19.9 0.1 pad_add_fusion.2.me_ref
  20.0 1.2 collective-permute-done.1
  21.2 0.0 collective-permute-done.3
  21.2 1.5 %all-to-all-done.group_ref.rest_0_ = bf16[16,144,128]{2,1,0:T(8,128)(2,1)S(1)} async-done(((bf16[16,144,128]{2,1,0:T(8,128)(2,1)}), bf16[16,144,128]{2,1,0:T(8,128)(2,1)S(1)}, u32[]{:S(2)}, u32[]{:S(2)}) %all-to-all-start) | async-done | bytes 589856 | tf_op jit(solution)/shard_map/row_exchange/all_to_all | solution.py:481
  22.7 1.6 %pack.1 = bf16[8,33,16,128]{3,2,1,0:T(8,128)(2,1)S(1)} custom-call(s32[2]{0:T(128)S(1)} %pad_add_fusion.2.me_ref, s32[8192]{0:T(1024)S(1)} %bitcast.30, bf16[16,144,128]{2,1,0:T(8,128)(2,1)S(1)} %all-to-all-done.group_ref.rest_0_), custom_call_target="tpu_custom_call" | custom-call | tf_op jit(solution)/shard_map/pack/pallas_call | solution.py:170
  24.4 23.0 %all_to_all.25 = bf16[8,33,16,128]{3,2,1,0:T(8,128)(2,1)} all-to-all(bf16[8,33,16,128]{3,2,1,0:T(8,128)(2,1)S(1)} %pack.1), channel_id=1, replica_groups=mesh['row'=16,'col'=8] {'col'}, dimensions={0} | all-to-all | bytes 2162688 | tf_op jit(solution)/shard_map/col_exchange/all_to_all | solution.py:484
  47.3 6.8 %optics.2 = (f32[2,8,2048]{2,1,0:T(8,128)}, bf16[256,16,128]{2,1,0:T(8,128)(2,1)}) custom-call(s32[129]{0:T(256)} %get-tuple-element.39.slot_in, f32[2,2048]{1,0:T(2,128)} %reflect_in.3, bf16[264,16,128]{2,1,0:T(8,128)(2,1)} %bitcast.37, bf16[16,8,2,128,128]{4,3,2,1,0:T(8,128)(2,1)} %coupling_ref.3), custom_call_target="tpu_custom_call" | custom-call | flops 268435456 | bytes 8388608 | tf_op jit(solution)/shard_map/optics/pallas_call | solution.py:338
  54.1 5.2 %all-to-all-start.2 = ((bf16[128,32,128]{2,1,0:T(8,128)(2,1)}), bf16[128,32,128]{2,1,0:T(8,128)(2,1)S(1)}, u32[]{:S(2)}, u32[]{:S(2)}) async-start(bf16[128,32,128]{2,1,0:T(8,128)(2,1)} %bitcast.40), calls=%async_computation.2 | async-start | bytes 2097152 | tf_op jit(solution)/shard_map/back_exchange/all_to_all | solution.py:456
  59.3 0.0 copy-start.1
  59.3 0.0 copy-start.3
  59.3 0.0 copy-start.5
  59.4 6.2 %near.2 = (f32[8,16,128]{2,1,0:T(8,128)}, bf16[8,16,128]{2,1,0:T(8,128)(2,1)}, bf16[8,16,128]{2,1,0:T(8,128)(2,1)}, bf16[8,16,128]{2,1,0:T(8,128)(2,1)}, bf16[8,...) custom-call(s32[2]{0:T(128)} %copy-done.6, ...), custom_call_target="tpu_custom_call" | custom-call | flops 134217728 | bytes 8388608 | tf_op jit(solution)/shard_map/near/pallas_call | solution.py:224
  65.5 1.8 %collective-permute-start.4 = (bf16[8,16,128]{2,1,0:T(8,128)(2,1)}, bf16[8,16,128]{2,1,0:T(8,128)(2,1)S(1)}, u32[]{:S(2)}, u32[]{:S(2)}) collective-permute-start(bf16[8,16,128]{2,1,0:T(8,128)(2,1)} %get-tuple-element.45), channel_id=1, source_target_pairs={{0,1},{1,2},{2,3},{3,4},{4,5},{5,6},{6,7},{7,0},{8,9},{9,10},{10,1... | collective-permute-start | bytes 98312 | tf_op jit(solution)/shard_map/near_exchange/ppermute | solution.py:442
  67.3 1.5 collective-permute-start.5
  68.8 1.9 %collective-permute-start.6 = (bf16[8,16,128]{2,1,0:T(8,128)(2,1)}, bf16[8,16,128]{2,1,0:T(8,128)(2,1)S(1)}, u32[]{:S(2)}, u32[]{:S(2)}) collective-permute-start(bf16[8,16,128]{2,1,0:T(8,128)(2,1)} %get-tuple-element.47), channel_id=1, source_target_pairs={{0,3},{1,4},{2,5},{3,6},{4,7},{5,0},{6,1},{7,2},{8,11},{9,12},{10,... | collective-permute-start | bytes 98312 | tf_op jit(solution)/shard_map/near_exchange/ppermute | solution.py:442
  70.7 0.0 collective-permute-start.7
  70.7 2.3 %collective-permute-start.8 = (bf16[8,16,128]{2,1,0:T(8,128)(2,1)}, bf16[8,16,128]{2,1,0:T(8,128)(2,1)S(1)}, u32[]{:S(2)}, u32[]{:S(2)}) collective-permute-start(bf16[8,16,128]{2,1,0:T(8,128)(2,1)} %get-tuple-element.49), channel_id=1, source_target_pairs={{0,5},{1,6},{2,7},{3,0},{4,1},{5,2},{6,3},{7,4},{8,13},{9,14},{10,... | collective-permute-start | bytes 98312 | tf_op jit(solution)/shard_map/near_exchange/ppermute | solution.py:442
  73.0 0.7 collective-permute-start.9
  73.7 3.1 %collective-permute-done.5.rest_2_ = bf16[8,16,128]{2,1,0:T(8,128)(2,1)S(1)} collective-permute-done((bf16[8,16,128]{2,1,0:T(8,128)(2,1)}, bf16[8,16,128]{2,1,0:T(8,128)(2,1)S(1)}, u32[]{:S(2)}, u32[]{:S(2)}) %collective-permute-start.5) | collective-permute-done | bytes 32800 | tf_op jit(solution)/shard_map/near_exchange/ppermute | solution.py:442
  76.8 0.0 collective-permute-start.10
  76.8 1.0 convert_reduce_fusion
  77.8 0.1 reshape.40.tag_ref
  77.9 0.0 collective-permute-done.6.rest_3_
  77.9 0.4 collective-permute-done.7.rest_4_
  78.3 0.6 collective-permute-done.8.rest_5_
  78.9 0.0 collective-permute-done.9.rest_6_
  78.9 1.5 collective-permute-done.10.rest_7_
  80.4 0.0 all-to-all-done.2
  80.4 0.0 copy-start.4
  80.4 0.8 copy-done.4
  81.3 2.6 %update.2 = (f32[2,8,1024]{2,1,0:T(8,128)S(1)}, bf16[128,128]{1,0:T(8,128)(2,1)S(1)}, bf16[256,16,128]{2,1,0:T(8,128)(2,1)}) custom-call(s32[128]{0:T(128)S(1)} %reshape.40.tag_ref, bf16[256,16,128]{2,1,0:T(8,128)(2,1)S(1)} %bitcast.28, f32[2,8,1024]{2,1,0:T(8,128)S(1)} %copy-done.3, f32[2,8,1024]{2,1,0:T(8,128)S(1)} %copy-done.1, f32[1,1024]{1,0:T(1,128)S(1)} %bitcast.32, ...), custom_call_target="tpu_custom_call" | custom-call | tf_op jit(solution)/shard_map/update/pallas_call | solution.py:426
  83.9 7.0 %all-to-all-start.3 = ((bf16[128,32,128]{2,1,0:T(8,128)(2,1)}), bf16[128,32,128]{2,1,0:T(8,128)(2,1)S(1)}, u32[]{:S(2)}, u32[]{:S(2)}) async-start(bf16[128,32,128]{2,1,0:T(8,128)(2,1)} %bitcast.17), calls=%async_computation.3 | async-start | bytes 2097152 | tf_op jit(solution)/shard_map/forward_exchange/all_to_all | solution.py:456
  90.9 2.7 %collective-permute-start.13 = (bf16[128,128]{1,0:T(8,128)(2,1)S(1)}, bf16[128,128]{1,0:T(8,128)(2,1)S(1)}, u32[]{:S(2)}, u32[]{:S(2)}) collective-permute-start(bf16[128,128]{1,0:T(8,128)(2,1)S(1)} %get-tuple-element.53), channel_id=1, source_target_pairs={{0,24},{8,0},{16,8},{24,16},{32,56},{40,32},{48,40},{56,48},{64,88... | collective-permute-start | bytes 98312 | tf_op jit(solution)/shard_map/row_gather/ppermute | solution.py:450
  93.6 0.5 collective-permute-start.12
  94.1 0.6 collective-permute-start.11
  94.7 3.0 %collective-permute-done.13 = bf16[128,128]{1,0:T(8,128)(2,1)S(1)} collective-permute-done((bf16[128,128]{1,0:T(8,128)(2,1)S(1)}, bf16[128,128]{1,0:T(8,128)(2,1)S(1)}, u32[]{:S(2)}, u32[]{:S(2)}) %collective-permute-start.13) | collective-permute-done | bytes 32800 | tf_op jit(solution)/shard_map/row_gather/ppermute | solution.py:450
  97.7 4.9 %collective-permute-done.12 = bf16[128,128]{1,0:T(8,128)(2,1)S(1)} collective-permute-done((bf16[128,128]{1,0:T(8,128)(2,1)S(1)}, bf16[128,128]{1,0:T(8,128)(2,1)S(1)}, u32[]{:S(2)}, u32[]{:S(2)}) %collective-permute-start.12) | collective-permute-done | bytes 32800 | tf_op jit(solution)/shard_map/row_gather/ppermute | solution.py:450
  102.6 3.2 %collective-permute-done.11 = bf16[128,128]{1,0:T(8,128)(2,1)S(1)} collective-permute-done((bf16[128,128]{1,0:T(8,128)(2,1)S(1)}, bf16[128,128]{1,0:T(8,128)(2,1)S(1)}, u32[]{:S(2)}, u32[]{:S(2)}) %collective-permute-start.11) | collective-permute-done | bytes 32800 | tf_op jit(solution)/shard_map/row_gather/ppermute | solution.py:450
  105.8 4.4 %all-to-all-done.3 = bf16[128,32,128]{2,1,0:T(8,128)(2,1)S(1)} async-done(((bf16[128,32,128]{2,1,0:T(8,128)(2,1)}), bf16[128,32,128]{2,1,0:T(8,128)(2,1)S(1)}, u32[]{:S(2)}, u32[]{:S(2)}) %all-to-all-start.3) | async-done | bytes 1048608 | tf_op jit(solution)/shard_map/forward_exchange/all_to_all | solution.py:456
  110.1 0.9 collective-permute-start.16
  111.0 1.2 collective-permute-start.15
  112.2 6.8 %optics.3 = (f32[2,8,2048]{2,1,0:T(8,128)}, bf16[256,16,128]{2,1,0:T(8,128)(2,1)}) custom-call(s32[129]{0:T(256)} %get-tuple-element.39.slot_in, f32[2,2048]{1,0:T(2,128)} %reflect_in.3, bf16[256,16,128]{2,1,0:T(8,128)(2,1)} %bitcast.38, bf16[16,8,2,128,128]{4,3,2,1,0:T(8,128)(2,1)} %coupling_ref.3), custom_call_target="tpu_custom_call" | custom-call | flops 268435456 | bytes 8388608 | tf_op jit(solution)/shard_map/optics/pallas_call | solution.py:338
  119.0 0.6 collective-permute-done.14.rest_1_
  119.6 6.8 %all-to-all-start.4 = ((bf16[128,32,128]{2,1,0:T(8,128)(2,1)}), bf16[128,32,128]{2,1,0:T(8,128)(2,1)S(1)}, u32[]{:S(2)}, u32[]{:S(2)}) async-start(bf16[128,32,128]{2,1,0:T(8,128)(2,1)} %bitcast.39), calls=%async_computation.4 | async-start | bytes 2097152 | tf_op jit(solution)/shard_map/back_exchange/all_to_all | solution.py:456
  126.4 6.2 %near.3 = (f32[8,16,128]{2,1,0:T(8,128)}, bf16[8,16,128]{2,1,0:T(8,128)(2,1)}, bf16[8,16,128]{2,1,0:T(8,128)(2,1)}, bf16[8,16,128]{2,1,0:T(8,128)(2,1)}, bf16[8,...) custom-call(s32[2]{0:T(128)} %copy-done.6, ...), custom_call_target="tpu_custom_call" | custom-call | flops 134217728 | bytes 8388608 | tf_op jit(solution)/shard_map/near/pallas_call | solution.py:224
  132.6 1.8 %collective-permute-start.17 = (bf16[8,16,128]{2,1,0:T(8,128)(2,1)}, bf16[8,16,128]{2,1,0:T(8,128)(2,1)S(1)}, u32[]{:S(2)}, u32[]{:S(2)}) collective-permute-start(bf16[8,16,128]{2,1,0:T(8,128)(2,1)} %get-tuple-element.64), channel_id=1, source_target_pairs={{0,1},{1,2},{2,3},{3,4},{4,5},{5,6},{6,7},{7,0},{8,9},{9,10},{10,1... | collective-permute-start | bytes 98312 | tf_op jit(solution)/shard_map/near_exchange/ppermute | solution.py:442
  134.4 1.5 collective-permute-start.18
  135.9 1.9 %collective-permute-start.19 = (bf16[8,16,128]{2,1,0:T(8,128)(2,1)}, bf16[8,16,128]{2,1,0:T(8,128)(2,1)S(1)}, u32[]{:S(2)}, u32[]{:S(2)}) collective-permute-start(bf16[8,16,128]{2,1,0:T(8,128)(2,1)} %get-tuple-element.66), channel_id=1, source_target_pairs={{0,3},{1,4},{2,5},{3,6},{4,7},{5,0},{6,1},{7,2},{8,11},{9,12},{10,... | collective-permute-start | bytes 98312 | tf_op jit(solution)/shard_map/near_exchange/ppermute | solution.py:442
  137.8 0.1 collective-permute-start.20
  137.8 2.4 %collective-permute-start.21 = (bf16[8,16,128]{2,1,0:T(8,128)(2,1)}, bf16[8,16,128]{2,1,0:T(8,128)(2,1)S(1)}, u32[]{:S(2)}, u32[]{:S(2)}) collective-permute-start(bf16[8,16,128]{2,1,0:T(8,128)(2,1)} %get-tuple-element.68), channel_id=1, source_target_pairs={{0,5},{1,6},{2,7},{3,0},{4,1},{5,2},{6,3},{7,4},{8,13},{9,14},{10,... | collective-permute-start | bytes 98312 | tf_op jit(solution)/shard_map/near_exchange/ppermute | solution.py:442
  140.3 0.6 collective-permute-start.22
  140.8 3.4 %collective-permute-done.18.rest_2_ = bf16[8,16,128]{2,1,0:T(8,128)(2,1)S(1)} collective-permute-done((bf16[8,16,128]{2,1,0:T(8,128)(2,1)}, bf16[8,16,128]{2,1,0:T(8,128)(2,1)S(1)}, u32[]{:S(2)}, u32[]{:S(2)}) %collective-permute-start.18) | collective-permute-done | bytes 32800 | tf_op jit(solution)/shard_map/near_exchange/ppermute | solution.py:442
  144.3 1.9 %collective-permute-done.19.rest_3_ = bf16[8,16,128]{2,1,0:T(8,128)(2,1)S(1)} collective-permute-done((bf16[8,16,128]{2,1,0:T(8,128)(2,1)}, bf16[8,16,128]{2,1,0:T(8,128)(2,1)S(1)}, u32[]{:S(2)}, u32[]{:S(2)}) %collective-permute-start.19) | collective-permute-done | bytes 32800 | tf_op jit(solution)/shard_map/near_exchange/ppermute | solution.py:442
  146.2 1.6 %collective-permute-done.23.rest_7_ = bf16[8,16,128]{2,1,0:T(8,128)(2,1)S(1)} collective-permute-done((bf16[8,16,128]{2,1,0:T(8,128)(2,1)}, bf16[8,16,128]{2,1,0:T(8,128)(2,1)S(1)}, u32[]{:S(2)}, u32[]{:S(2)}) %collective-permute-start.23) | collective-permute-done | bytes 32800 | tf_op jit(solution)/shard_map/near_exchange/ppermute | solution.py:442
  147.8 0.8 copy-done.2
  148.7 1.7 %update.3 = f32[2,8,1024]{2,1,0:T(8,128)} custom-call(s32[128]{0:T(128)S(1)} %reshape.40.tag_ref, bf16[256,16,128]{2,1,0:T(8,128)(2,1)S(1)} %bitcast.29, f32[2,8,1024]{2,1,0:T(8,128)S(1)} %get-tuple-element.58.currents_ref, f32[2,8,1024]{2,1,0:T(8,128)S(1)} %copy-done.1, f32[1,1024]{1,0:T(1,128)S(1)} %bitcast.33, f32[8,16,128]{2,1,0:T(8,128)S(1)} %copy-done.2, ...), custom_call_target="tpu_custom_call" | custom-call | tf_op jit(solution)/shard_map/update/pallas_call | solution.py:426
  (34 shorter events, 0.1 us)
Async XLA Ops:
  4.1 7.6 %copy-start.12 = (s32[9,128]{1,0:T(8,128)S(1)}, s32[9,128]{1,0:T(8,128)}, u32[]{:S(2)}) copy-start(s32[9,128]{1,0:T(8,128)} %get-tuple-element.37) | copy-start | bytes 13828
  4.1 18.6 %all-to-all-start = ((bf16[16,144,128]{2,1,0:T(8,128)(2,1)}), bf16[16,144,128]{2,1,0:T(8,128)(2,1)S(1)}, u32[]{:S(2)}, u32[]{:S(2)}) async-start(bf16[16,144,128]{2,1,0:T(8,128)(2,1)} %get-tuple-element.38), calls=%async_computation | async-start | bytes 1179648 | tf_op jit(solution)/shard_map/row_exchange/all_to_all | solution.py:481
  11.8 1.9 %collective-permute-start = (s32[8,128]{1,0:T(8,128)S(1)}, s32[8,128]{1,0:T(8,128)S(1)}, u32[]{:S(2)}, u32[]{:S(2)}) collective-permute-start(s32[8,128]{1,0:T(8,128)S(1)} %get-tuple-element.75), channel_id=1, source_target_pairs={{0,1},{1,0},{2,3},{3,2},{4,5},{5,4},{6,7},{7,6},{8,9},{9,8},{10,11... | collective-permute-start | bytes 12296 | tf_op jit(solution)/shard_map/wanted_exchange/ppermute | solution.py:471
  13.6 6.4 %collective-permute-start.2 = (s32[2,8,128]{2,1,0:T(8,128)S(1)}, s32[2,8,128]{2,1,0:T(8,128)S(1)}, u32[]{:S(2)}, u32[]{:S(2)}) collective-permute-start(s32[2,8,128]{2,1,0:T(8,128)S(1)} %get-tuple-element.73), channel_id=1, source_target_pairs={{0,4},{1,5},{2,6},{3,7},{4,0},{5,1},{6,2},{7,3},{8,12},{9,13},{10,... | collective-permute-start | bytes 24584 | tf_op jit(solution)/shard_map/wanted_exchange/ppermute | solution.py:442
  17.2 4.0 %collective-permute-start.1 = (s32[2,8,128]{2,1,0:T(8,128)S(1)}, s32[2,8,128]{2,1,0:T(8,128)S(1)}, u32[]{:S(2)}, u32[]{:S(2)}) collective-permute-start(s32[2,8,128]{2,1,0:T(8,128)S(1)} %get-tuple-element.73), channel_id=1, source_target_pairs={{0,2},{1,3},{2,4},{3,5},{4,6},{5,7},{6,0},{7,1},{8,10},{9,11},{10,... | collective-permute-start | bytes 24584 | tf_op jit(solution)/shard_map/wanted_exchange/ppermute | solution.py:442
  17.9 3.3 %collective-permute-start.3 = (s32[2,8,128]{2,1,0:T(8,128)S(1)}, s32[2,8,128]{2,1,0:T(8,128)S(1)}, u32[]{:S(2)}, u32[]{:S(2)}) collective-permute-start(s32[2,8,128]{2,1,0:T(8,128)S(1)} %get-tuple-element.73), channel_id=1, source_target_pairs={{0,6},{1,7},{2,0},{3,1},{4,2},{5,3},{6,4},{7,5},{8,14},{9,15},{10,... | collective-permute-start | bytes 24584 | tf_op jit(solution)/shard_map/wanted_exchange/ppermute | solution.py:442
  20.0 27.4 %copy-start.6 = (s32[2]{0:T(128)}, s32[2]{0:T(128)S(1)}, u32[]{:S(2)}) copy-start(s32[2]{0:T(128)S(1)} %pad_add_fusion.2.me_ref) | copy-start | bytes 28
  22.7 24.6 %copy-start = (bf16[16,144,128]{2,1,0:T(8,128)(2,1)}, bf16[16,144,128]{2,1,0:T(8,128)(2,1)S(1)}, u32[]{:S(2)}) copy-start(bf16[16,144,128]{2,1,0:T(8,128)(2,1)S(1)} %all-to-all-done.group_ref.rest_0_) | copy-start | bytes 1769476
  54.1 26.3 %all-to-all-start.2 = ((bf16[128,32,128]{2,1,0:T(8,128)(2,1)}), bf16[128,32,128]{2,1,0:T(8,128)(2,1)S(1)}, u32[]{:S(2)}, u32[]{:S(2)}) async-start(bf16[128,32,128]{2,1,0:T(8,128)(2,1)} %bitcast.40), calls=%async_computation.2 | async-start | bytes 2097152 | tf_op jit(solution)/shard_map/back_exchange/all_to_all | solution.py:456
  59.3 21.1 %copy-start.1 = (f32[2,8,1024]{2,1,0:T(8,128)S(1)}, f32[2,8,1024]{2,1,0:T(8,128)}, u32[]{:S(2)}) copy-start(f32[2,8,1024]{2,1,0:T(8,128)} %excitation_ref.3) | copy-start | bytes 196612
  59.3 21.1 %copy-start.3 = (f32[2,8,1024]{2,1,0:T(8,128)S(1)}, f32[2,8,1024]{2,1,0:T(8,128)}, u32[]{:S(2)}) copy-start(f32[2,8,1024]{2,1,0:T(8,128)} %get-tuple-element.42.currents_ref) | copy-start | bytes 196612
  59.3 21.1 %copy-start.5 = (f32[1024]{0:T(1024)S(1)}, f32[1024]{0:T(1024)}, u32[]{:S(2)}) copy-start(f32[1024]{0:T(1024)} %param.8) | copy-start | bytes 12292
  65.5 7.5 %collective-permute-start.4 = (bf16[8,16,128]{2,1,0:T(8,128)(2,1)}, bf16[8,16,128]{2,1,0:T(8,128)(2,1)S(1)}, u32[]{:S(2)}, u32[]{:S(2)}) collective-permute-start(bf16[8,16,128]{2,1,0:T(8,128)(2,1)} %get-tuple-element.45), channel_id=1, source_target_pairs={{0,1},{1,2},{2,3},{3,4},{4,5},{5,6},{6,7},{7,0},{8,9},{9,10},{10,1... | collective-permute-start | bytes 98312 | tf_op jit(solution)/shard_map/near_exchange/ppermute | solution.py:442
  67.3 9.5 %collective-permute-start.5 = (bf16[8,16,128]{2,1,0:T(8,128)(2,1)}, bf16[8,16,128]{2,1,0:T(8,128)(2,1)S(1)}, u32[]{:S(2)}, u32[]{:S(2)}) collective-permute-start(bf16[8,16,128]{2,1,0:T(8,128)(2,1)} %get-tuple-element.46), channel_id=1, source_target_pairs={{0,2},{1,3},{2,4},{3,5},{4,6},{5,7},{6,0},{7,1},{8,10},{9,11},{10,... | collective-permute-start | bytes 98312 | tf_op jit(solution)/shard_map/near_exchange/ppermute | solution.py:442
  68.8 9.1 %collective-permute-start.6 = (bf16[8,16,128]{2,1,0:T(8,128)(2,1)}, bf16[8,16,128]{2,1,0:T(8,128)(2,1)S(1)}, u32[]{:S(2)}, u32[]{:S(2)}) collective-permute-start(bf16[8,16,128]{2,1,0:T(8,128)(2,1)} %get-tuple-element.47), channel_id=1, source_target_pairs={{0,3},{1,4},{2,5},{3,6},{4,7},{5,0},{6,1},{7,2},{8,11},{9,12},{10,... | collective-permute-start | bytes 98312 | tf_op jit(solution)/shard_map/near_exchange/ppermute | solution.py:442
  70.7 7.6 %collective-permute-start.7 = (bf16[8,16,128]{2,1,0:T(8,128)(2,1)}, bf16[8,16,128]{2,1,0:T(8,128)(2,1)S(1)}, u32[]{:S(2)}, u32[]{:S(2)}) collective-permute-start(bf16[8,16,128]{2,1,0:T(8,128)(2,1)} %get-tuple-element.48), channel_id=1, source_target_pairs={{0,4},{1,5},{2,6},{3,7},{4,0},{5,1},{6,2},{7,3},{8,12},{9,13},{10,... | collective-permute-start | bytes 98312 | tf_op jit(solution)/shard_map/near_exchange/ppermute | solution.py:442
  70.7 8.2 %collective-permute-start.8 = (bf16[8,16,128]{2,1,0:T(8,128)(2,1)}, bf16[8,16,128]{2,1,0:T(8,128)(2,1)S(1)}, u32[]{:S(2)}, u32[]{:S(2)}) collective-permute-start(bf16[8,16,128]{2,1,0:T(8,128)(2,1)} %get-tuple-element.49), channel_id=1, source_target_pairs={{0,5},{1,6},{2,7},{3,0},{4,1},{5,2},{6,3},{7,4},{8,13},{9,14},{10,... | collective-permute-start | bytes 98312 | tf_op jit(solution)/shard_map/near_exchange/ppermute | solution.py:442
  73.0 5.9 %collective-permute-start.9 = (bf16[8,16,128]{2,1,0:T(8,128)(2,1)}, bf16[8,16,128]{2,1,0:T(8,128)(2,1)S(1)}, u32[]{:S(2)}, u32[]{:S(2)}) collective-permute-start(bf16[8,16,128]{2,1,0:T(8,128)(2,1)} %get-tuple-element.50), channel_id=1, source_target_pairs={{0,6},{1,7},{2,0},{3,1},{4,2},{5,3},{6,4},{7,5},{8,14},{9,15},{10,... | collective-permute-start | bytes 98312 | tf_op jit(solution)/shard_map/near_exchange/ppermute | solution.py:442
  76.8 3.6 %collective-permute-start.10 = (bf16[8,16,128]{2,1,0:T(8,128)(2,1)}, bf16[8,16,128]{2,1,0:T(8,128)(2,1)S(1)}, u32[]{:S(2)}, u32[]{:S(2)}) collective-permute-start(bf16[8,16,128]{2,1,0:T(8,128)(2,1)} %get-tuple-element.51), channel_id=1, source_target_pairs={{0,7},{1,0},{2,1},{3,2},{4,3},{5,4},{6,5},{7,6},{8,15},{9,8},{10,9... | collective-permute-start | bytes 98312 | tf_op jit(solution)/shard_map/near_exchange/ppermute | solution.py:442
  80.4 0.8 copy-start.4
  83.9 26.3 %all-to-all-start.3 = ((bf16[128,32,128]{2,1,0:T(8,128)(2,1)}), bf16[128,32,128]{2,1,0:T(8,128)(2,1)S(1)}, u32[]{:S(2)}, u32[]{:S(2)}) async-start(bf16[128,32,128]{2,1,0:T(8,128)(2,1)} %bitcast.17), calls=%async_computation.3 | async-start | bytes 2097152 | tf_op jit(solution)/shard_map/forward_exchange/all_to_all | solution.py:456
  90.9 6.8 %collective-permute-start.13 = (bf16[128,128]{1,0:T(8,128)(2,1)S(1)}, bf16[128,128]{1,0:T(8,128)(2,1)S(1)}, u32[]{:S(2)}, u32[]{:S(2)}) collective-permute-start(bf16[128,128]{1,0:T(8,128)(2,1)S(1)} %get-tuple-element.53), channel_id=1, source_target_pairs={{0,24},{8,0},{16,8},{24,16},{32,56},{40,32},{48,40},{56,48},{64,88... | collective-permute-start | bytes 98312 | tf_op jit(solution)/shard_map/row_gather/ppermute | solution.py:450
  93.6 9.0 %collective-permute-start.12 = (bf16[128,128]{1,0:T(8,128)(2,1)S(1)}, bf16[128,128]{1,0:T(8,128)(2,1)S(1)}, u32[]{:S(2)}, u32[]{:S(2)}) collective-permute-start(bf16[128,128]{1,0:T(8,128)(2,1)S(1)} %get-tuple-element.53), channel_id=1, source_target_pairs={{0,16},{8,24},{16,0},{24,8},{32,48},{40,56},{48,32},{56,40},{64,80... | collective-permute-start | bytes 98312 | tf_op jit(solution)/shard_map/row_gather/ppermute | solution.py:450
  94.1 11.6 %collective-permute-start.11 = (bf16[128,128]{1,0:T(8,128)(2,1)S(1)}, bf16[128,128]{1,0:T(8,128)(2,1)S(1)}, u32[]{:S(2)}, u32[]{:S(2)}) collective-permute-start(bf16[128,128]{1,0:T(8,128)(2,1)S(1)} %get-tuple-element.53), channel_id=1, source_target_pairs={{0,8},{8,16},{16,24},{24,0},{32,40},{40,48},{48,56},{56,32},{64,72... | collective-permute-start | bytes 98312 | tf_op jit(solution)/shard_map/row_gather/ppermute | solution.py:450
  105.8 13.2 %copy-start.8 = (bf16[4,128,128]{2,1,0:T(8,128)(2,1)}, bf16[4,128,128]{2,1,0:T(8,128)(2,1)S(1)}, u32[]{:S(2)}) copy-start(bf16[4,128,128]{2,1,0:T(8,128)(2,1)S(1)} %pad_maximum_fusion.rest_0_) | copy-start | bytes 393220
  110.1 2.1 %copy-start.7 = (bf16[128,32,128]{2,1,0:T(8,128)(2,1)}, bf16[128,32,128]{2,1,0:T(8,128)(2,1)S(1)}, u32[]{:S(2)}) copy-start(bf16[128,32,128]{2,1,0:T(8,128)(2,1)S(1)} %all-to-all-done.3) | copy-start | bytes 3145732
  110.1 8.9 %collective-permute-start.16 = (bf16[4,128,128]{2,1,0:T(8,128)(2,1)S(1)}, bf16[4,128,128]{2,1,0:T(8,128)(2,1)S(1)}, u32[]{:S(2)}, u32[]{:S(2)}) collective-permute-start(bf16[4,128,128]{2,1,0:T(8,128)(2,1)S(1)} %pad_maximum_fusion.rest_0_), channel_id=1, source_target_pairs={{0,96},{8,104},{16,112},{24,120},{32,0},{40,8},{48,16},{56,24},{64... | collective-permute-start | bytes 393224 | tf_op jit(solution)/shard_map/row_gather/ppermute | solution.py:450
  111.0 8.0 %collective-permute-start.15 = (bf16[4,128,128]{2,1,0:T(8,128)(2,1)S(1)}, bf16[4,128,128]{2,1,0:T(8,128)(2,1)S(1)}, u32[]{:S(2)}, u32[]{:S(2)}) collective-permute-start(bf16[4,128,128]{2,1,0:T(8,128)(2,1)S(1)} %pad_maximum_fusion.rest_0_), channel_id=1, source_target_pairs={{0,64},{8,72},{16,80},{24,88},{32,96},{40,104},{48,112},{56,120},{... | collective-permute-start | bytes 393224 | tf_op jit(solution)/shard_map/row_gather/ppermute | solution.py:450
  112.2 7.4 %collective-permute-start.14 = (bf16[4,128,128]{2,1,0:T(8,128)(2,1)S(1)}, bf16[4,128,128]{2,1,0:T(8,128)(2,1)S(1)}, u32[]{:S(2)}, u32[]{:S(2)}) collective-permute-start(bf16[4,128,128]{2,1,0:T(8,128)(2,1)S(1)} %pad_maximum_fusion.rest_0_), channel_id=1, source_target_pairs={{0,32},{8,40},{16,48},{24,56},{32,64},{40,72},{48,80},{56,88},{64,... | collective-permute-start | bytes 393224 | tf_op jit(solution)/shard_map/row_gather/ppermute | solution.py:450
  119.0 7.4 %copy-start.9 = (bf16[4,128,128]{2,1,0:T(8,128)(2,1)}, bf16[4,128,128]{2,1,0:T(8,128)(2,1)S(1)}, u32[]{:S(2)}) copy-start(bf16[4,128,128]{2,1,0:T(8,128)(2,1)S(1)} %collective-permute-done.16.rest_3_) | copy-start | bytes 393220
  119.0 7.4 %copy-start.10 = (bf16[4,128,128]{2,1,0:T(8,128)(2,1)}, bf16[4,128,128]{2,1,0:T(8,128)(2,1)S(1)}, u32[]{:S(2)}) copy-start(bf16[4,128,128]{2,1,0:T(8,128)(2,1)S(1)} %collective-permute-done.15.rest_2_) | copy-start | bytes 393220
  119.6 6.8 %copy-start.11 = (bf16[4,128,128]{2,1,0:T(8,128)(2,1)}, bf16[4,128,128]{2,1,0:T(8,128)(2,1)S(1)}, u32[]{:S(2)}) copy-start(bf16[4,128,128]{2,1,0:T(8,128)(2,1)S(1)} %collective-permute-done.14.rest_1_) | copy-start | bytes 393220
  119.6 28.2 %all-to-all-start.4 = ((bf16[128,32,128]{2,1,0:T(8,128)(2,1)}), bf16[128,32,128]{2,1,0:T(8,128)(2,1)S(1)}, u32[]{:S(2)}, u32[]{:S(2)}) async-start(bf16[128,32,128]{2,1,0:T(8,128)(2,1)} %bitcast.39), calls=%async_computation.4 | async-start | bytes 2097152 | tf_op jit(solution)/shard_map/back_exchange/all_to_all | solution.py:456
  132.6 7.6 %collective-permute-start.17 = (bf16[8,16,128]{2,1,0:T(8,128)(2,1)}, bf16[8,16,128]{2,1,0:T(8,128)(2,1)S(1)}, u32[]{:S(2)}, u32[]{:S(2)}) collective-permute-start(bf16[8,16,128]{2,1,0:T(8,128)(2,1)} %get-tuple-element.64), channel_id=1, source_target_pairs={{0,1},{1,2},{2,3},{3,4},{4,5},{5,6},{6,7},{7,0},{8,9},{9,10},{10,1... | collective-permute-start | bytes 98312 | tf_op jit(solution)/shard_map/near_exchange/ppermute | solution.py:442
  134.4 9.9 %collective-permute-start.18 = (bf16[8,16,128]{2,1,0:T(8,128)(2,1)}, bf16[8,16,128]{2,1,0:T(8,128)(2,1)S(1)}, u32[]{:S(2)}, u32[]{:S(2)}) collective-permute-start(bf16[8,16,128]{2,1,0:T(8,128)(2,1)} %get-tuple-element.65), channel_id=1, source_target_pairs={{0,2},{1,3},{2,4},{3,5},{4,6},{5,7},{6,0},{7,1},{8,10},{9,11},{10,... | collective-permute-start | bytes 98312 | tf_op jit(solution)/shard_map/near_exchange/ppermute | solution.py:442
  135.9 10.3 %collective-permute-start.19 = (bf16[8,16,128]{2,1,0:T(8,128)(2,1)}, bf16[8,16,128]{2,1,0:T(8,128)(2,1)S(1)}, u32[]{:S(2)}, u32[]{:S(2)}) collective-permute-start(bf16[8,16,128]{2,1,0:T(8,128)(2,1)} %get-tuple-element.66), channel_id=1, source_target_pairs={{0,3},{1,4},{2,5},{3,6},{4,7},{5,0},{6,1},{7,2},{8,11},{9,12},{10,... | collective-permute-start | bytes 98312 | tf_op jit(solution)/shard_map/near_exchange/ppermute | solution.py:442
  137.8 8.4 %collective-permute-start.20 = (bf16[8,16,128]{2,1,0:T(8,128)(2,1)}, bf16[8,16,128]{2,1,0:T(8,128)(2,1)S(1)}, u32[]{:S(2)}, u32[]{:S(2)}) collective-permute-start(bf16[8,16,128]{2,1,0:T(8,128)(2,1)} %get-tuple-element.67), channel_id=1, source_target_pairs={{0,4},{1,5},{2,6},{3,7},{4,0},{5,1},{6,2},{7,3},{8,12},{9,13},{10,... | collective-permute-start | bytes 98312 | tf_op jit(solution)/shard_map/near_exchange/ppermute | solution.py:442
  137.8 8.4 %collective-permute-start.21 = (bf16[8,16,128]{2,1,0:T(8,128)(2,1)}, bf16[8,16,128]{2,1,0:T(8,128)(2,1)S(1)}, u32[]{:S(2)}, u32[]{:S(2)}) collective-permute-start(bf16[8,16,128]{2,1,0:T(8,128)(2,1)} %get-tuple-element.68), channel_id=1, source_target_pairs={{0,5},{1,6},{2,7},{3,0},{4,1},{5,2},{6,3},{7,4},{8,13},{9,14},{10,... | collective-permute-start | bytes 98312 | tf_op jit(solution)/shard_map/near_exchange/ppermute | solution.py:442
  140.3 5.9 %collective-permute-start.22 = (bf16[8,16,128]{2,1,0:T(8,128)(2,1)}, bf16[8,16,128]{2,1,0:T(8,128)(2,1)S(1)}, u32[]{:S(2)}, u32[]{:S(2)}) collective-permute-start(bf16[8,16,128]{2,1,0:T(8,128)(2,1)} %get-tuple-element.69), channel_id=1, source_target_pairs={{0,6},{1,7},{2,0},{3,1},{4,2},{5,3},{6,4},{7,5},{8,14},{9,15},{10,... | collective-permute-start | bytes 98312 | tf_op jit(solution)/shard_map/near_exchange/ppermute | solution.py:442
  144.3 3.6 %collective-permute-start.23 = (bf16[8,16,128]{2,1,0:T(8,128)(2,1)}, bf16[8,16,128]{2,1,0:T(8,128)(2,1)S(1)}, u32[]{:S(2)}, u32[]{:S(2)}) collective-permute-start(bf16[8,16,128]{2,1,0:T(8,128)(2,1)} %get-tuple-element.70), channel_id=1, source_target_pairs={{0,7},{1,0},{2,1},{3,2},{4,3},{5,4},{6,5},{7,6},{8,15},{9,8},{10,9... | collective-permute-start | bytes 98312 | tf_op jit(solution)/shard_map/near_exchange/ppermute | solution.py:442
  147.8 0.8 copy-start.2

commit v5 on v4

--- a/solution.py
+++ b/solution.py
@@ -178,7 +178,7 @@
 
 
 def near_kernel(count, me_ref, index_ref, blocks_ref, *rest):
-    group_refs, outs, (weights_ref, sems, gather_ref) = rest[:count], rest[count:-3], rest[-3:]
+    groups, outs, (weights_ref, sems, group_ref) = rest[:count], rest[count:-3], rest[-3:]
     cols = len(outs)
     rows, per_row, _, size, _ = blocks_ref.shape
     seg, exc = outs[0].shape[:2]
@@ -186,19 +186,25 @@
     me = me_ref[0]
     peers = [(me + k) & (cols - 1) for k in range(cols)]
     order = list(range(1, cols)) + [0]
+    fetches = []
+    if count == 1:
+        fetches.append(pltpu.make_async_copy(groups[0], group_ref, sems.at[cols]))
+    else:
+        x, y = lax.shift_right_arithmetic(me_ref[1], log2(count)), me_ref[1] & (count - 1)
+        for i in range(count):
+            for j in range(count):
+                source = ((x - i) & (count - 1)) * count + ((y - j) & (count - 1))
+                sem = sems.at[cols + i * count + j]
+                fetches.append(pltpu.make_async_copy(groups[i].at[j], group_ref.at[source], sem))
+    for fetch in fetches:
+        fetch.start()
     copies = {}
     for k in order:
         some = pl.ds(pl.multiple_of(peers[k] * seg, seg), seg)
         copies[k] = pltpu.make_async_copy(blocks_ref.at[some], weights_ref.at[k], sems.at[k])
         copies[k].start()
-    group_ref = group_refs[0]
-    if count > 1:
-        group_ref = gather_ref
-        x, y = lax.shift_right_arithmetic(me_ref[1], log2(count)), me_ref[1] & (count - 1)
-        for i in range(count):
-            for j in range(count):
-                source = ((x - i) & (count - 1)) * count + ((y - j) & (count - 1))
-                gather_ref[source] = group_refs[i][j]
+    for fetch in fetches:
+        fetch.wait()
     for k in order:
         copies[k].wait()
         for i in range(seg):
@@ -220,18 +226,18 @@
     rows, per_row, _, size, _ = blocks.shape
     cols = rows // seg
     count = len(groups)
-    gather = (count * count, seg * exc, size) if count > 1 else (1, exc, size)
+    gather = (count * count, seg * exc, size) if count > 1 else groups[0].shape
     return pl.pallas_call(
         functools.partial(near_kernel, count),
         out_shape=[
             jax.ShapeDtypeStruct((seg, exc, size), jnp.bfloat16 if k else jnp.float32)
             for k in range(cols)
         ],
-        in_specs=[SMEM, SMEM, pl.BlockSpec(memory_space=pl.ANY)] + [VMEM] * count,
+        in_specs=[SMEM, SMEM] + [pl.BlockSpec(memory_space=pl.ANY)] * (1 + count),
         out_specs=[VMEM] * cols,
         scratch_shapes=[
             pltpu.VMEM((cols, seg) + blocks.shape[1:], jnp.bfloat16),
-            pltpu.SemaphoreType.DMA((cols,)),
+            pltpu.SemaphoreType.DMA((cols + count * count,)),
             pltpu.VMEM(gather, jnp.bfloat16),
         ],
         compiler_params=params(57),
@@ -362,6 +368,8 @@
 
 def update_kernel(cols, last, tag_ref, back_ref, currents_ref, excitation_ref, precond_ref, *rest):
     near_refs, rest = rest[:cols], rest[cols:]
+    if not last:
+        rest, more_last = rest[:-2], rest[-2:]
     out_ref, (total_ref, *more_refs, own_ref, sem) = rest[0], rest[-6:]
     own = pltpu.make_async_copy(near_refs[0], own_ref, sem)
     own.start()
@@ -404,7 +412,8 @@
             if not last:
                 total_ref[b, some] = new
     if not last:
-        rounded_ref, sent_ref = rest[1:3]
+        rounded_ref, sent_out = rest[1:3]
+        sent_ref, sent_sems = more_last
         for b in range(seg):
             rounded_ref[b * exc : (b + 1) * exc] = total_ref[b].astype(jnp.bfloat16)
 
@@ -414,7 +423,17 @@
                 sent_ref[slot] = rounded_ref[pl.ds(line, exc), :]
             return 0
 
-        lax.fori_loop(0, rows, fill, 0)
+        stores = []
+        for c in range(sent_sems.shape[0]):
+            some_rows = rows // sent_sems.shape[0]
+            lax.fori_loop(c * some_rows, (c + 1) * some_rows, fill, 0)
+            part = pl.ds(c * some_rows * cols * TURNS, some_rows * cols * TURNS)
+            stores.append(
+                pltpu.make_async_copy(sent_ref.at[part], sent_out.at[part], sent_sems.at[c])
+            )
+            stores[-1].start()
+        for store in stores:
+            store.wait()
 
 
 def update(tags, back, near, currents, excitation, precond, last):
@@ -427,12 +446,13 @@
         functools.partial(update_kernel, len(near), last),
         out_shape=out_shape,
         in_specs=[SMEM] + [VMEM] * 4 + [HBM] + [VMEM] * (len(near) - 1),
-        out_specs=[VMEM] * len(out_shape),
+        out_specs=[VMEM] * len(out_shape) if last else [VMEM, VMEM, HBM],
         scratch_shapes=[
             *[pltpu.VMEM((seg + 1, exc, size), jnp.float32)] * 4,
             pltpu.VMEM((seg, exc, size), jnp.float32),
             pltpu.SemaphoreType.DMA,
-        ],
+        ]
+        + ([] if last else [pltpu.VMEM(back.shape, jnp.bfloat16), pltpu.SemaphoreType.DMA((4,))]),
         compiler_params=params(16),
         name="update",
     )(tags, back, currents, excitation, precond[None, :], *near)

time: 151 us -> 151 us (level)
  transfers between devices with their start and end apart: 28 -> 28, of which waited for: 15 -> 14; matrix products, arithmetic and copies ran while one was open for 1% -> 1% of each run, Pallas kernels for 13% -> 13%
where the time goes in v5:
time: 151 us; the launch traced here: 150 us
  starting transfers between devices  55.8 us (37%)
  Pallas kernels  35 us (23%)
  waiting for transfers between devices  32.6 us (22%)
  blocking collectives  23 us (15%)
  local copies, waits for them, and re-layouts  1.81 us (1%)
    all_to_all x1, blocking collectives, shards(): x = lax.all_to_all(packed, 'col', 0, 0, tiled=True)  23 us
    ppermute x17, starting transfers between devices, along(): return lax.ppermute(x, 'col', [(i, (i + k) % cols) for i in range(cols)])  22.7 us
    all_to_all x3, starting transfers between devices, all_devices(): lax.all_to_all(sent, ('row', 'col'), 0, 0, tiled=True).reshape(x.shape)  18.6 us
    ppermute x17, waiting for transfers between devices, along(): return lax.ppermute(x, 'col', [(i, (i + k) % cols) for i in range(cols)])  14.3 us
    pallas_call x2, Pallas kernels, optics(): pl.pallas_call(functools.partial(optics_kernel, rows, cols, by_column), o...  13.5 us
    pallas_call x2, Pallas kernels, near_sums(): pl.pallas_call(functools.partial(near_kernel, count), out_shape=[jax.Shap...  12.3 us
    ppermute x6, waiting for transfers between devices, along_square(): return lax.ppermute(a, 'row', pairs)  11.7 us
    all_to_all x1, starting transfers between devices, shards(): groups = [lax.all_to_all(copies, 'row', 0, 0, tiled=True)]  7.6 us
  transfers between devices with their start and end apart: 28, of which 14 were waited for; matrix products, arithmetic and copies ran while one was open for 1% of the time, Pallas kernels for 13%

profile of v5, /device:TPU:1, one launch (start us, length us, event | category | flops | bytes accessed | tf_op | source)
XLA Modules:
  0.0 150.4 jit_solution(8979619085999672375)
XLA Ops:
  0.6 3.5 %start.1 = (s32[129]{0:T(256)}, s32[9,128]{1,0:T(8,128)}, f32[2,8,1024]{2,1,0:T(8,128)}, bf16[16,144,128]{2,1,0:T(8,128)(2,1)}) custom-call(s32[8,16]{1,0:T(8,128)} %bitcast.49, f32[2,8,1024]{2,1,0:T(8,128)} %excitation_ref.3, f32[1,1024]{1,0:T(1,128)} %bitcast.31), custom_call_target="tpu_custom_call" | custom-call | tf_op jit(solution)/shard_map/start/pallas_call | solution.py:119
  4.1 0.0 copy-start.12
  4.1 7.6 %all-to-all-start = ((bf16[16,144,128]{2,1,0:T(8,128)(2,1)}), bf16[16,144,128]{2,1,0:T(8,128)(2,1)S(1)}, u32[]{:S(2)}, u32[]{:S(2)}) async-start(bf16[16,144,128]{2,1,0:T(8,128)(2,1)} %get-tuple-element.38), calls=%async_computation | async-start | bytes 1179648 | tf_op jit(solution)/shard_map/row_exchange/all_to_all | solution.py:501
  11.8 1.0 collective-permute-start
  12.8 0.8 collective-permute-done
  13.6 3.6 %collective-permute-start.2 = (s32[2,8,128]{2,1,0:T(8,128)S(1)}, s32[2,8,128]{2,1,0:T(8,128)S(1)}, u32[]{:S(2)}, u32[]{:S(2)}) collective-permute-start(s32[2,8,128]{2,1,0:T(8,128)S(1)} %get-tuple-element.73), channel_id=1, source_target_pairs={{0,4},{1,5},{2,6},{3,7},{4,0},{5,1},{6,2},{7,3},{8,12},{9,13},{10,... | collective-permute-start | bytes 24584 | tf_op jit(solution)/shard_map/wanted_exchange/ppermute | solution.py:462
  17.2 0.7 collective-permute-start.1
  17.9 1.9 %collective-permute-start.3 = (s32[2,8,128]{2,1,0:T(8,128)S(1)}, s32[2,8,128]{2,1,0:T(8,128)S(1)}, u32[]{:S(2)}, u32[]{:S(2)}) collective-permute-start(s32[2,8,128]{2,1,0:T(8,128)S(1)} %get-tuple-element.73), channel_id=1, source_target_pairs={{0,6},{1,7},{2,0},{3,1},{4,2},{5,3},{6,4},{7,5},{8,14},{9,15},{10,... | collective-permute-start | bytes 24584 | tf_op jit(solution)/shard_map/wanted_exchange/ppermute | solution.py:462
  19.9 0.1 pad_add_fusion.2.me_ref
  20.0 1.2 collective-permute-done.1
  21.2 0.0 collective-permute-done.3
  21.2 1.5 %all-to-all-done.group_ref.rest_0_ = bf16[16,144,128]{2,1,0:T(8,128)(2,1)S(1)} async-done(((bf16[16,144,128]{2,1,0:T(8,128)(2,1)}), bf16[16,144,128]{2,1,0:T(8,128)(2,1)S(1)}, u32[]{:S(2)}, u32[]{:S(2)}) %all-to-all-start) | async-done | bytes 589856 | tf_op jit(solution)/shard_map/row_exchange/all_to_all | solution.py:501
  22.7 1.6 %pack.1 = bf16[8,33,16,128]{3,2,1,0:T(8,128)(2,1)S(1)} custom-call(s32[2]{0:T(128)S(1)} %pad_add_fusion.2.me_ref, s32[8192]{0:T(1024)S(1)} %bitcast.30, bf16[16,144,128]{2,1,0:T(8,128)(2,1)S(1)} %all-to-all-done.group_ref.rest_0_), custom_call_target="tpu_custom_call" | custom-call | tf_op jit(solution)/shard_map/pack/pallas_call | solution.py:170
  24.4 23.0 %all_to_all.25 = bf16[8,33,16,128]{3,2,1,0:T(8,128)(2,1)} all-to-all(bf16[8,33,16,128]{3,2,1,0:T(8,128)(2,1)S(1)} %pack.1), channel_id=1, replica_groups=mesh['row'=16,'col'=8] {'col'}, dimensions={0} | all-to-all | bytes 2162688 | tf_op jit(solution)/shard_map/col_exchange/all_to_all | solution.py:504
  47.3 6.8 %optics.2 = (f32[2,8,2048]{2,1,0:T(8,128)}, bf16[256,16,128]{2,1,0:T(8,128)(2,1)}) custom-call(s32[129]{0:T(256)} %get-tuple-element.39.slot_in, f32[2,2048]{1,0:T(2,128)} %reflect_in.3, bf16[264,16,128]{2,1,0:T(8,128)(2,1)} %bitcast.37, bf16[16,8,2,128,128]{4,3,2,1,0:T(8,128)(2,1)} %coupling_ref.3), custom_call_target="tpu_custom_call" | custom-call | flops 268435456 | bytes 8388608 | tf_op jit(solution)/shard_map/optics/pallas_call | solution.py:344
  54.1 5.2 %all-to-all-start.2 = ((bf16[128,32,128]{2,1,0:T(8,128)(2,1)}), bf16[128,32,128]{2,1,0:T(8,128)(2,1)S(1)}, u32[]{:S(2)}, u32[]{:S(2)}) async-start(bf16[128,32,128]{2,1,0:T(8,128)(2,1)} %bitcast.40), calls=%async_computation.2 | async-start | bytes 2097152 | tf_op jit(solution)/shard_map/back_exchange/all_to_all | solution.py:476
  59.3 0.0 copy-start.1
  59.3 0.0 copy-start.3
  59.3 0.0 copy-start.5
  59.4 6.1 %near.2 = (f32[8,16,128]{2,1,0:T(8,128)}, bf16[8,16,128]{2,1,0:T(8,128)(2,1)}, bf16[8,16,128]{2,1,0:T(8,128)(2,1)}, bf16[8,16,128]{2,1,0:T(8,128)(2,1)}, bf16[8,...) custom-call(s32[2]{0:T(128)} %copy-done.6, ...), custom_call_target="tpu_custom_call" | custom-call | flops 134217728 | bytes 8388608 | tf_op jit(solution)/shard_map/near/pallas_call | solution.py:230
  65.5 1.8 %collective-permute-start.4 = (bf16[8,16,128]{2,1,0:T(8,128)(2,1)}, bf16[8,16,128]{2,1,0:T(8,128)(2,1)S(1)}, u32[]{:S(2)}, u32[]{:S(2)}) collective-permute-start(bf16[8,16,128]{2,1,0:T(8,128)(2,1)} %get-tuple-element.45), channel_id=1, source_target_pairs={{0,1},{1,2},{2,3},{3,4},{4,5},{5,6},{6,7},{7,0},{8,9},{9,10},{10,1... | collective-permute-start | bytes 98312 | tf_op jit(solution)/shard_map/near_exchange/ppermute | solution.py:462
  67.2 1.5 collective-permute-start.5
  68.7 1.9 %collective-permute-start.6 = (bf16[8,16,128]{2,1,0:T(8,128)(2,1)}, bf16[8,16,128]{2,1,0:T(8,128)(2,1)S(1)}, u32[]{:S(2)}, u32[]{:S(2)}) collective-permute-start(bf16[8,16,128]{2,1,0:T(8,128)(2,1)} %get-tuple-element.47), channel_id=1, source_target_pairs={{0,3},{1,4},{2,5},{3,6},{4,7},{5,0},{6,1},{7,2},{8,11},{9,12},{10,... | collective-permute-start | bytes 98312 | tf_op jit(solution)/shard_map/near_exchange/ppermute | solution.py:462
  70.6 0.0 collective-permute-start.7
  70.6 2.3 %collective-permute-start.8 = (bf16[8,16,128]{2,1,0:T(8,128)(2,1)}, bf16[8,16,128]{2,1,0:T(8,128)(2,1)S(1)}, u32[]{:S(2)}, u32[]{:S(2)}) collective-permute-start(bf16[8,16,128]{2,1,0:T(8,128)(2,1)} %get-tuple-element.49), channel_id=1, source_target_pairs={{0,5},{1,6},{2,7},{3,0},{4,1},{5,2},{6,3},{7,4},{8,13},{9,14},{10,... | collective-permute-start | bytes 98312 | tf_op jit(solution)/shard_map/near_exchange/ppermute | solution.py:462
  72.9 0.0 collective-permute-done.4.rest_1_
  72.9 0.7 collective-permute-start.9
  73.7 3.5 %collective-permute-done.5.rest_2_ = bf16[8,16,128]{2,1,0:T(8,128)(2,1)S(1)} collective-permute-done((bf16[8,16,128]{2,1,0:T(8,128)(2,1)}, bf16[8,16,128]{2,1,0:T(8,128)(2,1)S(1)}, u32[]{:S(2)}, u32[]{:S(2)}) %collective-permute-start.5) | collective-permute-done | bytes 32800 | tf_op jit(solution)/shard_map/near_exchange/ppermute | solution.py:462
  77.2 1.0 convert_reduce_fusion
  78.1 0.1 reshape.40.tag_ref
  78.2 0.9 collective-permute-done.6.rest_3_
  79.1 0.0 collective-permute-done.7.rest_4_
  79.1 0.0 collective-permute-done.8.rest_5_
  79.1 0.0 collective-permute-done.9.rest_6_
  79.1 1.6 %collective-permute-done.10.rest_7_ = bf16[8,16,128]{2,1,0:T(8,128)(2,1)S(1)} collective-permute-done((bf16[8,16,128]{2,1,0:T(8,128)(2,1)}, bf16[8,16,128]{2,1,0:T(8,128)(2,1)S(1)}, u32[]{:S(2)}, u32[]{:S(2)}) %collective-permute-start.10) | collective-permute-done | bytes 32800 | tf_op jit(solution)/shard_map/near_exchange/ppermute | solution.py:462
  80.7 0.0 all-to-all-done.2
  80.7 0.0 copy-start.4
  80.7 0.8 copy-done.4
  81.6 2.3 %update.2 = (f32[2,8,1024]{2,1,0:T(8,128)S(1)}, bf16[128,128]{1,0:T(8,128)(2,1)S(1)}, bf16[256,16,128]{2,1,0:T(8,128)(2,1)}) custom-call(s32[128]{0:T(128)S(1)} %reshape.40.tag_ref, bf16[256,16,128]{2,1,0:T(8,128)(2,1)S(1)} %bitcast.28, f32[2,8,1024]{2,1,0:T(8,128)S(1)} %copy-done.3, f32[2,8,1024]{2,1,0:T(8,128)S(1)} %copy-done.1, f32[1,1024]{1,0:T(1,128)S(1)} %bitcast.32, ...), custom_call_target="tpu_custom_call" | custom-call | tf_op jit(solution)/shard_map/update/pallas_call | solution.py:445
  83.9 6.7 %all-to-all-start.3 = ((bf16[128,32,128]{2,1,0:T(8,128)(2,1)}), bf16[128,32,128]{2,1,0:T(8,128)(2,1)S(1)}, u32[]{:S(2)}, u32[]{:S(2)}) async-start(bf16[128,32,128]{2,1,0:T(8,128)(2,1)} %bitcast.17), calls=%async_computation.3 | async-start | bytes 2097152 | tf_op jit(solution)/shard_map/forward_exchange/all_to_all | solution.py:476
  90.6 2.7 %collective-permute-start.13 = (bf16[128,128]{1,0:T(8,128)(2,1)S(1)}, bf16[128,128]{1,0:T(8,128)(2,1)S(1)}, u32[]{:S(2)}, u32[]{:S(2)}) collective-permute-start(bf16[128,128]{1,0:T(8,128)(2,1)S(1)} %get-tuple-element.53), channel_id=1, source_target_pairs={{0,24},{8,0},{16,8},{24,16},{32,56},{40,32},{48,40},{56,48},{64,88... | collective-permute-start | bytes 98312 | tf_op jit(solution)/shard_map/row_gather/ppermute | solution.py:470
  93.3 0.5 collective-permute-start.12
  93.9 0.6 collective-permute-start.11
  94.4 3.0 %collective-permute-done.13 = bf16[128,128]{1,0:T(8,128)(2,1)S(1)} collective-permute-done((bf16[128,128]{1,0:T(8,128)(2,1)S(1)}, bf16[128,128]{1,0:T(8,128)(2,1)S(1)}, u32[]{:S(2)}, u32[]{:S(2)}) %collective-permute-start.13) | collective-permute-done | bytes 32800 | tf_op jit(solution)/shard_map/row_gather/ppermute | solution.py:470
  97.5 4.9 %collective-permute-done.12 = bf16[128,128]{1,0:T(8,128)(2,1)S(1)} collective-permute-done((bf16[128,128]{1,0:T(8,128)(2,1)S(1)}, bf16[128,128]{1,0:T(8,128)(2,1)S(1)}, u32[]{:S(2)}, u32[]{:S(2)}) %collective-permute-start.12) | collective-permute-done | bytes 32800 | tf_op jit(solution)/shard_map/row_gather/ppermute | solution.py:470
  102.3 3.2 %collective-permute-done.11 = bf16[128,128]{1,0:T(8,128)(2,1)S(1)} collective-permute-done((bf16[128,128]{1,0:T(8,128)(2,1)S(1)}, bf16[128,128]{1,0:T(8,128)(2,1)S(1)}, u32[]{:S(2)}, u32[]{:S(2)}) %collective-permute-start.11) | collective-permute-done | bytes 32800 | tf_op jit(solution)/shard_map/row_gather/ppermute | solution.py:470
  105.5 4.4 %all-to-all-done.3 = bf16[128,32,128]{2,1,0:T(8,128)(2,1)S(1)} async-done(((bf16[128,32,128]{2,1,0:T(8,128)(2,1)}), bf16[128,32,128]{2,1,0:T(8,128)(2,1)S(1)}, u32[]{:S(2)}, u32[]{:S(2)}) %all-to-all-start.3) | async-done | bytes 1048608 | tf_op jit(solution)/shard_map/forward_exchange/all_to_all | solution.py:476
  109.9 0.9 collective-permute-start.16
  110.8 1.2 collective-permute-start.15
  112.0 6.8 %optics.3 = (f32[2,8,2048]{2,1,0:T(8,128)}, bf16[256,16,128]{2,1,0:T(8,128)(2,1)}) custom-call(s32[129]{0:T(256)} %get-tuple-element.39.slot_in, f32[2,2048]{1,0:T(2,128)} %reflect_in.3, bf16[256,16,128]{2,1,0:T(8,128)(2,1)} %bitcast.38, bf16[16,8,2,128,128]{4,3,2,1,0:T(8,128)(2,1)} %coupling_ref.3), custom_call_target="tpu_custom_call" | custom-call | flops 268435456 | bytes 8388608 | tf_op jit(solution)/shard_map/optics/pallas_call | solution.py:344
  118.8 0.6 collective-permute-done.14.rest_1_
  119.4 6.8 %all-to-all-start.4 = ((bf16[128,32,128]{2,1,0:T(8,128)(2,1)}), bf16[128,32,128]{2,1,0:T(8,128)(2,1)S(1)}, u32[]{:S(2)}, u32[]{:S(2)}) async-start(bf16[128,32,128]{2,1,0:T(8,128)(2,1)} %bitcast.39), calls=%async_computation.4 | async-start | bytes 2097152 | tf_op jit(solution)/shard_map/back_exchange/all_to_all | solution.py:476
  126.2 6.2 %near.3 = (f32[8,16,128]{2,1,0:T(8,128)}, bf16[8,16,128]{2,1,0:T(8,128)(2,1)}, bf16[8,16,128]{2,1,0:T(8,128)(2,1)}, bf16[8,16,128]{2,1,0:T(8,128)(2,1)}, bf16[8,...) custom-call(s32[2]{0:T(128)} %copy-done.6, ...), custom_call_target="tpu_custom_call" | custom-call | flops 134217728 | bytes 8388608 | tf_op jit(solution)/shard_map/near/pallas_call | solution.py:230
  132.4 1.8 %collective-permute-start.17 = (bf16[8,16,128]{2,1,0:T(8,128)(2,1)}, bf16[8,16,128]{2,1,0:T(8,128)(2,1)S(1)}, u32[]{:S(2)}, u32[]{:S(2)}) collective-permute-start(bf16[8,16,128]{2,1,0:T(8,128)(2,1)} %get-tuple-element.64), channel_id=1, source_target_pairs={{0,1},{1,2},{2,3},{3,4},{4,5},{5,6},{6,7},{7,0},{8,9},{9,10},{10,1... | collective-permute-start | bytes 98312 | tf_op jit(solution)/shard_map/near_exchange/ppermute | solution.py:462
  134.2 1.5 collective-permute-start.18
  135.6 1.9 %collective-permute-start.19 = (bf16[8,16,128]{2,1,0:T(8,128)(2,1)}, bf16[8,16,128]{2,1,0:T(8,128)(2,1)S(1)}, u32[]{:S(2)}, u32[]{:S(2)}) collective-permute-start(bf16[8,16,128]{2,1,0:T(8,128)(2,1)} %get-tuple-element.66), channel_id=1, source_target_pairs={{0,3},{1,4},{2,5},{3,6},{4,7},{5,0},{6,1},{7,2},{8,11},{9,12},{10,... | collective-permute-start | bytes 98312 | tf_op jit(solution)/shard_map/near_exchange/ppermute | solution.py:462
  137.5 0.0 collective-permute-start.20
  137.6 2.5 %collective-permute-start.21 = (bf16[8,16,128]{2,1,0:T(8,128)(2,1)}, bf16[8,16,128]{2,1,0:T(8,128)(2,1)S(1)}, u32[]{:S(2)}, u32[]{:S(2)}) collective-permute-start(bf16[8,16,128]{2,1,0:T(8,128)(2,1)} %get-tuple-element.68), channel_id=1, source_target_pairs={{0,5},{1,6},{2,7},{3,0},{4,1},{5,2},{6,3},{7,4},{8,13},{9,14},{10,... | collective-permute-start | bytes 98312 | tf_op jit(solution)/shard_map/near_exchange/ppermute | solution.py:462
  140.1 0.6 collective-permute-start.22
  140.6 3.4 %collective-permute-done.18.rest_2_ = bf16[8,16,128]{2,1,0:T(8,128)(2,1)S(1)} collective-permute-done((bf16[8,16,128]{2,1,0:T(8,128)(2,1)}, bf16[8,16,128]{2,1,0:T(8,128)(2,1)S(1)}, u32[]{:S(2)}, u32[]{:S(2)}) %collective-permute-start.18) | collective-permute-done | bytes 32800 | tf_op jit(solution)/shard_map/near_exchange/ppermute | solution.py:462
  144.1 1.9 %collective-permute-done.19.rest_3_ = bf16[8,16,128]{2,1,0:T(8,128)(2,1)S(1)} collective-permute-done((bf16[8,16,128]{2,1,0:T(8,128)(2,1)}, bf16[8,16,128]{2,1,0:T(8,128)(2,1)S(1)}, u32[]{:S(2)}, u32[]{:S(2)}) %collective-permute-start.19) | collective-permute-done | bytes 32800 | tf_op jit(solution)/shard_map/near_exchange/ppermute | solution.py:462
  146.0 1.6 %collective-permute-done.23.rest_7_ = bf16[8,16,128]{2,1,0:T(8,128)(2,1)S(1)} collective-permute-done((bf16[8,16,128]{2,1,0:T(8,128)(2,1)}, bf16[8,16,128]{2,1,0:T(8,128)(2,1)S(1)}, u32[]{:S(2)}, u32[]{:S(2)}) %collective-permute-start.23) | collective-permute-done | bytes 32800 | tf_op jit(solution)/shard_map/near_exchange/ppermute | solution.py:462
  147.6 0.8 copy-done.2
  148.5 1.7 %update.3 = f32[2,8,1024]{2,1,0:T(8,128)} custom-call(s32[128]{0:T(128)S(1)} %reshape.40.tag_ref, bf16[256,16,128]{2,1,0:T(8,128)(2,1)S(1)} %bitcast.29, f32[2,8,1024]{2,1,0:T(8,128)S(1)} %get-tuple-element.58.currents_ref, f32[2,8,1024]{2,1,0:T(8,128)S(1)} %copy-done.1, f32[1,1024]{1,0:T(1,128)S(1)} %bitcast.33, f32[8,16,128]{2,1,0:T(8,128)S(1)} %copy-done.2, ...), custom_call_target="tpu_custom_call" | custom-call | tf_op jit(solution)/shard_map/update/pallas_call | solution.py:445
  (34 shorter events, 0.1 us)
Async XLA Ops:
  4.1 7.6 %copy-start.12 = (s32[9,128]{1,0:T(8,128)S(1)}, s32[9,128]{1,0:T(8,128)}, u32[]{:S(2)}) copy-start(s32[9,128]{1,0:T(8,128)} %get-tuple-element.37) | copy-start | bytes 13828
  4.1 18.6 %all-to-all-start = ((bf16[16,144,128]{2,1,0:T(8,128)(2,1)}), bf16[16,144,128]{2,1,0:T(8,128)(2,1)S(1)}, u32[]{:S(2)}, u32[]{:S(2)}) async-start(bf16[16,144,128]{2,1,0:T(8,128)(2,1)} %get-tuple-element.38), calls=%async_computation | async-start | bytes 1179648 | tf_op jit(solution)/shard_map/row_exchange/all_to_all | solution.py:501
  11.8 1.9 %collective-permute-start = (s32[8,128]{1,0:T(8,128)S(1)}, s32[8,128]{1,0:T(8,128)S(1)}, u32[]{:S(2)}, u32[]{:S(2)}) collective-permute-start(s32[8,128]{1,0:T(8,128)S(1)} %get-tuple-element.75), channel_id=1, source_target_pairs={{0,1},{1,0},{2,3},{3,2},{4,5},{5,4},{6,7},{7,6},{8,9},{9,8},{10,11... | collective-permute-start | bytes 12296 | tf_op jit(solution)/shard_map/wanted_exchange/ppermute | solution.py:491
  13.6 6.4 %collective-permute-start.2 = (s32[2,8,128]{2,1,0:T(8,128)S(1)}, s32[2,8,128]{2,1,0:T(8,128)S(1)}, u32[]{:S(2)}, u32[]{:S(2)}) collective-permute-start(s32[2,8,128]{2,1,0:T(8,128)S(1)} %get-tuple-element.73), channel_id=1, source_target_pairs={{0,4},{1,5},{2,6},{3,7},{4,0},{5,1},{6,2},{7,3},{8,12},{9,13},{10,... | collective-permute-start | bytes 24584 | tf_op jit(solution)/shard_map/wanted_exchange/ppermute | solution.py:462
  17.2 4.0 %collective-permute-start.1 = (s32[2,8,128]{2,1,0:T(8,128)S(1)}, s32[2,8,128]{2,1,0:T(8,128)S(1)}, u32[]{:S(2)}, u32[]{:S(2)}) collective-permute-start(s32[2,8,128]{2,1,0:T(8,128)S(1)} %get-tuple-element.73), channel_id=1, source_target_pairs={{0,2},{1,3},{2,4},{3,5},{4,6},{5,7},{6,0},{7,1},{8,10},{9,11},{10,... | collective-permute-start | bytes 24584 | tf_op jit(solution)/shard_map/wanted_exchange/ppermute | solution.py:462
  17.9 3.3 %collective-permute-start.3 = (s32[2,8,128]{2,1,0:T(8,128)S(1)}, s32[2,8,128]{2,1,0:T(8,128)S(1)}, u32[]{:S(2)}, u32[]{:S(2)}) collective-permute-start(s32[2,8,128]{2,1,0:T(8,128)S(1)} %get-tuple-element.73), channel_id=1, source_target_pairs={{0,6},{1,7},{2,0},{3,1},{4,2},{5,3},{6,4},{7,5},{8,14},{9,15},{10,... | collective-permute-start | bytes 24584 | tf_op jit(solution)/shard_map/wanted_exchange/ppermute | solution.py:462
  20.0 27.4 %copy-start.6 = (s32[2]{0:T(128)}, s32[2]{0:T(128)S(1)}, u32[]{:S(2)}) copy-start(s32[2]{0:T(128)S(1)} %pad_add_fusion.2.me_ref) | copy-start | bytes 28
  22.7 24.6 %copy-start = (bf16[16,144,128]{2,1,0:T(8,128)(2,1)}, bf16[16,144,128]{2,1,0:T(8,128)(2,1)S(1)}, u32[]{:S(2)}) copy-start(bf16[16,144,128]{2,1,0:T(8,128)(2,1)S(1)} %all-to-all-done.group_ref.rest_0_) | copy-start | bytes 1769476
  54.1 26.6 %all-to-all-start.2 = ((bf16[128,32,128]{2,1,0:T(8,128)(2,1)}), bf16[128,32,128]{2,1,0:T(8,128)(2,1)S(1)}, u32[]{:S(2)}, u32[]{:S(2)}) async-start(bf16[128,32,128]{2,1,0:T(8,128)(2,1)} %bitcast.40), calls=%async_computation.2 | async-start | bytes 2097152 | tf_op jit(solution)/shard_map/back_exchange/all_to_all | solution.py:476
  59.3 21.4 %copy-start.1 = (f32[2,8,1024]{2,1,0:T(8,128)S(1)}, f32[2,8,1024]{2,1,0:T(8,128)}, u32[]{:S(2)}) copy-start(f32[2,8,1024]{2,1,0:T(8,128)} %excitation_ref.3) | copy-start | bytes 196612
  59.3 21.4 %copy-start.3 = (f32[2,8,1024]{2,1,0:T(8,128)S(1)}, f32[2,8,1024]{2,1,0:T(8,128)}, u32[]{:S(2)}) copy-start(f32[2,8,1024]{2,1,0:T(8,128)} %get-tuple-element.42.currents_ref) | copy-start | bytes 196612
  59.3 21.4 %copy-start.5 = (f32[1024]{0:T(1024)S(1)}, f32[1024]{0:T(1024)}, u32[]{:S(2)}) copy-start(f32[1024]{0:T(1024)} %param.8) | copy-start | bytes 12292
  65.5 7.5 %collective-permute-start.4 = (bf16[8,16,128]{2,1,0:T(8,128)(2,1)}, bf16[8,16,128]{2,1,0:T(8,128)(2,1)S(1)}, u32[]{:S(2)}, u32[]{:S(2)}) collective-permute-start(bf16[8,16,128]{2,1,0:T(8,128)(2,1)} %get-tuple-element.45), channel_id=1, source_target_pairs={{0,1},{1,2},{2,3},{3,4},{4,5},{5,6},{6,7},{7,0},{8,9},{9,10},{10,1... | collective-permute-start | bytes 98312 | tf_op jit(solution)/shard_map/near_exchange/ppermute | solution.py:462
  67.2 9.9 %collective-permute-start.5 = (bf16[8,16,128]{2,1,0:T(8,128)(2,1)}, bf16[8,16,128]{2,1,0:T(8,128)(2,1)S(1)}, u32[]{:S(2)}, u32[]{:S(2)}) collective-permute-start(bf16[8,16,128]{2,1,0:T(8,128)(2,1)} %get-tuple-element.46), channel_id=1, source_target_pairs={{0,2},{1,3},{2,4},{3,5},{4,6},{5,7},{6,0},{7,1},{8,10},{9,11},{10,... | collective-permute-start | bytes 98312 | tf_op jit(solution)/shard_map/near_exchange/ppermute | solution.py:462
  68.7 10.4 %collective-permute-start.6 = (bf16[8,16,128]{2,1,0:T(8,128)(2,1)}, bf16[8,16,128]{2,1,0:T(8,128)(2,1)S(1)}, u32[]{:S(2)}, u32[]{:S(2)}) collective-permute-start(bf16[8,16,128]{2,1,0:T(8,128)(2,1)} %get-tuple-element.47), channel_id=1, source_target_pairs={{0,3},{1,4},{2,5},{3,6},{4,7},{5,0},{6,1},{7,2},{8,11},{9,12},{10,... | collective-permute-start | bytes 98312 | tf_op jit(solution)/shard_map/near_exchange/ppermute | solution.py:462
  70.6 8.5 %collective-permute-start.7 = (bf16[8,16,128]{2,1,0:T(8,128)(2,1)}, bf16[8,16,128]{2,1,0:T(8,128)(2,1)S(1)}, u32[]{:S(2)}, u32[]{:S(2)}) collective-permute-start(bf16[8,16,128]{2,1,0:T(8,128)(2,1)} %get-tuple-element.48), channel_id=1, source_target_pairs={{0,4},{1,5},{2,6},{3,7},{4,0},{5,1},{6,2},{7,3},{8,12},{9,13},{10,... | collective-permute-start | bytes 98312 | tf_op jit(solution)/shard_map/near_exchange/ppermute | solution.py:462
  70.6 8.4 %collective-permute-start.8 = (bf16[8,16,128]{2,1,0:T(8,128)(2,1)}, bf16[8,16,128]{2,1,0:T(8,128)(2,1)S(1)}, u32[]{:S(2)}, u32[]{:S(2)}) collective-permute-start(bf16[8,16,128]{2,1,0:T(8,128)(2,1)} %get-tuple-element.49), channel_id=1, source_target_pairs={{0,5},{1,6},{2,7},{3,0},{4,1},{5,2},{6,3},{7,4},{8,13},{9,14},{10,... | collective-permute-start | bytes 98312 | tf_op jit(solution)/shard_map/near_exchange/ppermute | solution.py:462
  72.9 6.2 %collective-permute-start.9 = (bf16[8,16,128]{2,1,0:T(8,128)(2,1)}, bf16[8,16,128]{2,1,0:T(8,128)(2,1)S(1)}, u32[]{:S(2)}, u32[]{:S(2)}) collective-permute-start(bf16[8,16,128]{2,1,0:T(8,128)(2,1)} %get-tuple-element.50), channel_id=1, source_target_pairs={{0,6},{1,7},{2,0},{3,1},{4,2},{5,3},{6,4},{7,5},{8,14},{9,15},{10,... | collective-permute-start | bytes 98312 | tf_op jit(solution)/shard_map/near_exchange/ppermute | solution.py:462
  77.2 3.6 %collective-permute-start.10 = (bf16[8,16,128]{2,1,0:T(8,128)(2,1)}, bf16[8,16,128]{2,1,0:T(8,128)(2,1)S(1)}, u32[]{:S(2)}, u32[]{:S(2)}) collective-permute-start(bf16[8,16,128]{2,1,0:T(8,128)(2,1)} %get-tuple-element.51), channel_id=1, source_target_pairs={{0,7},{1,0},{2,1},{3,2},{4,3},{5,4},{6,5},{7,6},{8,15},{9,8},{10,9... | collective-permute-start | bytes 98312 | tf_op jit(solution)/shard_map/near_exchange/ppermute | solution.py:462
  80.7 0.8 copy-start.4
  83.9 26.0 %all-to-all-start.3 = ((bf16[128,32,128]{2,1,0:T(8,128)(2,1)}), bf16[128,32,128]{2,1,0:T(8,128)(2,1)S(1)}, u32[]{:S(2)}, u32[]{:S(2)}) async-start(bf16[128,32,128]{2,1,0:T(8,128)(2,1)} %bitcast.17), calls=%async_computation.3 | async-start | bytes 2097152 | tf_op jit(solution)/shard_map/forward_exchange/all_to_all | solution.py:476
  90.6 6.8 %collective-permute-start.13 = (bf16[128,128]{1,0:T(8,128)(2,1)S(1)}, bf16[128,128]{1,0:T(8,128)(2,1)S(1)}, u32[]{:S(2)}, u32[]{:S(2)}) collective-permute-start(bf16[128,128]{1,0:T(8,128)(2,1)S(1)} %get-tuple-element.53), channel_id=1, source_target_pairs={{0,24},{8,0},{16,8},{24,16},{32,56},{40,32},{48,40},{56,48},{64,88... | collective-permute-start | bytes 98312 | tf_op jit(solution)/shard_map/row_gather/ppermute | solution.py:470
  93.3 9.0 %collective-permute-start.12 = (bf16[128,128]{1,0:T(8,128)(2,1)S(1)}, bf16[128,128]{1,0:T(8,128)(2,1)S(1)}, u32[]{:S(2)}, u32[]{:S(2)}) collective-permute-start(bf16[128,128]{1,0:T(8,128)(2,1)S(1)} %get-tuple-element.53), channel_id=1, source_target_pairs={{0,16},{8,24},{16,0},{24,8},{32,48},{40,56},{48,32},{56,40},{64,80... | collective-permute-start | bytes 98312 | tf_op jit(solution)/shard_map/row_gather/ppermute | solution.py:470
  93.9 11.6 %collective-permute-start.11 = (bf16[128,128]{1,0:T(8,128)(2,1)S(1)}, bf16[128,128]{1,0:T(8,128)(2,1)S(1)}, u32[]{:S(2)}, u32[]{:S(2)}) collective-permute-start(bf16[128,128]{1,0:T(8,128)(2,1)S(1)} %get-tuple-element.53), channel_id=1, source_target_pairs={{0,8},{8,16},{16,24},{24,0},{32,40},{40,48},{48,56},{56,32},{64,72... | collective-permute-start | bytes 98312 | tf_op jit(solution)/shard_map/row_gather/ppermute | solution.py:470
  105.5 13.2 %copy-start.8 = (bf16[4,128,128]{2,1,0:T(8,128)(2,1)}, bf16[4,128,128]{2,1,0:T(8,128)(2,1)S(1)}, u32[]{:S(2)}) copy-start(bf16[4,128,128]{2,1,0:T(8,128)(2,1)S(1)} %pad_maximum_fusion.rest_0_) | copy-start | bytes 393220
  109.9 2.1 %copy-start.7 = (bf16[128,32,128]{2,1,0:T(8,128)(2,1)}, bf16[128,32,128]{2,1,0:T(8,128)(2,1)S(1)}, u32[]{:S(2)}) copy-start(bf16[128,32,128]{2,1,0:T(8,128)(2,1)S(1)} %all-to-all-done.3) | copy-start | bytes 3145732
  109.9 8.9 %collective-permute-start.16 = (bf16[4,128,128]{2,1,0:T(8,128)(2,1)S(1)}, bf16[4,128,128]{2,1,0:T(8,128)(2,1)S(1)}, u32[]{:S(2)}, u32[]{:S(2)}) collective-permute-start(bf16[4,128,128]{2,1,0:T(8,128)(2,1)S(1)} %pad_maximum_fusion.rest_0_), channel_id=1, source_target_pairs={{0,96},{8,104},{16,112},{24,120},{32,0},{40,8},{48,16},{56,24},{64... | collective-permute-start | bytes 393224 | tf_op jit(solution)/shard_map/row_gather/ppermute | solution.py:470
  110.8 8.0 %collective-permute-start.15 = (bf16[4,128,128]{2,1,0:T(8,128)(2,1)S(1)}, bf16[4,128,128]{2,1,0:T(8,128)(2,1)S(1)}, u32[]{:S(2)}, u32[]{:S(2)}) collective-permute-start(bf16[4,128,128]{2,1,0:T(8,128)(2,1)S(1)} %pad_maximum_fusion.rest_0_), channel_id=1, source_target_pairs={{0,64},{8,72},{16,80},{24,88},{32,96},{40,104},{48,112},{56,120},{... | collective-permute-start | bytes 393224 | tf_op jit(solution)/shard_map/row_gather/ppermute | solution.py:470
  112.0 7.4 %collective-permute-start.14 = (bf16[4,128,128]{2,1,0:T(8,128)(2,1)S(1)}, bf16[4,128,128]{2,1,0:T(8,128)(2,1)S(1)}, u32[]{:S(2)}, u32[]{:S(2)}) collective-permute-start(bf16[4,128,128]{2,1,0:T(8,128)(2,1)S(1)} %pad_maximum_fusion.rest_0_), channel_id=1, source_target_pairs={{0,32},{8,40},{16,48},{24,56},{32,64},{40,72},{48,80},{56,88},{64,... | collective-permute-start | bytes 393224 | tf_op jit(solution)/shard_map/row_gather/ppermute | solution.py:470
  118.8 7.4 %copy-start.9 = (bf16[4,128,128]{2,1,0:T(8,128)(2,1)}, bf16[4,128,128]{2,1,0:T(8,128)(2,1)S(1)}, u32[]{:S(2)}) copy-start(bf16[4,128,128]{2,1,0:T(8,128)(2,1)S(1)} %collective-permute-done.16.rest_3_) | copy-start | bytes 393220
  118.8 7.4 %copy-start.10 = (bf16[4,128,128]{2,1,0:T(8,128)(2,1)}, bf16[4,128,128]{2,1,0:T(8,128)(2,1)S(1)}, u32[]{:S(2)}) copy-start(bf16[4,128,128]{2,1,0:T(8,128)(2,1)S(1)} %collective-permute-done.15.rest_2_) | copy-start | bytes 393220
  119.4 6.8 %copy-start.11 = (bf16[4,128,128]{2,1,0:T(8,128)(2,1)}, bf16[4,128,128]{2,1,0:T(8,128)(2,1)S(1)}, u32[]{:S(2)}) copy-start(bf16[4,128,128]{2,1,0:T(8,128)(2,1)S(1)} %collective-permute-done.14.rest_1_) | copy-start | bytes 393220
  119.4 28.2 %all-to-all-start.4 = ((bf16[128,32,128]{2,1,0:T(8,128)(2,1)}), bf16[128,32,128]{2,1,0:T(8,128)(2,1)S(1)}, u32[]{:S(2)}, u32[]{:S(2)}) async-start(bf16[128,32,128]{2,1,0:T(8,128)(2,1)} %bitcast.39), calls=%async_computation.4 | async-start | bytes 2097152 | tf_op jit(solution)/shard_map/back_exchange/all_to_all | solution.py:476
  132.4 7.6 %collective-permute-start.17 = (bf16[8,16,128]{2,1,0:T(8,128)(2,1)}, bf16[8,16,128]{2,1,0:T(8,128)(2,1)S(1)}, u32[]{:S(2)}, u32[]{:S(2)}) collective-permute-start(bf16[8,16,128]{2,1,0:T(8,128)(2,1)} %get-tuple-element.64), channel_id=1, source_target_pairs={{0,1},{1,2},{2,3},{3,4},{4,5},{5,6},{6,7},{7,0},{8,9},{9,10},{10,1... | collective-permute-start | bytes 98312 | tf_op jit(solution)/shard_map/near_exchange/ppermute | solution.py:462
  134.2 9.9 %collective-permute-start.18 = (bf16[8,16,128]{2,1,0:T(8,128)(2,1)}, bf16[8,16,128]{2,1,0:T(8,128)(2,1)S(1)}, u32[]{:S(2)}, u32[]{:S(2)}) collective-permute-start(bf16[8,16,128]{2,1,0:T(8,128)(2,1)} %get-tuple-element.65), channel_id=1, source_target_pairs={{0,2},{1,3},{2,4},{3,5},{4,6},{5,7},{6,0},{7,1},{8,10},{9,11},{10,... | collective-permute-start | bytes 98312 | tf_op jit(solution)/shard_map/near_exchange/ppermute | solution.py:462
  135.6 10.3 %collective-permute-start.19 = (bf16[8,16,128]{2,1,0:T(8,128)(2,1)}, bf16[8,16,128]{2,1,0:T(8,128)(2,1)S(1)}, u32[]{:S(2)}, u32[]{:S(2)}) collective-permute-start(bf16[8,16,128]{2,1,0:T(8,128)(2,1)} %get-tuple-element.66), channel_id=1, source_target_pairs={{0,3},{1,4},{2,5},{3,6},{4,7},{5,0},{6,1},{7,2},{8,11},{9,12},{10,... | collective-permute-start | bytes 98312 | tf_op jit(solution)/shard_map/near_exchange/ppermute | solution.py:462
  137.5 8.4 %collective-permute-start.20 = (bf16[8,16,128]{2,1,0:T(8,128)(2,1)}, bf16[8,16,128]{2,1,0:T(8,128)(2,1)S(1)}, u32[]{:S(2)}, u32[]{:S(2)}) collective-permute-start(bf16[8,16,128]{2,1,0:T(8,128)(2,1)} %get-tuple-element.67), channel_id=1, source_target_pairs={{0,4},{1,5},{2,6},{3,7},{4,0},{5,1},{6,2},{7,3},{8,12},{9,13},{10,... | collective-permute-start | bytes 98312 | tf_op jit(solution)/shard_map/near_exchange/ppermute | solution.py:462
  137.6 8.4 %collective-permute-start.21 = (bf16[8,16,128]{2,1,0:T(8,128)(2,1)}, bf16[8,16,128]{2,1,0:T(8,128)(2,1)S(1)}, u32[]{:S(2)}, u32[]{:S(2)}) collective-permute-start(bf16[8,16,128]{2,1,0:T(8,128)(2,1)} %get-tuple-element.68), channel_id=1, source_target_pairs={{0,5},{1,6},{2,7},{3,0},{4,1},{5,2},{6,3},{7,4},{8,13},{9,14},{10,... | collective-permute-start | bytes 98312 | tf_op jit(solution)/shard_map/near_exchange/ppermute | solution.py:462
  140.1 5.9 %collective-permute-start.22 = (bf16[8,16,128]{2,1,0:T(8,128)(2,1)}, bf16[8,16,128]{2,1,0:T(8,128)(2,1)S(1)}, u32[]{:S(2)}, u32[]{:S(2)}) collective-permute-start(bf16[8,16,128]{2,1,0:T(8,128)(2,1)} %get-tuple-element.69), channel_id=1, source_target_pairs={{0,6},{1,7},{2,0},{3,1},{4,2},{5,3},{6,4},{7,5},{8,14},{9,15},{10,... | collective-permute-start | bytes 98312 | tf_op jit(solution)/shard_map/near_exchange/ppermute | solution.py:462
  144.1 3.6 %collective-permute-start.23 = (bf16[8,16,128]{2,1,0:T(8,128)(2,1)}, bf16[8,16,128]{2,1,0:T(8,128)(2,1)S(1)}, u32[]{:S(2)}, u32[]{:S(2)}) collective-permute-start(bf16[8,16,128]{2,1,0:T(8,128)(2,1)} %get-tuple-element.70), channel_id=1, source_target_pairs={{0,7},{1,0},{2,1},{3,2},{4,3},{5,4},{6,5},{7,6},{8,15},{9,8},{10,9... | collective-permute-start | bytes 98312 | tf_op jit(solution)/shard_map/near_exchange/ppermute | solution.py:462
  147.6 0.8 copy-start.2
